TPU v7x, 32 devices: a whole 2x2x4 slice. The times are simulated.
32 devices in a mesh: seq: 16 (over z, y, core), batch: 2 (over x).
Axes of the slice: x: 2, y: 2, z: 4, core: 2. Of those that a mesh axis runs over, the one named last changes fastest.
Arguments:
- coarse: bfloat16 [2, 4096, 1536], P('batch', 'seq'), may hold values from -6 to 6
- skip: bfloat16 [2, 8192, 1536], P('batch', 'seq'), may hold values from -6 to 6
- depth_kernel: float32 [3, 1536], replicated, may hold values from -3.5 to 3.5
- sep_weight: bfloat16 [1536, 1536], P('seq'), may hold values from -0.15625 to 0.15625
- sep_bias: float32 [1536], replicated, may hold values from -3 to 3
- head_weight: bfloat16 [1536, 3840], P(None, 'seq'), may hold values from -0.15625 to 0.15625
- head_bias: float32 [3840], replicated, may hold values from -4 to 4
- strand_pair: int32 [3840], replicated, may hold values from 0 to 3839, as said below
Outputs:
- preds: bfloat16 [2, 8192, 3840], P('batch', 'seq')
Inputs may be any that keep to these rules, and one draw needn't show every extreme that they name: strand_pair is a permutation with strand_pair[strand_pair[t]] == t; about half of the tracks are paired with another one.
All inputs are finite; a program needn't handle non-finite values.
Results may differ from a plain program's by a relative error of at most 0.0053.
Values may be sent and summed in bfloat16 or wider, within the bound.
No kernel may reach another device: no remote copies, remote signals or barrier semaphores. Data moves between devices by JAX's collectives and lax.ppermute only.
A program may use at most 64 MiB of HBM per device.

v0:
```python
import jax
import jax.numpy as jnp
from jax import lax
from jax.sharding import PartitionSpec as P


def with_halo(cells, sides, width):
    for axis, dim in sides:
        count = lax.axis_size(axis)
        ends = count - 1
        head = lax.slice_in_dim(cells, 0, width, axis=dim)
        tail = lax.slice_in_dim(cells, cells.shape[dim] - width, cells.shape[dim], axis=dim)
        cells = jnp.concatenate(
            [
                lax.ppermute(tail, axis, [(i, (i + 1) % count) for i in range(ends)]),
                cells,
                lax.ppermute(head, axis, [((i + 1) % count, i) for i in range(ends)]),
            ],
            axis=dim,
        )
    return cells


def from_partner(block, axis, apart):
    count = lax.axis_size(axis)
    route = []
    for low in range(count):
        high = low | 1 << apart
        if high != low and high < count:
            route += [(low, high), (high, low)]
    return lax.ppermute(block, axis, route)


def mirror_blocks(payload):
    devices = lax.axis_size("seq")
    rows = payload.shape[0]
    spread = lax.all_to_all(payload, "seq", split_axis=1, concat_axis=0, tiled=True)
    width = spread.shape[1]
    flipped = spread.reshape(devices, rows, width)[::-1].reshape(devices * rows, width)
    return lax.all_to_all(flipped, "seq", split_axis=0, concat_axis=1, tiled=True)


def per_device(
    coarse, skip, depth_kernel, sep_weight, sep_bias, head_weight, head_bias, strand_pair
):
    upsampled = jnp.repeat(coarse[0].astype(jnp.float32), 2, axis=0)
    merged = (upsampled + skip[0]).astype(jnp.bfloat16)
    padded = with_halo(merged, (("seq", 0),), 1)
    depthwise = (
        depth_kernel[0] * padded[:-2]
        + depth_kernel[1] * padded[1:-1]
        + depth_kernel[2] * padded[2:]
    )
    depthwise = depthwise.astype(jnp.bfloat16)
    pointwise = jnp.dot(
        depthwise,
        lax.all_gather(sep_weight, "seq", axis=0, tiled=True),
        preferred_element_type=jnp.float32,
    )
    features = jax.nn.gelu(pointwise + sep_bias, approximate=True).astype(jnp.bfloat16)
    strand_bit = lax.axis_size("batch").bit_length() - 2
    logits = jnp.dot(
        features,
        lax.all_gather(head_weight, "seq", axis=1, tiled=True),
        preferred_element_type=jnp.float32,
    )
    logits = logits + head_bias
    own_head = jax.nn.softplus(logits).astype(jnp.bfloat16)
    outgoing = jnp.take(own_head, strand_pair, axis=1)[::-1]
    crossed = from_partner(outgoing, "batch", strand_bit)
    received = mirror_blocks(crossed)
    averaged = 0.5 * (own_head.astype(jnp.float32) + received.astype(jnp.float32))
    return averaged.astype(jnp.bfloat16)[None]


def solution(mesh):
    in_specs = (
        P("batch", "seq", None),
        P("batch", "seq", None),
        P(),
        P("seq", None),
        P(),
        P(None, "seq"),
        P(),
        P(),
    )
    out_specs = P("batch", "seq", None)
    return jax.shard_map(
        per_device, mesh=mesh, in_specs=in_specs, out_specs=out_specs, check_vma=False
    )
```

profile of v0, /device:TPU:0, one launch (start us, length us, event | category | flops | bytes accessed | tf_op | source)
XLA Modules:
  0.0 568.4 jit_solution(10641653344981456063)
XLA Ops:
  6.5 0.0 all-gather.3.cloned.1.call-start
  6.5 0.7 all-gather.3.cloned.1.call-update
  7.3 0.0 all-gather.5.cloned.1.call-start
  7.3 0.7 all-gather.5.cloned.1.call-update
  8.0 1.3 bitcast_convert_fusion
  9.3 1.1 broadcast_in_dim.20
  10.4 3.3 reshape.28
  13.7 0.0 copy-start.1
  13.7 0.0 copy-start
  13.7 0.0 copy-start.2
  13.7 0.0 copy-start.3
  13.8 2.9 fusion.9
  16.6 2.4 collective-permute-start
  19.0 1.5 collective-permute-start.1
  20.5 0.0 copy-done.1
  20.5 0.1 slice_reduce_fusion.2
  20.6 0.0 copy-done
  20.6 0.0 collective-permute-done
  20.6 3.6 collective-permute-done.1
  24.2 41.6 %all-gather.3.cloned.1.call-done = bf16[1536,1536]{1,0:T(8,128)(2,1)} async-done(((bf16[96,1536]{1,0:T(8,128)(2,1)}), bf16[1536,1536]{1,0:T(8,128)(2,1)}) %all-gather.3.cloned.1.call-update) | async-done | bytes 4718608 | tf_op jit(solution)/shard_map/all_gather | solution.py:57
  65.8 96.8 %all-gather.5.cloned.1.call-done = bf16[1536,3840]{0,1:T(8,128)(2,1)} async-done(((bf16[1536,240]{0,1:T(8,128)(2,1)}), bf16[1536,3840]{0,1:T(8,128)(2,1)}) %all-gather.5.cloned.1.call-update) | async-done | bytes 11796496 | tf_op jit(solution)/shard_map/all_gather | solution.py:64
  162.6 0.0 copy-done.2
  162.6 0.0 copy-done.3
  162.6 19.8 %fusion = bf16[512,3840]{1,0:T(8,128)(2,1)} fusion(bf16[1536,3840]{0,1:T(8,128)(2,1)} %all-gather.5.cloned.1.call-done, f32[3840]{0:T(1024)S(1)} %copy-done.2, bf16[1536,1536]{1,0:T(8,128)(2,1)} %all-gather.3.cloned.1.call-done, bf16[512,1536]{1,0:T(8,128)(2,1)S(1)} %fusion.9, bf16[1,1536]{1,0:T(2,128)(2,1)S(1)} %collective-permute-done.1, ...), kind=kOutput, calls=%fused_computation.2 | convolution fusion | flops 8491106304 | bytes 22066176 | tf_op jit(solution)/shard_map/dot_general | solution.py:62
  182.4 6.3 %copy.11 = bf16[512,3840]{0,1:T(8,128)(2,1)} copy(bf16[512,3840]{1,0:T(8,128)(2,1)} %fusion) | data formatting | bytes 7864320 | tf_op jit(solution)/shard_map/convert_element_type | solution.py:68
  188.7 14.5 %gather_fusion = bf16[3840,512]{1,0:T(8,128)(2,1)} fusion(bf16[512,3840]{0,1:T(8,128)(2,1)} %copy.11, s32[4096]{0:T(1024)S(1)} %pad_clamp_fusion), kind=kCustom, calls=%fused_computation | custom fusion | bytes 7879680 | tf_op jit(solution)/shard_map/jit(_take)/gather | solution.py:69
  203.2 4.7 select_bitcast_fusion
  207.9 58.9 %rev.4 = bf16[512,3840]{0,1:T(8,128)(2,1)} reverse(bf16[512,3840]{0,1:T(8,128)(2,1)} %select_bitcast_fusion), dimensions={0} | reverse | bytes 7864320 | tf_op jit(solution)/shard_map/rev | solution.py:69
  266.8 1.5 collective-permute-start.2
  268.3 85.9 %collective-permute-done.2 = bf16[512,3840]{0,1:T(8,128)(2,1)S(1)} collective-permute-done((bf16[512,3840]{0,1:T(8,128)(2,1)}, bf16[512,3840]{0,1:T(8,128)(2,1)S(1)}, u32[]{:S(2)}, u32[]{:S(2)}) %collective-permute-start.2) | collective-permute-done | bytes 3932192 | tf_op jit(solution)/shard_map/ppermute | solution.py:31
  354.2 91.0 %all_to_all.29 = bf16[512,16,240]{0,2,1:T(8,128)(2,1)} all-to-all(bf16[512,16,240]{0,2,1:T(8,128)(2,1)S(1)} %bitcast.19), channel_id=1, replica_groups=mesh['seq'=16,'batch'=2] {'seq'}, dimensions={1} | all-to-all | bytes 7864320 | tf_op jit(solution)/shard_map/all_to_all | solution.py:37
  445.2 4.3 all_to_all.25
  449.5 91.6 %all_to_all.30 = bf16[16,512,240]{1,2,0:T(8,128)(2,1)S(1)} all-to-all(bf16[16,512,240]{1,2,0:T(8,128)(2,1)} %all_to_all.25), channel_id=1, replica_groups=mesh['seq'=16,'batch'=2] {'seq'}, dimensions={0} | all-to-all | bytes 7864320 | tf_op jit(solution)/shard_map/all_to_all | solution.py:40
  541.1 4.2 convert_element_type.67
  545.3 9.1 %copy.12 = f32[512,3840]{1,0:T(8,128)} copy(f32[512,3840]{0,1:T(8,128)} %bitcast.17) | data formatting | bytes 15728640 | tf_op jit(solution)/shard_map/convert_element_type | solution.py:72
  554.4 7.2 %fusion.1 = bf16[1,512,3840]{2,1,0:T(8,128)(2,1)} fusion(f32[512,3840]{1,0:T(8,128)} %copy.12, bf16[512,3840]{1,0:T(8,128)(2,1)} %fusion), kind=kLoop, calls=%fused_computation.5 | loop fusion | flops 7864320 | bytes 15728640 | tf_op jit(solution)/shard_map/broadcast_in_dim | solution.py:73
  (4 shorter events, 0.0 us)
Async XLA Ops:
  6.5 59.2 %all-gather.3.cloned.1.call-start = ((), (), s32[]{:S(2)}) async-start(), calls=%async_computation.2 | async-start | bytes 5013504 | tf_op jit(solution)/shard_map/all_gather | solution.py:57
  7.3 155.3 %all-gather.5.cloned.1.call-start = ((), (), s32[]{:S(2)}) async-start(), calls=%async_computation.3 | async-start | bytes 12533760 | tf_op jit(solution)/shard_map/all_gather | solution.py:64
  13.7 6.7 %copy-start.1 = (f32[3,1536]{1,0:T(4,128)S(1)}, f32[3,1536]{1,0:T(4,128)}, u32[]{:S(2)}) copy-start(f32[3,1536]{1,0:T(4,128)} %param.10) | copy-start | bytes 55300
  13.7 6.8 %copy-start = (s32[3840]{0:T(1024)S(1)}, s32[3840]{0:T(1024)}, u32[]{:S(2)}) copy-start(s32[3840]{0:T(1024)} %param.15) | copy-start | bytes 46084
  13.7 148.8 %copy-start.2 = (f32[3840]{0:T(1024)S(1)}, f32[3840]{0:T(1024)}, u32[]{:S(2)}) copy-start(f32[3840]{0:T(1024)} %param.14) | copy-start | bytes 46084
  13.7 148.8 %copy-start.3 = (f32[1536]{0:T(1024)S(1)}, f32[1536]{0:T(1024)}, u32[]{:S(2)}) copy-start(f32[1536]{0:T(1024)} %param.12) | copy-start | bytes 18436
  16.6 4.0 collective-permute-start
  19.0 5.2 collective-permute-start.1
  266.8 87.3 %collective-permute-start.2 = (bf16[512,3840]{0,1:T(8,128)(2,1)}, bf16[512,3840]{0,1:T(8,128)(2,1)S(1)}, u32[]{:S(2)}, u32[]{:S(2)}) collective-permute-start(bf16[512,3840]{0,1:T(8,128)(2,1)} %rev.4), channel_id=1, source_target_pairs={{0,1},{1,0},{2,3},{3,2},{4,5},{5,4},{6,7},{7,6},{8,9},{9,8},{10,11... | collective-permute-start | bytes 11796488 | tf_op jit(solution)/shard_map/ppermute | solution.py:31
Sparse Core Ops, SparseCore 0:
  9.6 56.0 all-gather.2
  68.0 94.4 all-gather.4
where the time goes:
time: 576 us; the launch traced here: 568 us
  waiting for transfers between devices  229 us (40%)
  blocking collectives  183 us (32%)
  local copies, waits for them, and re-layouts  97.6 us (17%)
  other arithmetic  20.3 us (4%)
  matrix products  19.8 us (3%)
  between operations  13.5 us (2%)
    all_gather x1, waiting for transfers between devices, per_device(): lax.all_gather(head_weight, 'seq', axis=1, tiled=True)  96.8 us
    all_to_all x1, blocking collectives, mirror_blocks(): lax.all_to_all(flipped, 'seq', split_axis=0, concat_axis=1, tiled=True)  91.6 us
    all_to_all x1, blocking collectives, mirror_blocks(): lax.all_to_all(payload, 'seq', split_axis=1, concat_axis=0, tiled=True)  91 us
    ppermute x1, waiting for transfers between devices, from_partner(): return lax.ppermute(block, axis, route)  85.9 us
    rev x1, local copies, waits for them, and re-layouts, per_device(): outgoing = jnp.take(own_head, strand_pair, axis=1)[::-1]  58.9 us
    all_gather x1, waiting for transfers between devices, per_device(): lax.all_gather(sep_weight, 'seq', axis=0, tiled=True)  41.6 us
    dot_general x1, matrix products, per_device(): jnp.dot(features, lax.all_gather(head_weight, 'seq', axis=1, tiled=True),...  19.8 us
    gather x1, local copies, waits for them, and re-layouts, per_device(): outgoing = jnp.take(own_head, strand_pair, axis=1)[::-1]  14.5 us
  transfers between devices with their start and end apart: 5, of which 4 were waited for; matrix products, arithmetic and copies ran while one was open for 2% of the time, Pallas kernels for 0%

commit v1 on v0

v1 whole, which is shorter than its diff:
```python
import functools

import jax
import jax.numpy as jnp
from jax import lax
from jax.experimental import pallas as pl
from jax.experimental.pallas import tpu as pltpu
from jax.sharding import PartitionSpec as P

BOTH = ("seq", "batch")
VMEM_LIMIT = 56 * 1024 * 1024


def params():
    return pltpu.CompilerParams(vmem_limit_bytes=VMEM_LIMIT)


def route(seq, batch, move):
    pairs = []
    for s in range(seq):
        for b in range(batch):
            target = move(s, b)
            if target is not None:
                pairs.append((s * batch + b, target[0] * batch + target[1]))
    return pairs


def send(array, move):
    seq, batch = lax.axis_size("seq"), lax.axis_size("batch")
    return lax.ppermute(array, BOTH, route(seq, batch, move))


def one_hot(shape, hit):
    rows = lax.broadcasted_iota(jnp.int32, shape, 0)
    columns = lax.broadcasted_iota(jnp.int32, shape, 1)
    return jnp.where(hit(rows, columns), 1.0, 0.0).astype(jnp.bfloat16)


def conv_kernel(coarse, skip, top, bottom, taps, own, flipped):
    bins = skip.shape[0]
    spread = one_hot((bins, coarse.shape[0]), lambda r, c: r // 2 == c)
    up = jnp.dot(spread, coarse[...], preferred_element_type=jnp.float32)
    merged = (up + skip[...].astype(jnp.float32)).astype(jnp.bfloat16).astype(jnp.float32)
    row = lax.broadcasted_iota(jnp.int32, merged.shape, 0)
    before = jnp.where(row == 0, top[...].astype(jnp.float32), pltpu.roll(merged, 1, 0))
    after = jnp.where(
        row == bins - 1, bottom[...].astype(jnp.float32), pltpu.roll(merged, bins - 1, 0)
    )
    result = taps[0:1, :] * before + taps[1:2, :] * merged + taps[2:3, :] * after
    result = result.astype(jnp.bfloat16)
    own[...] = result
    mirror = one_hot((bins, bins), lambda r, c: r + c == bins - 1)
    flipped[...] = jnp.dot(mirror, result, preferred_element_type=jnp.float32).astype(jnp.bfloat16)


def conv(coarse, skip, top, bottom, taps):
    bins, width = skip.shape
    step = 256
    column = lambda rows: pl.BlockSpec((rows, step), lambda j: (0, j))
    return pl.pallas_call(
        conv_kernel,
        grid=(width // step,),
        in_specs=[column(coarse.shape[0]), column(bins), column(1), column(1), column(3)],
        out_specs=[column(bins), column(bins)],
        out_shape=[jax.ShapeDtypeStruct((bins, width), jnp.bfloat16)] * 2,
        compiler_params=params(),
        name="conv",
    )(coarse, skip, top, bottom, taps)


def features_kernel(own, other, weight, bias, out):
    bins = own.shape[0]
    for place, part in enumerate((own, other)):
        product = jnp.dot(part[...], weight[...], preferred_element_type=jnp.float32)
        out[pl.ds(place * bins, bins), :] = jax.nn.gelu(
            product + bias[...], approximate=True
        ).astype(jnp.bfloat16)


def features(own, other, weight, bias):
    bins, width = own.shape
    step = 256
    whole = pl.BlockSpec((bins, width), lambda j: (0, 0))
    return pl.pallas_call(
        features_kernel,
        grid=(width // step,),
        in_specs=[
            whole,
            whole,
            pl.BlockSpec((width, step), lambda j: (0, j)),
            pl.BlockSpec((1, step), lambda j: (0, j)),
        ],
        out_specs=pl.BlockSpec((2 * bins, step), lambda j: (0, j)),
        out_shape=jax.ShapeDtypeStruct((2 * bins, width), jnp.bfloat16),
        compiler_params=params(),
        name="features",
    )(own, other, weight, bias)


def softplus(v):
    return jnp.maximum(v, 0.0) + jnp.log1p(jnp.exp(-jnp.abs(v)))


def heads_kernel(values, weight, bias, out):
    product = lax.dot_general(
        values[...], weight[...], (((1,), (1,)), ((), ())), preferred_element_type=jnp.float32
    )
    out[...] = softplus(product + bias[...]).astype(jnp.bfloat16)


def heads(values, weight, bias):
    rows, width = values.shape
    tracks = weight.shape[0]
    step = 256
    return pl.pallas_call(
        heads_kernel,
        grid=(tracks // step,),
        in_specs=[
            pl.BlockSpec((rows, width), lambda j: (0, 0)),
            pl.BlockSpec((step, width), lambda j: (j, 0)),
            pl.BlockSpec((1, step), lambda j: (0, j)),
        ],
        out_specs=pl.BlockSpec((rows, step), lambda j: (0, j)),
        out_shape=jax.ShapeDtypeStruct((rows, tracks), jnp.bfloat16),
        compiler_params=params(),
        name="heads",
    )(values, weight, bias)


def average_kernel(own, other, pair, out):
    tracks = other.shape[1]
    rows = lax.broadcasted_iota(jnp.int32, (tracks, pair.shape[1]), 0)
    chosen = jnp.where(rows == pair[...], 1.0, 0.0).astype(jnp.bfloat16)
    received = jnp.dot(other[...], chosen, preferred_element_type=jnp.float32)
    out[...] = (0.5 * (own[...].astype(jnp.float32) + received)).astype(jnp.bfloat16)


def average(both, pair):
    rows, tracks = both.shape
    bins = rows // 2
    step = 256
    return pl.pallas_call(
        average_kernel,
        grid=(tracks // step,),
        in_specs=[
            pl.BlockSpec((bins, step), lambda j: (0, j)),
            pl.BlockSpec((bins, tracks), lambda j: (1, 0)),
            pl.BlockSpec((1, step), lambda j: (0, j)),
        ],
        out_specs=pl.BlockSpec((bins, step), lambda j: (0, j)),
        out_shape=jax.ShapeDtypeStruct((bins, tracks), jnp.bfloat16),
        compiler_params=params(),
        name="average",
    )(both, both, pair)


def gather_rows(shard):
    batch = lax.axis_size("batch")
    part = shard.shape[0] // batch
    mine = lax.dynamic_slice_in_dim(shard, lax.axis_index("batch") * part, part, axis=0)
    return lax.all_gather(mine, BOTH, axis=0, tiled=True)


def edge(coarse_row, skip_row):
    total = coarse_row.astype(jnp.float32) + skip_row.astype(jnp.float32)
    return total.astype(jnp.bfloat16)


def per_device(
    coarse, skip, depth_kernel, sep_weight, sep_bias, head_weight, head_bias, strand_pair
):
    seq, batch = lax.axis_size("seq"), lax.axis_size("batch")
    coarse, skip = coarse[0], skip[0]
    first = edge(coarse[:1], skip[:1])
    last = edge(coarse[-1:], skip[-1:])
    top = send(last, lambda s, b: (s + 1, b) if s + 1 < seq else None)
    bottom = send(first, lambda s, b: (s - 1, b) if s > 0 else None)
    own, flipped = conv(coarse, skip, top, bottom, depth_kernel)
    other = send(flipped, lambda s, b: (seq - 1 - s, (b + batch // 2) % batch))
    values = features(own, other, gather_rows(sep_weight), sep_bias[None])
    both = heads(values, gather_rows(head_weight.T), head_bias[None])
    return average(both, strand_pair[None])[None]


def solution(mesh):
    in_specs = (
        P("batch", "seq", None),
        P("batch", "seq", None),
        P(),
        P("seq", None),
        P(),
        P(None, "seq"),
        P(),
        P(),
    )
    out_specs = P("batch", "seq", None)
    return jax.shard_map(
        per_device, mesh=mesh, in_specs=in_specs, out_specs=out_specs, check_vma=False
    )
```

time: 576 us -> 265 us (0.46); the launches traced: 568 us -> 265 us
  blocking collectives: 183 us -> 0 us
  local copies, waits for them, and re-layouts: 97.6 us -> 4.83 us
  Pallas kernels: 0 us -> 62.2 us
  waiting for transfers between devices: 229 us -> 175 us
  matrix products: 19.8 us -> 0 us
  other arithmetic: 20.3 us -> 0.82 us
    all_to_all x2 -> x0, blocking collectives: 183 us -> none  [the longest x1 91.6 us: mirror_blocks(): lax.all_to_all(flipped, 'seq', split_axis=0, concat_axis=1, tiled=True)]
    pallas_call x0 -> x4, Pallas kernels: none -> 62.2 us  [the longest x1 23.5 us: heads(): pl.pallas_call(heads_kernel, grid=(tracks // step,), in_specs=[pl.BlockSp...]
    rev x1 -> x0, local copies, waits for them, and re-layouts: 58.9 us -> none  [per_device(): outgoing = jnp.take(own_head, strand_pair, axis=1)[::-1]]
    ppermute x3, waiting for transfers between devices: 89.4 us -> 37.5 us  [send(): return lax.ppermute(array, BOTH, route(seq, batch, move))]
    dot_general x1 -> x0, matrix products: 19.8 us -> none  [per_device(): jnp.dot(features, lax.all_gather(head_weight, 'seq', axis=1, tiled=True),...]
    convert_element_type x2 -> x0, local copies, waits for them, and re-layouts: 15.4 us -> none  [the longest x1 9.13 us: per_device(): received.astype(jnp.float32)]
    gather x1 -> x0, local copies, waits for them, and re-layouts: 14.5 us -> none  [per_device(): outgoing = jnp.take(own_head, strand_pair, axis=1)[::-1]]
    convert_element_type x3 -> x1, other arithmetic: 8.36 us -> 0.82 us  [edge(): return total.astype(jnp.bfloat16)]
  transfers between devices with their start and end apart: 5 -> 5, of which waited for: 4 -> 4; matrix products, arithmetic and copies ran while one was open for 2% -> 1% of each run, Pallas kernels for 0% -> 7%
where the time goes in v1:
time: 265 us
  waiting for transfers between devices  175 us (66%)
  Pallas kernels  62.2 us (23%)
  between operations  13.5 us (5%)
  starting transfers between devices  7.85 us (3%)
  local copies, waits for them, and re-layouts  4.83 us (2%)
    all_gather x2, waiting for transfers between devices, gather_rows(): return lax.all_gather(mine, BOTH, axis=0, tiled=True)  138 us
    ppermute x3, waiting for transfers between devices, send(): return lax.ppermute(array, BOTH, route(seq, batch, move))  37.5 us
    pallas_call x1, Pallas kernels, heads(): pl.pallas_call(heads_kernel, grid=(tracks // step,), in_specs=[pl.BlockSp...  23.5 us
    pallas_call x1, Pallas kernels, average(): pl.pallas_call(average_kernel, grid=(tracks // step,), in_specs=[pl.Block...  21.2 us
    pallas_call x1, Pallas kernels, features(): pl.pallas_call(features_kernel, grid=(width // step,), in_specs=[whole, w...  10.5 us
    ppermute x3, starting transfers between devices, send(): return lax.ppermute(array, BOTH, route(seq, batch, move))  7.77 us
    pallas_call x1, Pallas kernels, conv(): pl.pallas_call(conv_kernel, grid=(width // step,), in_specs=[column(coars...  6.92 us
  transfers between devices with their start and end apart: 5, of which 4 were waited for; matrix products, arithmetic and copies ran while one was open for 1% of the time, Pallas kernels for 7%

profile of v1, /device:TPU:0, one launch (start us, length us, event | category | flops | bytes accessed | tf_op | source)
XLA Modules:
  0.0 264.5 jit_solution(1916482503756854833)
XLA Ops:
  6.5 0.0 copy-start
  6.5 0.0 copy-start.4
  6.5 0.0 copy-start.2
  6.5 0.0 copy-start.3
  6.5 0.0 all-gather.3.cloned.1.call-start
  6.6 1.6 constant_dynamic-slice_fusion
  8.2 0.0 all-gather.3.cloned.1.call-update
  8.2 0.0 all-gather.5.cloned.1.call-start
  8.3 0.0 copy-done
  8.3 0.8 dynamic-slice_bitcast_fusion
  9.1 0.0 all-gather.5.cloned.1.call-update
  9.1 0.8 convert_bitcast_fusion
  9.9 2.4 collective-permute-start
  12.3 1.3 collective-permute-start.1
  13.6 0.0 collective-permute-done.top
  13.6 0.0 copy-start.5
  13.6 3.9 %collective-permute-done.1.bottom = bf16[1,1536]{1,0:T(2,128)(2,1)S(1)} collective-permute-done((bf16[1,1536]{1,0:T(2,128)(2,1)S(1)}, bf16[1,1536]{1,0:T(2,128)(2,1)S(1)}, u32[]{:S(2)}, u32[]{:S(2)}) %collective-permute-start.1) | collective-permute-done | bytes 3104 | tf_op jit(solution)/shard_map/ppermute | solution.py:30
  17.5 0.0 copy-start.6
  17.5 0.0 copy-done.5
  17.5 0.6 copy-done.6
  18.1 6.9 %conv.1 = (bf16[512,1536]{1,0:T(8,128)(2,1)}, bf16[512,1536]{1,0:T(8,128)(2,1)}) custom-call(bf16[256,1536]{1,0:T(8,128)(2,1)} %bitcast.10, bf16[512,1536]{1,0:T(8,128)(2,1)} %bitcast.9, bf16[1,1536]{1,0:T(2,128)(2,1)} %copy-done.5, bf16[1,1536]{1,0:T(2,128)(2,1)} %copy-done.6, f32[3,1536]{1,0:T(4,128)} %taps.1), custom_call_target="tpu_custom_call" | custom-call | tf_op jit(solution)/shard_map/conv/pallas_call | solution.py:60
  25.0 4.1 %collective-permute-start.2 = (bf16[512,1536]{1,0:T(8,128)(2,1)}, bf16[512,1536]{1,0:T(8,128)(2,1)S(1)}, u32[]{:S(2)}, u32[]{:S(2)}) collective-permute-start(bf16[512,1536]{1,0:T(8,128)(2,1)} %get-tuple-element.8), channel_id=1, source_target_pairs={{0,31},{1,30},{2,29},{3,28},{4,27},{5,26},{6,25},{7,24},{8,23},{9,... | collective-permute-start | bytes 4718600 | tf_op jit(solution)/shard_map/ppermute | solution.py:30
  29.1 0.0 copy-done.4
  29.1 0.6 broadcast_in_dim.12.bias
  29.7 0.0 copy-done.2
  29.7 0.6 broadcast_in_dim.13.bias
  30.3 0.0 copy-done.3
  30.3 0.6 broadcast_in_dim.14.pair
  31.0 33.6 %collective-permute-done.2.other = bf16[512,1536]{1,0:T(8,128)(2,1)S(1)} collective-permute-done((bf16[512,1536]{1,0:T(8,128)(2,1)}, bf16[512,1536]{1,0:T(8,128)(2,1)S(1)}, u32[]{:S(2)}, u32[]{:S(2)}) %collective-permute-start.2) | collective-permute-done | bytes 1572896 | tf_op jit(solution)/shard_map/ppermute | solution.py:30
  64.6 0.0 copy-start.1
  64.6 54.1 %all-gather.3.cloned.1.call-done.weight = bf16[1536,1536]{1,0:T(8,128)(2,1)} async-done(((bf16[48,1536]{1,0:T(8,128)(2,1)}), bf16[1536,1536]{1,0:T(8,128)(2,1)}) %all-gather.3.cloned.1.call-update) | async-done | bytes 4718608 | tf_op jit(solution)/shard_map/all_gather | solution.py:161
  118.7 0.0 copy-done.1
  118.7 10.5 %features.1.values = bf16[1024,1536]{1,0:T(8,128)(2,1)} custom-call(bf16[512,1536]{1,0:T(8,128)(2,1)} %get-tuple-element.7.own, bf16[512,1536]{1,0:T(8,128)(2,1)} %copy-done.1, bf16[1536,1536]{1,0:T(8,128)(2,1)} %all-gather.3.cloned.1.call-done.weight, f32[1,1536]{1,0:T(1,128)} %broadcast_in_dim.12.bias), custom_call_target="tpu_custom_call" | custom-call | tf_op jit(solution)/shard_map/features/pallas_call | solution.py:84
  129.2 83.8 %all-gather.5.cloned.1.call-done.weight = bf16[3840,1536]{1,0:T(8,128)(2,1)} async-done(((bf16[120,1536]{1,0:T(8,128)(2,1)}), bf16[3840,1536]{1,0:T(8,128)(2,1)}) %all-gather.5.cloned.1.call-update) | async-done | bytes 11796496 | tf_op jit(solution)/shard_map/all_gather | solution.py:161
  213.0 23.5 %heads.1.own.other = bf16[1024,3840]{1,0:T(8,128)(2,1)} custom-call(bf16[1024,1536]{1,0:T(8,128)(2,1)} %features.1.values, bf16[3840,1536]{1,0:T(8,128)(2,1)} %all-gather.5.cloned.1.call-done.weight, f32[1,3840]{1,0:T(1,128)} %broadcast_in_dim.13.bias), custom_call_target="tpu_custom_call" | custom-call | tf_op jit(solution)/shard_map/heads/pallas_call | solution.py:115
  236.5 21.2 %average.1 = bf16[512,3840]{1,0:T(8,128)(2,1)} custom-call(bf16[1024,3840]{1,0:T(8,128)(2,1)} %heads.1.own.other, bf16[1024,3840]{1,0:T(8,128)(2,1)} %heads.1.own.other, s32[1,3840]{1,0:T(1,128)} %broadcast_in_dim.14.pair), custom_call_target="tpu_custom_call" | custom-call | tf_op jit(solution)/shard_map/average/pallas_call | solution.py:142
Async XLA Ops:
  6.5 1.8 copy-start
  6.5 22.6 %copy-start.4 = (f32[1536]{0:T(1024)S(1)}, f32[1536]{0:T(1024)}, u32[]{:S(2)}) copy-start(f32[1536]{0:T(1024)} %param.12) | copy-start | bytes 18436
  6.5 23.2 %copy-start.2 = (f32[3840]{0:T(1024)S(1)}, f32[3840]{0:T(1024)}, u32[]{:S(2)}) copy-start(f32[3840]{0:T(1024)} %param.14) | copy-start | bytes 46084
  6.5 23.8 %copy-start.3 = (s32[3840]{0:T(1024)S(1)}, s32[3840]{0:T(1024)}, u32[]{:S(2)}) copy-start(s32[3840]{0:T(1024)} %param.15) | copy-start | bytes 46084
  6.5 112.1 %all-gather.3.cloned.1.call-start = ((), (), s32[]{:S(2)}) async-start(), calls=%async_computation | async-start | bytes 4866048 | tf_op jit(solution)/shard_map/all_gather | solution.py:161
  8.2 204.7 %all-gather.5.cloned.1.call-start = ((), (), s32[]{:S(2)}) async-start(), calls=%async_computation.1 | async-start | bytes 12165120 | tf_op jit(solution)/shard_map/all_gather | solution.py:161
  9.9 3.7 %collective-permute-start = (bf16[1,1536]{1,0:T(2,128)(2,1)S(1)}, bf16[1,1536]{1,0:T(2,128)(2,1)S(1)}, u32[]{:S(2)}, u32[]{:S(2)}) collective-permute-start(bf16[1,1536]{1,0:T(2,128)(2,1)S(1)} %get-tuple-element.10), channel_id=1, source_target_pairs={{0,2},{1,3},{2,4},{3,5},{4,6},{5,7},{6,8},{7,9},{8,10},{9,11},{10,... | collective-permute-start | bytes 9224 | tf_op jit(solution)/shard_map/ppermute | solution.py:30
  12.3 5.2 %collective-permute-start.1 = (bf16[1,1536]{1,0:T(2,128)(2,1)S(1)}, bf16[1,1536]{1,0:T(2,128)(2,1)S(1)}, u32[]{:S(2)}, u32[]{:S(2)}) collective-permute-start(bf16[1,1536]{1,0:T(2,128)(2,1)S(1)} %get-tuple-element.9), channel_id=1, source_target_pairs={{2,0},{3,1},{4,2},{5,3},{6,4},{7,5},{8,6},{9,7},{10,8},{11,9},{12,... | collective-permute-start | bytes 9224 | tf_op jit(solution)/shard_map/ppermute | solution.py:30
  13.6 3.9 %copy-start.5 = (bf16[1,1536]{1,0:T(2,128)(2,1)}, bf16[1,1536]{1,0:T(2,128)(2,1)S(1)}, u32[]{:S(2)}) copy-start(bf16[1,1536]{1,0:T(2,128)(2,1)S(1)} %collective-permute-done.top) | copy-start | bytes 9220
  17.5 0.6 copy-start.6
  25.0 39.6 %collective-permute-start.2 = (bf16[512,1536]{1,0:T(8,128)(2,1)}, bf16[512,1536]{1,0:T(8,128)(2,1)S(1)}, u32[]{:S(2)}, u32[]{:S(2)}) collective-permute-start(bf16[512,1536]{1,0:T(8,128)(2,1)} %get-tuple-element.8), channel_id=1, source_target_pairs={{0,31},{1,30},{2,29},{3,28},{4,27},{5,26},{6,25},{7,24},{8,23},{9,... | collective-permute-start | bytes 4718600 | tf_op jit(solution)/shard_map/ppermute | solution.py:30
  64.6 54.1 %copy-start.1 = (bf16[512,1536]{1,0:T(8,128)(2,1)}, bf16[512,1536]{1,0:T(8,128)(2,1)S(1)}, u32[]{:S(2)}) copy-start(bf16[512,1536]{1,0:T(8,128)(2,1)S(1)} %collective-permute-done.2.other) | copy-start | bytes 4718596
Sparse Core Ops, SparseCore 0:
  10.3 108.3 all-gather.2
  121.6 91.3 all-gather.4

commit v2 on v1

--- a/solution.py
+++ b/solution.py
@@ -13,6 +13,10 @@
 
 def params():
     return pltpu.CompilerParams(vmem_limit_bytes=VMEM_LIMIT)
+
+
+def cost(flops, bytes_accessed):
+    return pl.CostEstimate(flops=flops, bytes_accessed=bytes_accessed, transcendentals=0)
 
 
 def route(seq, batch, move):
@@ -64,11 +68,358 @@
         out_specs=[column(bins), column(bins)],
         out_shape=[jax.ShapeDtypeStruct((bins, width), jnp.bfloat16)] * 2,
         compiler_params=params(),
+        cost_estimate=cost(2 * bins * bins * width, 6 * bins * width),
         name="conv",
     )(coarse, skip, top, bottom, taps)
 
 
-def features_kernel(own, other, weight, bias, out):
+def softplus(v):
+    e = jnp.exp(-jnp.abs(v))
+    return jnp.maximum(v, 0.0) + jnp.where(e < 1e-4, e, jnp.log(1.0 + e))
+
+
+def gelu(v):
+    return jax.nn.gelu(v, approximate=True)
+
+
+def rows_by_rows(values, weight):
+    return lax.dot_general(
+        values, weight, (((1,), (1,)), ((), ())), preferred_element_type=jnp.float32
+    )
+
+
+def load_blocks(blocks, place, pieces, weight, sems, first):
+    copies = []
+    for i, (piece, start, rows, slot) in enumerate(blocks):
+        target = pl.multiple_of(place[slot] * rows, rows)
+        copies.append(
+            pltpu.make_async_copy(
+                pieces[piece].at[pl.ds(start, rows), :],
+                weight.at[pl.ds(target, rows), :],
+                sems.at[first + i],
+            )
+        )
+    for copy in copies:
+        copy.start()
+    return copies
+
+
+def columns_of(j, step):
+    return pl.ds(pl.multiple_of(j * step, step), step)
+
+
+def own_features_kernel(step, values, weight, bias, out):
+    product = jnp.dot(values[...], weight[...], preferred_element_type=jnp.float32)
+    out[...] = gelu(product + bias[...]).astype(jnp.bfloat16)
+
+
+def own_features(values, weight, bias):
+    rows, width = values.shape
+    step = 256
+    return pl.pallas_call(
+        functools.partial(own_features_kernel, step),
+        grid=(width // step,),
+        in_specs=[
+            pl.BlockSpec((rows, width), lambda j: (0, 0)),
+            pl.BlockSpec((width, step), lambda j: (0, j)),
+            pl.BlockSpec((1, step), lambda j: (0, j)),
+        ],
+        out_specs=pl.BlockSpec((rows, step), lambda j: (0, j)),
+        out_shape=jax.ShapeDtypeStruct((rows, width), jnp.bfloat16),
+        compiler_params=params(),
+        cost_estimate=cost(2 * rows * width * width, 2 * width * width),
+        name="own_features",
+    )(values, weight, bias)
+
+
+def own_near_kernel(blocks, step, place, values, bias, *rest):
+    *pieces, out, weight, sems = rest
+    for copy in load_blocks(blocks, place, pieces, weight, sems, 0):
+        copy.wait()
+
+    @pl.loop(0, out.shape[1] // step)
+    def _(j):
+        columns = columns_of(j, step)
+        product = rows_by_rows(values[...], weight[columns, :])
+        out[:, columns] = softplus(product + bias[:, columns]).astype(jnp.bfloat16)
+
+
+def own_near(values, bias, pieces, blocks, place):
+    rows, width = values.shape
+    tracks = bias.shape[1]
+    vmem = pl.BlockSpec(memory_space=pltpu.VMEM)
+    return pl.pallas_call(
+        functools.partial(own_near_kernel, blocks, 384),
+        in_specs=[pl.BlockSpec(memory_space=pltpu.SMEM), vmem, vmem]
+        + [pl.BlockSpec(memory_space=pl.ANY)] * len(pieces),
+        out_specs=vmem,
+        out_shape=jax.ShapeDtypeStruct((rows, tracks), jnp.bfloat16),
+        scratch_shapes=[
+            pltpu.VMEM((tracks, width), jnp.bfloat16),
+            pltpu.SemaphoreType.DMA((len(blocks),)),
+        ],
+        compiler_params=params(),
+        cost_estimate=cost(2 * rows * width * tracks, 2 * width * tracks),
+        name="own_near",
+    )(place, values, bias, *pieces)
+
+
+def finish_kernel(
+    near_blocks,
+    far_blocks,
+    place,
+    own_values,
+    other_values,
+    own_near_heads,
+    sep_bias,
+    head_bias,
+    pair,
+    sep_weight,
+    *rest,
+):
+    bins, width = own_values.shape
+    tracks = head_bias.shape[1]
+    half_tracks = tracks // 2
+    count = 1 + max(piece for piece, *_ in near_blocks)
+    near_pieces, far_pieces = rest[:count], rest[count : 2 * count]
+    out, sep, near, far, values, own, other, chosen, result, sems = rest[2 * count :]
+    sep_copy = pltpu.make_async_copy(sep_weight, sep, sems.at[0])
+    sep_copy.start()
+    near_copies = load_blocks(near_blocks, place, near_pieces, near, sems, 1)
+    far_copies = load_blocks(far_blocks, place, far_pieces, far, sems, 1 + len(near_blocks))
+    which = place[place.shape[0] - 1]
+    near_start = which * half_tracks
+    far_start = (1 - which) * half_tracks
+
+    values[:bins, :] = own_values[...]
+    sep_copy.wait()
+
+    @pl.loop(0, width // 256)
+    def _(j):
+        columns = columns_of(j, 256)
+        product = jnp.dot(
+            other_values[...], sep[:, columns], preferred_element_type=jnp.float32
+        )
+        values[bins:, columns] = gelu(product + sep_bias[:, columns]).astype(jnp.bfloat16)
+
+    step = 384
+    for copy in near_copies:
+        copy.wait()
+
+    @pl.loop(0, half_tracks // step)
+    def _(j):
+        columns = columns_of(j, step)
+        target = pl.ds(pl.multiple_of(near_start + j * step, 128), step)
+        product = rows_by_rows(values[bins:, :], near[columns, :])
+        other[:, target] = softplus(product + head_bias[:, target]).astype(jnp.bfloat16)
+        own[:, target] = own_near_heads[:, columns]
+
+    for copy in far_copies:
+        copy.wait()
+
+    @pl.loop(0, half_tracks // step)
+    def _(j):
+        columns = columns_of(j, step)
+        target = pl.ds(pl.multiple_of(far_start + j * step, 128), step)
+        product = rows_by_rows(values[...], far[columns, :])
+        heads = softplus(product + head_bias[:, target]).astype(jnp.bfloat16)
+        own[:, target] = heads[:bins]
+        other[:, target] = heads[bins:]
+
+    step = 256
+
+    def choose(j, slot):
+        rows = lax.broadcasted_iota(jnp.int32, (tracks, step), 0)
+        hit = rows == pair[:, columns_of(j, step)]
+        chosen[slot] = jnp.where(hit, 1.0, 0.0).astype(jnp.bfloat16)
+
+    def result_copy(j):
+        columns = columns_of(j, step)
+        return pltpu.make_async_copy(
+            result.at[:, columns], out.at[:, columns], sems.at[sems.shape[0] - 1]
+        )
+
+    def combine(j, slot):
+        columns = columns_of(j, step)
+        received = jnp.dot(other[...], chosen[slot], preferred_element_type=jnp.float32)
+        average = 0.5 * (own[:, columns].astype(jnp.float32) + received)
+        result[:, columns] = average.astype(jnp.bfloat16)
+
+    last = tracks // step - 1
+    choose(0, 0)
+
+    @pl.loop(0, last // 2)
+    def _(i):
+        combine(2 * i, 0)
+        choose(2 * i + 1, 1)
+        combine(2 * i + 1, 1)
+        choose(2 * i + 2, 0)
+
+    if last % 2:
+        combine(last - 1, 0)
+        choose(last, 1)
+    combine(last, last % 2)
+    done = pltpu.make_async_copy(result, out, sems.at[sems.shape[0] - 1])
+    done.start()
+    done.wait()
+
+
+def finish(
+    place, own_values, other_values, own_near_heads, sep_bias, head_bias, pair, sep_weight,
+    near_pieces, far_pieces, near_blocks, far_blocks,
+):
+    bins, width = own_values.shape
+    tracks = head_bias.shape[1]
+    vmem = pl.BlockSpec(memory_space=pltpu.VMEM)
+    anywhere = pl.BlockSpec(memory_space=pl.ANY)
+    bf16 = lambda *shape: pltpu.VMEM(shape, jnp.bfloat16)
+    return pl.pallas_call(
+        functools.partial(finish_kernel, near_blocks, far_blocks),
+        in_specs=[pl.BlockSpec(memory_space=pltpu.SMEM)]
+        + [vmem] * 6
+        + [anywhere] * (1 + len(near_pieces) + len(far_pieces)),
+        out_specs=anywhere,
+        out_shape=jax.ShapeDtypeStruct((bins, tracks), jnp.bfloat16),
+        scratch_shapes=[
+            bf16(width, width),
+            bf16(tracks // 2, width),
+            bf16(tracks // 2, width),
+            bf16(2 * bins, width),
+            bf16(bins, tracks),
+            bf16(bins, tracks),
+            bf16(2, tracks, 256),
+            bf16(bins, tracks),
+            pltpu.SemaphoreType.DMA((2 + len(near_blocks) + len(far_blocks),)),
+        ],
+        compiler_params=params(),
+        cost_estimate=cost(8 * bins * tracks * tracks, 16 * bins * tracks),
+        name="finish",
+    )(
+        place, own_values, other_values, own_near_heads, sep_bias, head_bias, pair, sep_weight,
+        *near_pieces, *far_pieces,
+    )
+
+
+def along_line(s, b):
+    return s ^ 4, b
+
+
+def across_middle(s, b):
+    return ((3 - s // 4) * 4 + s % 4, b) if s // 4 in (1, 2) else None
+
+
+def to_line_ends(s, b):
+    return (s ^ 4, b) if s // 4 in (1, 2) else None
+
+
+def across_pair(s, b):
+    return s ^ 2, b
+
+
+def across_cores(s, b):
+    return s ^ 1, b
+
+
+def blocks_of(rows, first):
+    blocks = []
+    for group in range(2):
+        base, slot = 3 * group, first + 4 * group
+        blocks += [(base, 0, rows, slot), (base + 1, 0, rows, slot + 1)]
+        blocks += [(base + 2, 0, rows, slot + 2), (base + 2, rows, rows, slot + 3)]
+    return blocks
+
+
+def places():
+    s = lax.axis_index("seq")
+    z, y, c = s // 4, (s // 2) % 2, s % 2
+    inner = jnp.where(z < 2, 2, 1)
+    result = []
+    for zz in (z, z ^ 1, inner, inner ^ 1):
+        for core in (c, 1 - c):
+            for yy in (y, 1 - y):
+                result.append((zz % 2) * 4 + yy * 2 + core)
+    return jnp.stack(result + [s // 8]).astype(jnp.int32)
+
+
+def edge(coarse_row, skip_row):
+    total = coarse_row.astype(jnp.float32) + skip_row.astype(jnp.float32)
+    return total.astype(jnp.bfloat16)
+
+
+def tied(*trees):
+    return lax.optimization_barrier(trees)
+
+
+def per_device_tree(
+    coarse, skip, depth_kernel, sep_weight, sep_bias, head_weight, head_bias, strand_pair
+):
+    seq, batch = lax.axis_size("seq"), lax.axis_size("batch")
+    coarse, skip = coarse[0], skip[0]
+    bins = skip.shape[0]
+    sep = gather_rows(sep_weight)
+    first = edge(coarse[:1], skip[:1])
+    last = edge(coarse[-1:], skip[-1:])
+    top = send(last, lambda s, b: (s + 1, b) if s + 1 < seq else None)
+    bottom = send(first, lambda s, b: (s - 1, b) if s > 0 else None)
+    to_mirror = lambda s, b: (seq - 1 - s, (b + batch // 2) % batch)
+    z = lax.axis_index("seq") // 4
+    pick = lambda a, c: jnp.where((z == 1) | (z == 2), a, c)
+    pair_of = lambda a, c: jnp.concatenate([a, c])
+
+    own = head_weight.T
+    near = send(own, along_line)
+    q0 = send(own, across_middle)
+    y0 = send(own, across_pair)
+    own_values, flipped = conv(coarse, skip, top, bottom, depth_kernel)
+    near, q0, y0, flipped = tied(near, q0, y0, flipped)
+
+    q1 = send(near, across_middle)
+    y1 = send(near, across_pair)
+    s0 = send(q0, to_line_ends)
+    c0 = send(pair_of(own, y0), across_cores)
+    q1, y1, s0, c0, flipped = tied(q1, y1, s0, c0, flipped)
+
+    m0 = send(flipped[: bins // 2], to_mirror)
+    o0 = pick(q0, s0)
+    y2 = send(o0, across_pair)
+    s1 = send(q1, to_line_ends)
+    c1 = send(pair_of(near, y1), across_cores)
+    m0, y2, s1, c1, sep, flipped = tied(m0, y2, s1, c1, sep, flipped)
+
+    m1 = send(flipped[bins // 2 :], to_mirror)
+    o1 = pick(q1, s1)
+    y3 = send(o1, across_pair)
+    c2 = send(pair_of(o0, y2), across_cores)
+    place = places()
+    rows = own.shape[0]
+    values = own_features(own_values, sep, sep_bias[None])
+    near_pieces = [own, y0, c0, near, y1, c1]
+    half = place[-1]
+    bias = lax.dynamic_slice_in_dim(
+        head_bias[None], half * (head_bias.shape[0] // 2), head_bias.shape[0] // 2, axis=1
+    )
+    near_blocks = blocks_of(rows, 0)
+    own_heads = own_near(values, bias, near_pieces, near_blocks, place)
+    m1, y3, c2, own_heads = tied(m1, y3, c2, own_heads)
+
+    c3 = send(pair_of(o1, y3), across_cores)
+    return finish(
+        place,
+        values,
+        jnp.concatenate([m0, m1]),
+        own_heads,
+        sep_bias[None],
+        head_bias[None],
+        strand_pair[None],
+        sep,
+        near_pieces,
+        [o0, y2, c2, o1, y3, c3],
+        near_blocks,
+        blocks_of(rows, 8),
+    )[None]
+
+
+def plain_features_kernel(own, other, weight, bias, out):
     bins = own.shape[0]
     for place, part in enumerate((own, other)):
         product = jnp.dot(part[...], weight[...], preferred_element_type=jnp.float32)
@@ -77,12 +428,12 @@
         ).astype(jnp.bfloat16)
 
 
-def features(own, other, weight, bias):
+def plain_features(own, other, weight, bias):
     bins, width = own.shape
     step = 256
     whole = pl.BlockSpec((bins, width), lambda j: (0, 0))
     return pl.pallas_call(
-        features_kernel,
+        plain_features_kernel,
         grid=(width // step,),
         in_specs=[
             whole,
@@ -97,23 +448,19 @@
     )(own, other, weight, bias)
 
 
-def softplus(v):
-    return jnp.maximum(v, 0.0) + jnp.log1p(jnp.exp(-jnp.abs(v)))
-
-
-def heads_kernel(values, weight, bias, out):
+def plain_heads_kernel(values, weight, bias, out):
     product = lax.dot_general(
         values[...], weight[...], (((1,), (1,)), ((), ())), preferred_element_type=jnp.float32
     )
     out[...] = softplus(product + bias[...]).astype(jnp.bfloat16)
 
 
-def heads(values, weight, bias):
+def plain_heads(values, weight, bias):
     rows, width = values.shape
     tracks = weight.shape[0]
     step = 256
     return pl.pallas_call(
-        heads_kernel,
+        plain_heads_kernel,
         grid=(tracks // step,),
         in_specs=[
             pl.BlockSpec((rows, width), lambda j: (0, 0)),
@@ -127,7 +474,7 @@
     )(values, weight, bias)
 
 
-def average_kernel(own, other, pair, out):
+def plain_average_kernel(own, other, pair, out):
     tracks = other.shape[1]
     rows = lax.broadcasted_iota(jnp.int32, (tracks, pair.shape[1]), 0)
     chosen = jnp.where(rows == pair[...], 1.0, 0.0).astype(jnp.bfloat16)
@@ -135,12 +482,12 @@
     out[...] = (0.5 * (own[...].astype(jnp.float32) + received)).astype(jnp.bfloat16)
 
 
-def average(both, pair):
+def plain_average(both, pair):
     rows, tracks = both.shape
     bins = rows // 2
     step = 256
     return pl.pallas_call(
-        average_kernel,
+        plain_average_kernel,
         grid=(tracks // step,),
         in_specs=[
             pl.BlockSpec((bins, step), lambda j: (0, j)),
@@ -161,12 +508,7 @@
     return lax.all_gather(mine, BOTH, axis=0, tiled=True)
 
 
-def edge(coarse_row, skip_row):
-    total = coarse_row.astype(jnp.float32) + skip_row.astype(jnp.float32)
-    return total.astype(jnp.bfloat16)
-
-
-def per_device(
+def per_device_plain(
     coarse, skip, depth_kernel, sep_weight, sep_bias, head_weight, head_bias, strand_pair
 ):
     seq, batch = lax.axis_size("seq"), lax.axis_size("batch")
@@ -177,12 +519,13 @@
     bottom = send(first, lambda s, b: (s - 1, b) if s > 0 else None)
     own, flipped = conv(coarse, skip, top, bottom, depth_kernel)
     other = send(flipped, lambda s, b: (seq - 1 - s, (b + batch // 2) % batch))
-    values = features(own, other, gather_rows(sep_weight), sep_bias[None])
-    both = heads(values, gather_rows(head_weight.T), head_bias[None])
-    return average(both, strand_pair[None])[None]
+    values = plain_features(own, other, gather_rows(sep_weight), sep_bias[None])
+    both = plain_heads(values, gather_rows(head_weight.T), head_bias[None])
+    return plain_average(both, strand_pair[None])[None]
 
 
 def solution(mesh):
+    tree = mesh.shape["seq"] == 16 and mesh.shape["batch"] == 2
     in_specs = (
         P("batch", "seq", None),
         P("batch", "seq", None),
@@ -195,5 +538,9 @@
     )
     out_specs = P("batch", "seq", None)
     return jax.shard_map(
-        per_device, mesh=mesh, in_specs=in_specs, out_specs=out_specs, check_vma=False
-    )
+        per_device_tree if tree else per_device_plain,
+        mesh=mesh,
+        in_specs=in_specs,
+        out_specs=out_specs,
+        check_vma=False,
+    )

time: 265 us -> 219 us (0.83); the launches traced: 265 us -> 215 us
  waiting for transfers between devices: 175 us -> 78.8 us
  starting transfers between devices: 7.85 us -> 35.1 us
  Pallas kernels: 62.2 us -> 70.9 us
  local copies, waits for them, and re-layouts: 4.83 us -> 10.8 us
  other arithmetic: 0.82 us -> 6.15 us
    all_gather x2 -> x1, waiting for transfers between devices: 138 us -> 0.01 us  [gather_rows(): return lax.all_gather(mine, BOTH, axis=0, tiled=True)]
    ppermute x3 -> x17, waiting for transfers between devices: 37.5 us -> 78.8 us  [send(): return lax.ppermute(array, BOTH, route(seq, batch, move))]
    ppermute x3 -> x17, starting transfers between devices: 7.77 us -> 35.1 us  [send(): return lax.ppermute(array, BOTH, route(seq, batch, move))]
    pallas_call x3, Pallas kernels: 55.2 us -> 63.9 us  [the longest x1 44.9 us: finish(): pl.pallas_call(functools.partial(finish_kernel, near_blocks, far_blocks),...]
    unnamed x14 -> x48, local copies, waits for them, and re-layouts: 0.61 us -> 6.89 us
    concatenate x0 -> x5, other arithmetic: none -> 5.15 us  [the longest x4 3.88 us: per_device_tree(): pair_of = lambda a, c: jnp.concatenate([a, c])]
  transfers between devices with their start and end apart: 5 -> 18, of which waited for: 4 -> 7; matrix products, arithmetic and copies ran while one was open for 1% -> 3% of each run, Pallas kernels for 7% -> 12%
where the time goes in v2:
time: 219 us; the launch traced here: 215 us
  waiting for transfers between devices  78.8 us (36%)
  Pallas kernels  70.9 us (32%)
  starting transfers between devices  35.1 us (16%)
  between operations  13.6 us (6%)
  local copies, waits for them, and re-layouts  10.8 us (5%)
  other arithmetic  6.15 us (3%)
    ppermute x17, waiting for transfers between devices, send(): return lax.ppermute(array, BOTH, route(seq, batch, move))  78.8 us
    pallas_call x1, Pallas kernels, finish(): pl.pallas_call(functools.partial(finish_kernel, near_blocks, far_blocks),...  44.9 us
    ppermute x17, starting transfers between devices, send(): return lax.ppermute(array, BOTH, route(seq, batch, move))  35.1 us
    pallas_call x1, Pallas kernels, own_near(): pl.pallas_call(functools.partial(own_near_kernel, blocks, 384), in_specs=...  11.4 us
    pallas_call x1, Pallas kernels, own_features(): pl.pallas_call(functools.partial(own_features_kernel, step), grid=(width...  7.67 us
    pallas_call x1, Pallas kernels, conv(): pl.pallas_call(conv_kernel, grid=(width // step,), in_specs=[column(coars...  6.95 us
    unnamed x48, local copies, waits for them, and re-layouts  6.89 us
  transfers between devices with their start and end apart: 18, of which 7 were waited for; matrix products, arithmetic and copies ran while one was open for 3% of the time, Pallas kernels for 12%

profile of v2, /device:TPU:0, one launch (start us, length us, event | category | flops | bytes accessed | tf_op | source)
XLA Modules:
  0.0 215.4 jit_solution(8503027862949082071)
XLA Ops:
  6.5 1.0 copy-done
  7.5 0.7 constant_dynamic-slice_fusion
  8.2 3.0 %collective-permute-start.4 = (bf16[240,1536]{1,0:T(8,128)(2,1)}, bf16[240,1536]{1,0:T(8,128)(2,1)S(1)}, u32[]{:S(2)}, u32[]{:S(2)}) collective-permute-start(bf16[240,1536]{1,0:T(8,128)(2,1)} %bitcast.25), channel_id=1, source_target_pairs={{0,4},{1,5},{2,6},{3,7},{4,0},{5,1},{6,2},{7,3},{8,12},{9,13},{10,... | collective-permute-start | bytes 2211848 | tf_op jit(solution)/shard_map/ppermute | solution.py:34
  11.2 0.7 collective-permute-start.3
  11.9 4.4 %collective-permute-start.2 = (bf16[240,1536]{1,0:T(8,128)(2,1)}, bf16[240,1536]{1,0:T(8,128)(2,1)S(1)}, u32[]{:S(2)}, u32[]{:S(2)}) collective-permute-start(bf16[240,1536]{1,0:T(8,128)(2,1)} %bitcast.27), channel_id=1, source_target_pairs={{0,8},{1,9},{2,10},{3,11},{4,12},{5,13},{6,14},{7,15},{8,0},{9,1},... | collective-permute-start | bytes 2211848 | tf_op jit(solution)/shard_map/ppermute | solution.py:34
  16.4 0.8 convert_bitcast_fusion
  17.2 1.3 collective-permute-start.1
  18.5 3.0 %collective-permute-start = (bf16[1,1536]{1,0:T(2,128)(2,1)S(1)}, bf16[1,1536]{1,0:T(2,128)(2,1)S(1)}, u32[]{:S(2)}, u32[]{:S(2)}) collective-permute-start(bf16[1,1536]{1,0:T(2,128)(2,1)S(1)} %get-tuple-element.48), channel_id=1, source_target_pairs={{0,2},{1,3},{2,4},{3,5},{4,6},{5,7},{6,8},{7,9},{8,10},{9,11},{10,... | collective-permute-start | bytes 9224 | tf_op jit(solution)/shard_map/ppermute | solution.py:34
  21.5 0.8 collective-permute-done.top
  22.3 0.6 copy-done.23
  22.9 6.9 %conv.1 = (bf16[512,1536]{1,0:T(8,128)(2,1)}, bf16[512,1536]{1,0:T(8,128)(2,1)}) custom-call(bf16[256,1536]{1,0:T(8,128)(2,1)} %bitcast.31, bf16[512,1536]{1,0:T(8,128)(2,1)} %bitcast.32, bf16[1,1536]{1,0:T(2,128)(2,1)} %copy-done.23, bf16[1,1536]{1,0:T(2,128)(2,1)} %copy-done.22, f32[3,1536]{1,0:T(4,128)} %taps.1), custom_call_target="tpu_custom_call" | custom-call | flops 805306368 | bytes 4718592 | tf_op jit(solution)/shard_map/conv/pallas_call | solution.py:64
  29.9 5.8 %collective-permute-done.2.rest_3_ = bf16[240,1536]{1,0:T(8,128)(2,1)S(1)} collective-permute-done((bf16[240,1536]{1,0:T(8,128)(2,1)}, bf16[240,1536]{1,0:T(8,128)(2,1)S(1)}, u32[]{:S(2)}, u32[]{:S(2)}) %collective-permute-start.2) | collective-permute-done | bytes 737312 | tf_op jit(solution)/shard_map/ppermute | solution.py:34
  35.7 0.1 pad_maximum_fusion.1
  35.8 2.0 collective-permute-start.8
  37.8 1.3 collective-permute-start.7
  39.1 7.9 %collective-permute-start.6 = (bf16[240,1536]{1,0:T(8,128)(2,1)S(1)}, bf16[240,1536]{1,0:T(8,128)(2,1)S(1)}, u32[]{:S(2)}, u32[]{:S(2)}) collective-permute-start(bf16[240,1536]{1,0:T(8,128)(2,1)S(1)} %collective-permute-done.2.rest_3_), channel_id=1, source_target_pairs={{0,4},{1,5},{2,6},{3,7},{4,0},{5,1},{6,2},{7,3},{8,12},{9,13},{10,... | collective-permute-start | bytes 2211848 | tf_op jit(solution)/shard_map/ppermute | solution.py:34
  47.0 0.7 collective-permute-start.5
  47.7 25.7 %collective-permute-done.7 = bf16[240,1536]{1,0:T(8,128)(2,1)S(1)} collective-permute-done((bf16[240,1536]{1,0:T(8,128)(2,1)S(1)}, bf16[240,1536]{1,0:T(8,128)(2,1)S(1)}, u32[]{:S(2)}, u32[]{:S(2)}) %collective-permute-start.7) | collective-permute-done | bytes 737312 | tf_op jit(solution)/shard_map/ppermute | solution.py:34
  73.4 0.8 copy-done.8
  74.3 0.3 copy-done.15
  74.6 1.3 pad_maximum_fusion.2
  75.9 0.3 copy-done.20
  76.2 0.1 collective-permute-start.12
  76.4 4.4 %collective-permute-start.9 = (bf16[256,1536]{1,0:T(8,128)(2,1)S(1)}, bf16[256,1536]{1,0:T(8,128)(2,1)S(1)}, u32[]{:S(2)}, u32[]{:S(2)}) collective-permute-start(bf16[256,1536]{1,0:T(8,128)(2,1)S(1)} %slice.26), channel_id=1, source_target_pairs={{0,31},{1,30},{2,29},{3,28},{4,27},{5,26},{6,25},{7,24},{8,23},{9,... | collective-permute-start | bytes 2359304 | tf_op jit(solution)/shard_map/ppermute | solution.py:34
  80.9 0.4 collective-permute-start.10
  81.3 0.9 copy-done.7
  82.2 1.3 collective-permute-start.11
  83.5 32.2 %collective-permute-done.10.rest_7_ = bf16[240,1536]{1,0:T(8,128)(2,1)S(1)} collective-permute-done((bf16[240,1536]{1,0:T(8,128)(2,1)S(1)}, bf16[240,1536]{1,0:T(8,128)(2,1)S(1)}, u32[]{:S(2)}, u32[]{:S(2)}) %collective-permute-start.10) | collective-permute-done | bytes 737312 | tf_op jit(solution)/shard_map/ppermute | solution.py:34
  115.7 0.5 collective-permute-done.11
  116.2 0.9 copy-done.10
  117.1 0.9 copy-done.4
  118.1 1.3 pad_maximum_fusion.3
  119.4 3.0 %collective-permute-start.13 = (bf16[256,1536]{1,0:T(8,128)(2,1)S(1)}, bf16[256,1536]{1,0:T(8,128)(2,1)S(1)}, u32[]{:S(2)}, u32[]{:S(2)}) collective-permute-start(bf16[256,1536]{1,0:T(8,128)(2,1)S(1)} %slice.27), channel_id=1, source_target_pairs={{0,31},{1,30},{2,29},{3,28},{4,27},{5,26},{6,25},{7,24},{8,23},{9,... | collective-permute-start | bytes 2359304 | tf_op jit(solution)/shard_map/ppermute | solution.py:34
  122.4 0.1 broadcast_select_fusion.rest_9_
  122.5 1.4 collective-permute-start.14
  123.9 0.6 broadcast_in_dim.14.bias.sep_bias
  124.6 0.6 dynamic_slice.7.bias
  125.2 0.7 stack.71.place
  125.9 7.7 %own_features.1.values.own_values = bf16[512,1536]{1,0:T(8,128)(2,1)} custom-call(bf16[512,1536]{1,0:T(8,128)(2,1)} %get-tuple-element.26.values, bf16[1536,1536]{1,0:T(8,128)(2,1)} %all-gather.2.cloned.1.call-done.weight.sep_weight, f32[1,1536]{1,0:T(1,128)} %broadcast_in_dim.14.bias.sep_bias), custom_call_target="tpu_custom_call" | custom-call | flops 2415919104 | bytes 4718592 | tf_op jit(solution)/shard_map/own_features/pallas_call | solution.py:119
  133.6 11.4 %own_near.1.own_near_heads = bf16[512,1920]{1,0:T(8,128)(2,1)} custom-call(s32[17]{0:T(128)} %stack.71.place, bf16[512,1536]{1,0:T(8,128)(2,1)} %own_features.1.values.own_values, f32[1,1920]{1,0:T(1,128)} %dynamic_slice.7.bias, bf16[240,1536]{1,0:T(8,128)(2,1)} %bitcast.28, bf16[240,1536]{1,0:T(8,128)(2,1)} %copy-done.13, bf16[480,1536]{1,0:T(8,128)(2,1)} %copy-done.20, ...), custom_call_target="tpu_custom_call" | custom-call | flops 3019898880 | bytes 5898240 | tf_op jit(solution)/shard_map/own_near/pallas_call | solution.py:151
  145.0 13.0 %collective-permute-done.14.rest_10_ = bf16[240,1536]{1,0:T(8,128)(2,1)} collective-permute-done((bf16[240,1536]{1,0:T(8,128)(2,1)S(1)}, bf16[240,1536]{1,0:T(8,128)(2,1)}, u32[]{:S(2)}, u32[]{:S(2)}) %collective-permute-start.14) | collective-permute-done | bytes 737312 | tf_op jit(solution)/shard_map/ppermute | solution.py:34
  158.0 1.2 pad_maximum_fusion.4
  159.3 0.6 broadcast_in_dim.15.head_bias
  159.9 0.6 broadcast_in_dim.16.pair
  160.5 1.3 pad_maximum_fusion.other_values
  161.8 0.8 collective-permute-done.16.rest_11_
  162.5 1.1 copy-done.21
  163.7 44.9 %finish.1 = bf16[512,3840]{1,0:T(8,128)(2,1)} custom-call(s32[17]{0:T(128)} %stack.71.place, bf16[512,1536]{1,0:T(8,128)(2,1)} %own_features.1.values.own_values, bf16[512,1536]{1,0:T(8,128)(2,1)} %pad_maximum_fusion.other_values, bf16[512,1920]{1,0:T(8,128)(2,1)} %own_near.1.own_near_heads, f32[1,1536]{1,0:T(1,128)} %broadcast_in_dim.14.bias.sep_bias, ...), custom_call_target="tpu_custom_call" | custom-call | flops 60397977600 | bytes 31457280 | tf_op jit(solution)/shard_map/finish/pallas_call | solution.py:276
  (58 shorter events, 0.5 us)
Async XLA Ops:
  6.5 1.0 copy-start
  6.5 111.5 %all-gather.2.cloned.1.call-start = ((), (), s32[]{:S(2)}) async-start(), calls=%async_computation | async-start | bytes 4866048 | tf_op jit(solution)/shard_map/all_gather | solution.py:508
  8.2 27.5 %copy-start.12 = (bf16[1536,240]{0,1:T(8,128)(2,1)S(1)}, bf16[1536,240]{0,1:T(8,128)(2,1)}, u32[]{:S(2)}) copy-start(bf16[1536,240]{0,1:T(8,128)(2,1)} %param.13) | copy-start | bytes 2211844
  8.2 21.7 %collective-permute-start.4 = (bf16[240,1536]{1,0:T(8,128)(2,1)}, bf16[240,1536]{1,0:T(8,128)(2,1)S(1)}, u32[]{:S(2)}, u32[]{:S(2)}) collective-permute-start(bf16[240,1536]{1,0:T(8,128)(2,1)} %bitcast.25), channel_id=1, source_target_pairs={{0,4},{1,5},{2,6},{3,7},{4,0},{5,1},{6,2},{7,3},{8,12},{9,13},{10,... | collective-permute-start | bytes 2211848 | tf_op jit(solution)/shard_map/ppermute | solution.py:34
  11.2 18.6 %collective-permute-start.3 = (bf16[240,1536]{1,0:T(8,128)(2,1)}, bf16[240,1536]{1,0:T(8,128)(2,1)S(1)}, u32[]{:S(2)}, u32[]{:S(2)}) collective-permute-start(bf16[240,1536]{1,0:T(8,128)(2,1)} %bitcast.26), channel_id=1, source_target_pairs={{8,16},{9,17},{10,18},{11,19},{12,20},{13,21},{14,22},{15,23},{16,... | collective-permute-start | bytes 2211848 | tf_op jit(solution)/shard_map/ppermute | solution.py:34
  11.9 23.7 %collective-permute-start.2 = (bf16[240,1536]{1,0:T(8,128)(2,1)}, bf16[240,1536]{1,0:T(8,128)(2,1)S(1)}, u32[]{:S(2)}, u32[]{:S(2)}) collective-permute-start(bf16[240,1536]{1,0:T(8,128)(2,1)} %bitcast.27), channel_id=1, source_target_pairs={{0,8},{1,9},{2,10},{3,11},{4,12},{5,13},{6,14},{7,15},{8,0},{9,1},... | collective-permute-start | bytes 2211848 | tf_op jit(solution)/shard_map/ppermute | solution.py:34
  17.2 4.3 %collective-permute-start.1 = (bf16[1,1536]{1,0:T(2,128)(2,1)S(1)}, bf16[1,1536]{1,0:T(2,128)(2,1)S(1)}, u32[]{:S(2)}, u32[]{:S(2)}) collective-permute-start(bf16[1,1536]{1,0:T(2,128)(2,1)S(1)} %get-tuple-element.47), channel_id=1, source_target_pairs={{2,0},{3,1},{4,2},{5,3},{6,4},{7,5},{8,6},{9,7},{10,8},{11,9},{12,... | collective-permute-start | bytes 9224 | tf_op jit(solution)/shard_map/ppermute | solution.py:34
  18.5 3.8 %collective-permute-start = (bf16[1,1536]{1,0:T(2,128)(2,1)S(1)}, bf16[1,1536]{1,0:T(2,128)(2,1)S(1)}, u32[]{:S(2)}, u32[]{:S(2)}) collective-permute-start(bf16[1,1536]{1,0:T(2,128)(2,1)S(1)} %get-tuple-element.48), channel_id=1, source_target_pairs={{0,2},{1,3},{2,4},{3,5},{4,6},{5,7},{6,8},{7,9},{8,10},{9,11},{10,... | collective-permute-start | bytes 9224 | tf_op jit(solution)/shard_map/ppermute | solution.py:34
  21.5 0.8 copy-start.22
  22.3 0.6 copy-start.23
  29.9 5.8 %copy-start.13 = (bf16[240,1536]{1,0:T(8,128)(2,1)}, bf16[240,1536]{1,0:T(8,128)(2,1)S(1)}, u32[]{:S(2)}) copy-start(bf16[240,1536]{1,0:T(8,128)(2,1)S(1)} %collective-permute-done.4.rest_1_) | copy-start | bytes 2211844
  35.7 40.2 %copy-start.14 = (bf16[240,1536]{1,0:T(8,128)(2,1)}, bf16[240,1536]{1,0:T(8,128)(2,1)S(1)}, u32[]{:S(2)}) copy-start(bf16[240,1536]{1,0:T(8,128)(2,1)S(1)} %collective-permute-done.2.rest_3_) | copy-start | bytes 2211844
  35.8 40.6 %copy-start.3 = (bf16[512,1536]{1,0:T(8,128)(2,1)S(1)}, bf16[512,1536]{1,0:T(8,128)(2,1)}, u32[]{:S(2)}) copy-start(bf16[512,1536]{1,0:T(8,128)(2,1)} %get-tuple-element.38) | copy-start | bytes 4718596
  35.8 38.5 %collective-permute-start.8 = (bf16[480,1536]{1,0:T(8,128)(2,1)S(1)}, bf16[480,1536]{1,0:T(8,128)(2,1)S(1)}, u32[]{:S(2)}, u32[]{:S(2)}) collective-permute-start(bf16[480,1536]{1,0:T(8,128)(2,1)S(1)} %pad_maximum_fusion.1), channel_id=1, source_target_pairs={{0,2},{1,3},{2,0},{3,1},{4,6},{5,7},{6,4},{7,5},{8,10},{9,11},{10,... | collective-permute-start | bytes 4423688 | tf_op jit(solution)/shard_map/ppermute | solution.py:34
  37.8 35.6 %collective-permute-start.7 = (bf16[240,1536]{1,0:T(8,128)(2,1)S(1)}, bf16[240,1536]{1,0:T(8,128)(2,1)S(1)}, u32[]{:S(2)}, u32[]{:S(2)}) collective-permute-start(bf16[240,1536]{1,0:T(8,128)(2,1)S(1)} %collective-permute-done.3), channel_id=1, source_target_pairs={{8,0},{9,1},{10,2},{11,3},{12,4},{13,5},{14,6},{15,7},{16,24},{17,... | collective-permute-start | bytes 2211848 | tf_op jit(solution)/shard_map/ppermute | solution.py:34
  39.1 34.4 %collective-permute-start.6 = (bf16[240,1536]{1,0:T(8,128)(2,1)S(1)}, bf16[240,1536]{1,0:T(8,128)(2,1)S(1)}, u32[]{:S(2)}, u32[]{:S(2)}) collective-permute-start(bf16[240,1536]{1,0:T(8,128)(2,1)S(1)} %collective-permute-done.2.rest_3_), channel_id=1, source_target_pairs={{0,4},{1,5},{2,6},{3,7},{4,0},{5,1},{6,2},{7,3},{8,12},{9,13},{10,... | collective-permute-start | bytes 2211848 | tf_op jit(solution)/shard_map/ppermute | solution.py:34
  47.0 26.4 %collective-permute-start.5 = (bf16[240,1536]{1,0:T(8,128)(2,1)S(1)}, bf16[240,1536]{1,0:T(8,128)(2,1)S(1)}, u32[]{:S(2)}, u32[]{:S(2)}) collective-permute-start(bf16[240,1536]{1,0:T(8,128)(2,1)S(1)} %collective-permute-done.2.rest_3_), channel_id=1, source_target_pairs={{8,16},{9,17},{10,18},{11,19},{12,20},{13,21},{14,22},{15,23},{16,... | collective-permute-start | bytes 2211848 | tf_op jit(solution)/shard_map/ppermute | solution.py:34
  73.4 0.9 copy-start.8
  73.4 1.1 copy-start.15
  74.3 2.1 copy-start.6
  74.6 1.6 copy-start.20
  76.2 41.8 %collective-permute-start.12 = (bf16[480,1536]{1,0:T(8,128)(2,1)}, bf16[480,1536]{1,0:T(8,128)(2,1)}, u32[]{:S(2)}, u32[]{:S(2)}) collective-permute-start(bf16[480,1536]{1,0:T(8,128)(2,1)} %pad_maximum_fusion.2), channel_id=1, source_target_pairs={{0,2},{1,3},{2,0},{3,1},{4,6},{5,7},{6,4},{7,5},{8,10},{9,11},{10,... | collective-permute-start | bytes 4423688 | tf_op jit(solution)/shard_map/ppermute | solution.py:34
  76.3 4.5 %copy-start.9 = (bf16[240,1536]{1,0:T(8,128)(2,1)S(1)}, bf16[240,1536]{1,0:T(8,128)(2,1)}, u32[]{:S(2)}) copy-start(bf16[240,1536]{1,0:T(8,128)(2,1)} %copy-done.8) | copy-start | bytes 2211844
  76.4 39.8 %collective-permute-start.9 = (bf16[256,1536]{1,0:T(8,128)(2,1)S(1)}, bf16[256,1536]{1,0:T(8,128)(2,1)S(1)}, u32[]{:S(2)}, u32[]{:S(2)}) collective-permute-start(bf16[256,1536]{1,0:T(8,128)(2,1)S(1)} %slice.26), channel_id=1, source_target_pairs={{0,31},{1,30},{2,29},{3,28},{4,27},{5,26},{6,25},{7,24},{8,23},{9,... | collective-permute-start | bytes 2359304 | tf_op jit(solution)/shard_map/ppermute | solution.py:34
  80.8 1.4 copy-start.7
  80.9 38.5 %copy-start.1 = (bf16[240,1536]{1,0:T(8,128)(2,1)}, bf16[240,1536]{1,0:T(8,128)(2,1)S(1)}, u32[]{:S(2)}) copy-start(bf16[240,1536]{1,0:T(8,128)(2,1)S(1)} %broadcast_select_fusion.1.rest_6_) | copy-start | bytes 2211844
  80.9 34.8 %collective-permute-start.10 = (bf16[240,1536]{1,0:T(8,128)(2,1)S(1)}, bf16[240,1536]{1,0:T(8,128)(2,1)S(1)}, u32[]{:S(2)}, u32[]{:S(2)}) collective-permute-start(bf16[240,1536]{1,0:T(8,128)(2,1)S(1)} %broadcast_select_fusion.1.rest_6_), channel_id=1, source_target_pairs={{0,4},{1,5},{2,6},{3,7},{4,0},{5,1},{6,2},{7,3},{8,12},{9,13},{10,... | collective-permute-start | bytes 2211848 | tf_op jit(solution)/shard_map/ppermute | solution.py:34
  82.2 34.0 %collective-permute-start.11 = (bf16[240,1536]{1,0:T(8,128)(2,1)S(1)}, bf16[240,1536]{1,0:T(8,128)(2,1)S(1)}, u32[]{:S(2)}, u32[]{:S(2)}) collective-permute-start(bf16[240,1536]{1,0:T(8,128)(2,1)S(1)} %copy-done.7), channel_id=1, source_target_pairs={{8,0},{9,1},{10,2},{11,3},{12,4},{13,5},{14,6},{15,7},{16,24},{17,... | collective-permute-start | bytes 2211848 | tf_op jit(solution)/shard_map/ppermute | solution.py:34
  115.7 3.6 %copy-start.16 = (bf16[240,1536]{1,0:T(8,128)(2,1)}, bf16[240,1536]{1,0:T(8,128)(2,1)S(1)}, u32[]{:S(2)}) copy-start(bf16[240,1536]{1,0:T(8,128)(2,1)S(1)} %collective-permute-done.10.rest_7_) | copy-start | bytes 2211844
  116.2 0.9 copy-start.10
  117.1 0.9 copy-start.4
  118.1 4.4 %copy-start.11 = (bf16[240,1536]{1,0:T(8,128)(2,1)S(1)}, bf16[240,1536]{1,0:T(8,128)(2,1)}, u32[]{:S(2)}) copy-start(bf16[240,1536]{1,0:T(8,128)(2,1)} %copy-done.10) | copy-start | bytes 2211844
  119.3 38.7 %collective-permute-start.15 = (bf16[480,1536]{1,0:T(8,128)(2,1)}, bf16[480,1536]{1,0:T(8,128)(2,1)}, u32[]{:S(2)}, u32[]{:S(2)}) collective-permute-start(bf16[480,1536]{1,0:T(8,128)(2,1)} %pad_maximum_fusion.3), channel_id=1, source_target_pairs={{0,2},{1,3},{2,0},{3,1},{4,6},{5,7},{6,4},{7,5},{8,10},{9,11},{10,... | collective-permute-start | bytes 4423688 | tf_op jit(solution)/shard_map/ppermute | solution.py:34
  119.4 4.5 %copy-start.19 = (f32[1536]{0:T(1024)S(1)}, f32[1536]{0:T(1024)}, u32[]{:S(2)}) copy-start(f32[1536]{0:T(1024)} %param.12) | copy-start | bytes 18436
  119.4 5.1 %copy-start.17 = (f32[3840]{0:T(1024)S(1)}, f32[3840]{0:T(1024)}, u32[]{:S(2)}) copy-start(f32[3840]{0:T(1024)} %param.14) | copy-start | bytes 46084
  119.4 38.5 %collective-permute-start.13 = (bf16[256,1536]{1,0:T(8,128)(2,1)S(1)}, bf16[256,1536]{1,0:T(8,128)(2,1)S(1)}, u32[]{:S(2)}, u32[]{:S(2)}) collective-permute-start(bf16[256,1536]{1,0:T(8,128)(2,1)S(1)} %slice.27), channel_id=1, source_target_pairs={{0,31},{1,30},{2,29},{3,28},{4,27},{5,26},{6,25},{7,24},{8,23},{9,... | collective-permute-start | bytes 2359304 | tf_op jit(solution)/shard_map/ppermute | solution.py:34
  122.5 35.4 %copy-start.2 = (bf16[240,1536]{1,0:T(8,128)(2,1)}, bf16[240,1536]{1,0:T(8,128)(2,1)S(1)}, u32[]{:S(2)}) copy-start(bf16[240,1536]{1,0:T(8,128)(2,1)S(1)} %broadcast_select_fusion.rest_9_) | copy-start | bytes 2211844
  122.5 35.4 %collective-permute-start.14 = (bf16[240,1536]{1,0:T(8,128)(2,1)S(1)}, bf16[240,1536]{1,0:T(8,128)(2,1)}, u32[]{:S(2)}, u32[]{:S(2)}) collective-permute-start(bf16[240,1536]{1,0:T(8,128)(2,1)S(1)} %broadcast_select_fusion.rest_9_), channel_id=1, source_target_pairs={{0,4},{1,5},{2,6},{3,7},{4,0},{5,1},{6,2},{7,3},{8,12},{9,13},{10,... | collective-permute-start | bytes 2211848 | tf_op jit(solution)/shard_map/ppermute | solution.py:34
  145.0 14.9 %copy-start.18 = (s32[3840]{0:T(1024)S(1)}, s32[3840]{0:T(1024)}, u32[]{:S(2)}) copy-start(s32[3840]{0:T(1024)} %param.15) | copy-start | bytes 46084
  145.0 15.5 %copy-start.5 = (bf16[256,1536]{1,0:T(8,128)(2,1)S(1)}, bf16[256,1536]{1,0:T(8,128)(2,1)}, u32[]{:S(2)}) copy-start(bf16[256,1536]{1,0:T(8,128)(2,1)} %copy-done.4) | copy-start | bytes 2359300
  159.2 3.3 %collective-permute-start.16 = (bf16[480,1536]{1,0:T(8,128)(2,1)S(1)}, bf16[480,1536]{1,0:T(8,128)(2,1)S(1)}, u32[]{:S(2)}, u32[]{:S(2)}) collective-permute-start(bf16[480,1536]{1,0:T(8,128)(2,1)S(1)} %pad_maximum_fusion.4), channel_id=1, source_target_pairs={{0,2},{1,3},{2,0},{3,1},{4,6},{5,7},{6,4},{7,5},{8,10},{9,11},{10,... | collective-permute-start | bytes 4423688 | tf_op jit(solution)/shard_map/ppermute | solution.py:34
  162.5 1.1 copy-start.21
Sparse Core Ops, SparseCore 0:
  10.3 72.7 all-gather.1

commit v3 on v1

--- a/solution.py
+++ b/solution.py
@@ -13,6 +13,10 @@
 
 def params():
     return pltpu.CompilerParams(vmem_limit_bytes=VMEM_LIMIT)
+
+
+def cost(flops, bytes_accessed):
+    return pl.CostEstimate(flops=flops, bytes_accessed=bytes_accessed, transcendentals=0)
 
 
 def route(seq, batch, move):
@@ -36,7 +40,7 @@
     return jnp.where(hit(rows, columns), 1.0, 0.0).astype(jnp.bfloat16)
 
 
-def conv_kernel(coarse, skip, top, bottom, taps, own, flipped):
+def conv_kernel(coarse, skip, top, bottom, taps, own, *flipped):
     bins = skip.shape[0]
     spread = one_hot((bins, coarse.shape[0]), lambda r, c: r // 2 == c)
     up = jnp.dot(spread, coarse[...], preferred_element_type=jnp.float32)
@@ -50,25 +54,264 @@
     result = result.astype(jnp.bfloat16)
     own[...] = result
     mirror = one_hot((bins, bins), lambda r, c: r + c == bins - 1)
-    flipped[...] = jnp.dot(mirror, result, preferred_element_type=jnp.float32).astype(jnp.bfloat16)
-
-
-def conv(coarse, skip, top, bottom, taps):
+    turned = jnp.dot(mirror, result, preferred_element_type=jnp.float32).astype(jnp.bfloat16)
+    start = 0
+    for part in flipped:
+        part[...] = turned[start : start + part.shape[0]]
+        start += part.shape[0]
+
+
+def conv(coarse, skip, top, bottom, taps, cut=()):
     bins, width = skip.shape
     step = 256
+    parts = [b - a for a, b in zip((0, *cut), (*cut, bins))]
     column = lambda rows: pl.BlockSpec((rows, step), lambda j: (0, j))
     return pl.pallas_call(
         conv_kernel,
         grid=(width // step,),
         in_specs=[column(coarse.shape[0]), column(bins), column(1), column(1), column(3)],
-        out_specs=[column(bins), column(bins)],
-        out_shape=[jax.ShapeDtypeStruct((bins, width), jnp.bfloat16)] * 2,
+        out_specs=[column(rows) for rows in (bins, *parts)],
+        out_shape=[jax.ShapeDtypeStruct((rows, width), jnp.bfloat16) for rows in (bins, *parts)],
         compiler_params=params(),
+        cost_estimate=cost(2 * bins * bins * width, 6 * bins * width),
         name="conv",
     )(coarse, skip, top, bottom, taps)
 
 
-def features_kernel(own, other, weight, bias, out):
+def softplus(v):
+    e = jnp.exp(-jnp.abs(v))
+    return jnp.maximum(v, 0.0) + jnp.where(e < 1e-4, e, jnp.log(1.0 + e))
+
+
+def gelu(v):
+    return jax.nn.gelu(v, approximate=True)
+
+
+def rows_by_rows(values, weight):
+    return lax.dot_general(
+        values, weight, (((1,), (1,)), ((), ())), preferred_element_type=jnp.float32
+    )
+
+
+def columns_of(j, step):
+    return pl.ds(pl.multiple_of(j * step, step), step)
+
+
+def finish_kernel(place, sep_bias, head_bias, pair, own_values, *rest):
+    shards = place.shape[0]
+    parts = len(rest) - shards - 10
+    others, pieces = rest[:parts], rest[parts : parts + shards]
+    out, sep, head, inputs, values, own, other, chosen, result, sems = rest[parts + shards :]
+    bins, tracks = own.shape
+    width = values.shape[1]
+    depth = width // shards
+    share = tracks // shards
+    copies = []
+
+    def fetch(source, target):
+        copy = pltpu.make_async_copy(source, target, sems.at[len(copies)])
+        copy.start()
+        copies.append(copy)
+
+    fetch(own_values, inputs.at[pl.ds(0, bins), :])
+    start = bins
+    for part in others:
+        fetch(part, inputs.at[pl.ds(start, part.shape[0]), :])
+        start += part.shape[0]
+    for i, piece in enumerate(pieces):
+        target = pl.multiple_of(place[i] * depth, depth)
+        fetch(piece.at[pl.ds(0, depth), :], sep.at[pl.ds(target, depth), :])
+    first = len(copies)
+    for i, piece in enumerate(pieces):
+        target = pl.multiple_of(place[i] * share, share)
+        fetch(piece.at[pl.ds(depth, share), :], head.at[pl.ds(target, share), :])
+    for copy in copies[:first]:
+        copy.wait()
+
+    @pl.loop(0, width // 256)
+    def _(j):
+        columns = columns_of(j, 256)
+        product = jnp.dot(inputs[...], sep[:, columns], preferred_element_type=jnp.float32)
+        values[:, columns] = gelu(product + sep_bias[:, columns]).astype(jnp.bfloat16)
+
+    for copy in copies[first:]:
+        copy.wait()
+    step = 256
+
+    @pl.loop(0, tracks // step)
+    def _(j):
+        columns = columns_of(j, step)
+        product = rows_by_rows(values[...], head[columns, :])
+        heads = softplus(product + head_bias[:, columns]).astype(jnp.bfloat16)
+        own[:, columns] = heads[:bins]
+        other[:, columns] = heads[bins:]
+
+    used = len(copies)
+
+    def choose(j, slot):
+        rows = lax.broadcasted_iota(jnp.int32, (tracks, step), 0)
+        hit = rows == pair[:, columns_of(j, step)]
+        chosen[slot] = jnp.where(hit, 1.0, 0.0).astype(jnp.bfloat16)
+
+    def result_copy(j):
+        columns = columns_of(j, step)
+        return pltpu.make_async_copy(
+            result.at[:, columns], out.at[:, columns], sems.at[used + j]
+        )
+
+    def combine(j, slot):
+        columns = columns_of(j, step)
+        received = jnp.dot(other[...], chosen[slot], preferred_element_type=jnp.float32)
+        average = 0.5 * (own[:, columns].astype(jnp.float32) + received)
+        result[:, columns] = average.astype(jnp.bfloat16)
+        result_copy(j).start()
+
+    last = tracks // step - 1
+    choose(0, 0)
+
+    @pl.loop(0, last // 2)
+    def _(i):
+        combine(2 * i, 0)
+        choose(2 * i + 1, 1)
+        combine(2 * i + 1, 1)
+        choose(2 * i + 2, 0)
+
+    if last % 2:
+        combine(last - 1, 0)
+        choose(last, 1)
+    combine(last, last % 2)
+    for j in range(last + 1):
+        result_copy(j).wait()
+
+
+def finish(place, sep_bias, head_bias, pair, own_values, others, pieces):
+    bins, width = own_values.shape
+    tracks = head_bias.shape[1]
+    vmem = pl.BlockSpec(memory_space=pltpu.VMEM)
+    anywhere = pl.BlockSpec(memory_space=pl.ANY)
+    bf16 = lambda *shape: pltpu.VMEM(shape, jnp.bfloat16)
+    count = 1 + len(others) + 2 * len(pieces) + tracks // 256
+    return pl.pallas_call(
+        finish_kernel,
+        in_specs=[pl.BlockSpec(memory_space=pltpu.SMEM)]
+        + [vmem] * 3
+        + [anywhere] * (1 + len(others) + len(pieces)),
+        out_specs=anywhere,
+        out_shape=jax.ShapeDtypeStruct((bins, tracks), jnp.bfloat16),
+        scratch_shapes=[
+            bf16(width, width),
+            bf16(tracks, width),
+            bf16(2 * bins, width),
+            bf16(2 * bins, width),
+            bf16(bins, tracks),
+            bf16(bins, tracks),
+            bf16(2, tracks, 256),
+            bf16(bins, tracks),
+            pltpu.SemaphoreType.DMA((count,)),
+        ],
+        compiler_params=params(),
+        cost_estimate=cost(8 * bins * tracks * tracks, 16 * bins * tracks),
+        name="finish",
+    )(place, sep_bias, head_bias, pair, own_values, *others, *pieces)
+
+
+def along_line(s, b):
+    return s ^ 4, b
+
+
+def across_middle(s, b):
+    return ((3 - s // 4) * 4 + s % 4, b) if s // 4 in (1, 2) else None
+
+
+def to_line_ends(s, b):
+    return (s ^ 4, b) if s // 4 in (1, 2) else None
+
+
+def across_pair(s, b):
+    return s ^ 2, b
+
+
+def across_cores(s, b):
+    return s ^ 1, b
+
+
+def places():
+    s = lax.axis_index("seq")
+    z, y, c = s // 4, (s // 2) % 2, s % 2
+    inner = jnp.where(z < 2, 2, 1)
+    result = []
+    for zz in (z, z ^ 1, inner, inner ^ 1):
+        for core in (c, 1 - c):
+            for yy in (y, 1 - y):
+                result.append(zz * 4 + yy * 2 + core)
+    return jnp.stack(result).astype(jnp.int32)
+
+
+def edge(coarse_row, skip_row):
+    total = coarse_row.astype(jnp.float32) + skip_row.astype(jnp.float32)
+    return total.astype(jnp.bfloat16)
+
+
+def tied(*trees):
+    return lax.optimization_barrier(trees)
+
+
+def per_device_tree(
+    coarse, skip, depth_kernel, sep_weight, sep_bias, head_weight, head_bias, strand_pair
+):
+    seq, batch = lax.axis_size("seq"), lax.axis_size("batch")
+    coarse, skip = coarse[0], skip[0]
+    first = edge(coarse[:1], skip[:1])
+    last = edge(coarse[-1:], skip[-1:])
+    top = send(last, lambda s, b: (s + 1, b) if s + 1 < seq else None)
+    bottom = send(first, lambda s, b: (s - 1, b) if s > 0 else None)
+    to_mirror = lambda s, b: (seq - 1 - s, (b + batch // 2) % batch)
+    z = lax.axis_index("seq") // 4
+    pick = lambda a, c: jnp.where((z == 1) | (z == 2), a, c)
+
+    own = jnp.concatenate([sep_weight, head_weight.T])
+    near = send(own, along_line)
+    q0 = send(own, across_middle)
+    y0 = send(own, across_pair)
+    k_own = send(own, across_cores)
+    small = (sep_bias[None], head_bias[None], strand_pair[None], places())
+    edges = (top, bottom)
+    near, q0, y0, k_own, edges, small = tied(near, q0, y0, k_own, edges, small)
+    sep_bias, head_bias, strand_pair, place = small
+
+    top, bottom = edges
+    own_values, *flipped = conv(coarse, skip, top, bottom, depth_kernel, (skip.shape[0] // 2,))
+    q1 = send(near, across_middle)
+    y1 = send(near, across_pair)
+    s0 = send(q0, to_line_ends)
+    k_y0 = send(y0, across_cores)
+    k_near = send(near, across_cores)
+    q1, y1, s0, k_y0, k_near, flipped, own_values = tied(
+        q1, y1, s0, k_y0, k_near, flipped, own_values
+    )
+
+    m0 = send(flipped[0], to_mirror)
+    o0 = pick(q0, s0)
+    y2 = send(o0, across_pair)
+    s1 = send(q1, to_line_ends)
+    k_y1 = send(y1, across_cores)
+    k_o0 = send(o0, across_cores)
+    m0, y2, s1, k_y1, k_o0, flipped = tied(m0, y2, s1, k_y1, k_o0, flipped)
+
+    m1 = send(flipped[1], to_mirror)
+    o1 = pick(q1, s1)
+    y3 = send(o1, across_pair)
+    k_y2 = send(y2, across_cores)
+    k_o1 = send(o1, across_cores)
+    m1, y3, k_y2, k_o1 = tied(m1, y3, k_y2, k_o1)
+
+    k_y3 = send(y3, across_cores)
+    pieces = [own, y0, k_own, k_y0, near, y1, k_near, k_y1]
+    pieces += [o0, y2, k_o0, k_y2, o1, y3, k_o1, k_y3]
+    return finish(place, sep_bias, head_bias, strand_pair, own_values, [m0, m1], pieces)[None]
+
+
+def plain_features_kernel(own, other, weight, bias, out):
     bins = own.shape[0]
     for place, part in enumerate((own, other)):
         product = jnp.dot(part[...], weight[...], preferred_element_type=jnp.float32)
@@ -77,12 +320,12 @@
         ).astype(jnp.bfloat16)
 
 
-def features(own, other, weight, bias):
+def plain_features(own, other, weight, bias):
     bins, width = own.shape
     step = 256
     whole = pl.BlockSpec((bins, width), lambda j: (0, 0))
     return pl.pallas_call(
-        features_kernel,
+        plain_features_kernel,
         grid=(width // step,),
         in_specs=[
             whole,
@@ -97,23 +340,19 @@
     )(own, other, weight, bias)
 
 
-def softplus(v):
-    return jnp.maximum(v, 0.0) + jnp.log1p(jnp.exp(-jnp.abs(v)))
-
-
-def heads_kernel(values, weight, bias, out):
+def plain_heads_kernel(values, weight, bias, out):
     product = lax.dot_general(
         values[...], weight[...], (((1,), (1,)), ((), ())), preferred_element_type=jnp.float32
     )
     out[...] = softplus(product + bias[...]).astype(jnp.bfloat16)
 
 
-def heads(values, weight, bias):
+def plain_heads(values, weight, bias):
     rows, width = values.shape
     tracks = weight.shape[0]
     step = 256
     return pl.pallas_call(
-        heads_kernel,
+        plain_heads_kernel,
         grid=(tracks // step,),
         in_specs=[
             pl.BlockSpec((rows, width), lambda j: (0, 0)),
@@ -127,7 +366,7 @@
     )(values, weight, bias)
 
 
-def average_kernel(own, other, pair, out):
+def plain_average_kernel(own, other, pair, out):
     tracks = other.shape[1]
     rows = lax.broadcasted_iota(jnp.int32, (tracks, pair.shape[1]), 0)
     chosen = jnp.where(rows == pair[...], 1.0, 0.0).astype(jnp.bfloat16)
@@ -135,12 +374,12 @@
     out[...] = (0.5 * (own[...].astype(jnp.float32) + received)).astype(jnp.bfloat16)
 
 
-def average(both, pair):
+def plain_average(both, pair):
     rows, tracks = both.shape
     bins = rows // 2
     step = 256
     return pl.pallas_call(
-        average_kernel,
+        plain_average_kernel,
         grid=(tracks // step,),
         in_specs=[
             pl.BlockSpec((bins, step), lambda j: (0, j)),
@@ -161,12 +400,7 @@
     return lax.all_gather(mine, BOTH, axis=0, tiled=True)
 
 
-def edge(coarse_row, skip_row):
-    total = coarse_row.astype(jnp.float32) + skip_row.astype(jnp.float32)
-    return total.astype(jnp.bfloat16)
-
-
-def per_device(
+def per_device_plain(
     coarse, skip, depth_kernel, sep_weight, sep_bias, head_weight, head_bias, strand_pair
 ):
     seq, batch = lax.axis_size("seq"), lax.axis_size("batch")
@@ -177,12 +411,13 @@
     bottom = send(first, lambda s, b: (s - 1, b) if s > 0 else None)
     own, flipped = conv(coarse, skip, top, bottom, depth_kernel)
     other = send(flipped, lambda s, b: (seq - 1 - s, (b + batch // 2) % batch))
-    values = features(own, other, gather_rows(sep_weight), sep_bias[None])
-    both = heads(values, gather_rows(head_weight.T), head_bias[None])
-    return average(both, strand_pair[None])[None]
+    values = plain_features(own, other, gather_rows(sep_weight), sep_bias[None])
+    both = plain_heads(values, gather_rows(head_weight.T), head_bias[None])
+    return plain_average(both, strand_pair[None])[None]
 
 
 def solution(mesh):
+    tree = mesh.shape["seq"] == 16 and mesh.shape["batch"] == 2
     in_specs = (
         P("batch", "seq", None),
         P("batch", "seq", None),
@@ -195,5 +430,9 @@
     )
     out_specs = P("batch", "seq", None)
     return jax.shard_map(
-        per_device, mesh=mesh, in_specs=in_specs, out_specs=out_specs, check_vma=False
-    )
+        per_device_tree if tree else per_device_plain,
+        mesh=mesh,
+        in_specs=in_specs,
+        out_specs=out_specs,
+        check_vma=False,
+    )

time: 265 us -> 206 us (0.78)
  waiting for transfers between devices: 175 us -> 98.9 us
  starting transfers between devices: 7.85 us -> 45.5 us
  between operations: 13.5 us -> 0.3 us
  Pallas kernels: 62.2 us -> 54.1 us
    all_gather x2 -> x0, waiting for transfers between devices: 138 us -> none  [gather_rows(): return lax.all_gather(mine, BOTH, axis=0, tiled=True)]
    ppermute x3 -> x21, waiting for transfers between devices: 37.5 us -> 98.9 us  [send(): return lax.ppermute(array, BOTH, route(seq, batch, move))]
    ppermute x3 -> x21, starting transfers between devices: 7.77 us -> 45.5 us  [send(): return lax.ppermute(array, BOTH, route(seq, batch, move))]
    pallas_call x3 -> x1, Pallas kernels: 55.2 us -> 47.3 us  [finish(): pl.pallas_call(finish_kernel, in_specs=[pl.BlockSpec(memory_space=pltpu.S...]
  transfers between devices with their start and end apart: 5 -> 21, of which waited for: 4 -> 9; matrix products, arithmetic and copies ran while one was open for 1% -> 2% of each run, Pallas kernels for 7% -> 3%
where the time goes in v3:
time: 206 us
  waiting for transfers between devices  98.9 us (48%)
  Pallas kernels  54.1 us (26%)
  starting transfers between devices  45.5 us (22%)
  local copies, waits for them, and re-layouts  4.5 us (2%)
  other arithmetic  2.32 us (1%)
    ppermute x21, waiting for transfers between devices, send(): return lax.ppermute(array, BOTH, route(seq, batch, move))  98.9 us
    pallas_call x1, Pallas kernels, finish(): pl.pallas_call(finish_kernel, in_specs=[pl.BlockSpec(memory_space=pltpu.S...  47.3 us
    ppermute x21, starting transfers between devices, send(): return lax.ppermute(array, BOTH, route(seq, batch, move))  45.5 us
    pallas_call x1, Pallas kernels, conv(): pl.pallas_call(conv_kernel, grid=(width // step,), in_specs=[column(coars...  6.82 us
  transfers between devices with their start and end apart: 21, of which 9 were waited for; matrix products, arithmetic and copies ran while one was open for 2% of the time, Pallas kernels for 3%

profile of v3, /device:TPU:0, one launch (start us, length us, event | category | flops | bytes accessed | tf_op | source)
XLA Modules:
  0.0 205.6 jit_solution(5191307285737482658)
XLA Ops:
  0.0 1.3 pad_maximum_fusion.rest_2_
  1.3 0.5 collective-permute-start.3
  1.8 2.6 %collective-permute-start.2 = (bf16[336,1536]{1,0:T(8,128)(2,1)S(1)}, bf16[336,1536]{1,0:T(8,128)(2,1)}, u32[]{:S(2)}, u32[]{:S(2)}) collective-permute-start(bf16[336,1536]{1,0:T(8,128)(2,1)S(1)} %pad_maximum_fusion.rest_2_), channel_id=1, source_target_pairs={{0,4},{1,5},{2,6},{3,7},{4,0},{5,1},{6,2},{7,3},{8,12},{9,13},{10,... | collective-permute-start | bytes 3096584 | tf_op jit(solution)/shard_map/ppermute | solution.py:34
  4.4 0.7 collective-permute-start.1
  5.1 4.4 %collective-permute-start = (bf16[336,1536]{1,0:T(8,128)(2,1)S(1)}, bf16[336,1536]{1,0:T(8,128)(2,1)}, u32[]{:S(2)}, u32[]{:S(2)}) collective-permute-start(bf16[336,1536]{1,0:T(8,128)(2,1)S(1)} %pad_maximum_fusion.rest_2_), channel_id=1, source_target_pairs={{0,8},{1,9},{2,10},{3,11},{4,12},{5,13},{6,14},{7,15},{8,0},{9,1},... | collective-permute-start | bytes 3096584 | tf_op jit(solution)/shard_map/ppermute | solution.py:34
  9.5 0.8 convert_bitcast_fusion
  10.4 1.3 collective-permute-start.5
  11.7 1.7 collective-permute-done.5.bottom
  13.4 16.6 %collective-permute-start.4 = (bf16[1,1536]{1,0:T(2,128)(2,1)S(1)}, bf16[1,1536]{1,0:T(2,128)(2,1)S(1)}, u32[]{:S(2)}, u32[]{:S(2)}) collective-permute-start(bf16[1,1536]{1,0:T(2,128)(2,1)S(1)} %get-tuple-element.68), channel_id=1, source_target_pairs={{0,2},{1,3},{2,4},{3,5},{4,6},{5,7},{6,8},{7,9},{8,10},{9,11},{10,... | collective-permute-start | bytes 9224 | tf_op jit(solution)/shard_map/ppermute | solution.py:34
  30.0 0.6 broadcast_in_dim.12.sep_bias
  30.6 0.6 broadcast_in_dim.13.head_bias
  31.3 0.6 broadcast_in_dim.14.pair
  31.9 0.6 stack.67.place
  32.5 0.0 collective-permute-done.4.top
  32.5 0.0 collective-permute-done.3.rest_4_
  32.5 0.0 collective-permute-done.2.rest_3_
  32.5 0.0 collective-permute-done.1
  32.5 1.0 copy-done.6
  33.5 0.0 collective-permute-done.rest_6_
  33.5 1.3 collective-permute-start.8
  34.8 0.1 collective-permute-start.9
  34.9 0.5 collective-permute-start.10
  35.4 5.6 %collective-permute-start.7 = (bf16[336,1536]{1,0:T(8,128)(2,1)}, bf16[336,1536]{1,0:T(8,128)(2,1)}, u32[]{:S(2)}, u32[]{:S(2)}) collective-permute-start(bf16[336,1536]{1,0:T(8,128)(2,1)} %collective-permute-done.rest_6_), channel_id=1, source_target_pairs={{0,4},{1,5},{2,6},{3,7},{4,0},{5,1},{6,2},{7,3},{8,12},{9,13},{10,... | collective-permute-start | bytes 3096584 | tf_op jit(solution)/shard_map/ppermute | solution.py:34
  41.0 0.7 collective-permute-start.6
  41.8 6.8 %conv.1 = (bf16[512,1536]{1,0:T(8,128)(2,1)}, bf16[256,1536]{1,0:T(8,128)(2,1)}, bf16[256,1536]{1,0:T(8,128)(2,1)}) custom-call(bf16[256,1536]{1,0:T(8,128)(2,1)} %bitcast.25, bf16[512,1536]{1,0:T(8,128)(2,1)} %bitcast.26, bf16[1,1536]{1,0:T(2,128)(2,1)} %copy-done.18, bf16[1,1536]{1,0:T(2,128)(2,1)} %copy-done.17, f32[3,1536]{1,0:T(4,128)} %taps.1), custom_call_target="tpu_custom_call" | custom-call | flops 805306368 | bytes 4718592 | tf_op jit(solution)/shard_map/conv/pallas_call | solution.py:69
  48.6 11.7 %collective-permute-done.8 = bf16[336,1536]{1,0:T(8,128)(2,1)S(1)} collective-permute-done((bf16[336,1536]{1,0:T(8,128)(2,1)S(1)}, bf16[336,1536]{1,0:T(8,128)(2,1)S(1)}, u32[]{:S(2)}, u32[]{:S(2)}) %collective-permute-start.8) | collective-permute-done | bytes 1032224 | tf_op jit(solution)/shard_map/ppermute | solution.py:34
  60.3 4.1 %collective-permute-done.7.rest_7_ = bf16[336,1536]{1,0:T(8,128)(2,1)} collective-permute-done((bf16[336,1536]{1,0:T(8,128)(2,1)}, bf16[336,1536]{1,0:T(8,128)(2,1)}, u32[]{:S(2)}, u32[]{:S(2)}) %collective-permute-start.7) | collective-permute-done | bytes 1032224 | tf_op jit(solution)/shard_map/ppermute | solution.py:34
  64.4 0.1 broadcast_select_fusion.1.rest_10_
  64.5 0.1 collective-permute-start.15
  64.6 1.8 collective-permute-start.12
  66.4 1.3 collective-permute-start.13
  67.7 0.2 collective-permute-start.14
  67.9 3.3 %collective-permute-start.11 = (bf16[256,1536]{1,0:T(8,128)(2,1)S(1)}, bf16[256,1536]{1,0:T(8,128)(2,1)S(1)}, u32[]{:S(2)}, u32[]{:S(2)}) collective-permute-start(bf16[256,1536]{1,0:T(8,128)(2,1)S(1)} %copy-done.15), channel_id=1, source_target_pairs={{0,31},{1,30},{2,29},{3,28},{4,27},{5,26},{6,25},{7,24},{8,23},{9,... | collective-permute-start | bytes 2359304 | tf_op jit(solution)/shard_map/ppermute | solution.py:34
  71.2 19.9 %collective-permute-done.11.rest_0_ = bf16[256,1536]{1,0:T(8,128)(2,1)S(1)} collective-permute-done((bf16[256,1536]{1,0:T(8,128)(2,1)S(1)}, bf16[256,1536]{1,0:T(8,128)(2,1)S(1)}, u32[]{:S(2)}, u32[]{:S(2)}) %collective-permute-start.11) | collective-permute-done | bytes 786464 | tf_op jit(solution)/shard_map/ppermute | solution.py:34
  91.1 15.6 %collective-permute-done.12.rest_11_ = bf16[336,1536]{1,0:T(8,128)(2,1)S(1)} collective-permute-done((bf16[336,1536]{1,0:T(8,128)(2,1)S(1)}, bf16[336,1536]{1,0:T(8,128)(2,1)S(1)}, u32[]{:S(2)}, u32[]{:S(2)}) %collective-permute-start.12) | collective-permute-done | bytes 1032224 | tf_op jit(solution)/shard_map/ppermute | solution.py:34
  106.7 5.5 %collective-permute-done.13 = bf16[336,1536]{1,0:T(8,128)(2,1)S(1)} collective-permute-done((bf16[336,1536]{1,0:T(8,128)(2,1)S(1)}, bf16[336,1536]{1,0:T(8,128)(2,1)S(1)}, u32[]{:S(2)}, u32[]{:S(2)}) %collective-permute-start.13) | collective-permute-done | bytes 1032224 | tf_op jit(solution)/shard_map/ppermute | solution.py:34
  112.2 0.1 broadcast_select_fusion.rest_14_
  112.3 0.1 collective-permute-start.19
  112.4 1.8 collective-permute-start.17
  114.2 0.2 collective-permute-start.18
  114.4 2.5 %collective-permute-start.16 = (bf16[256,1536]{1,0:T(8,128)(2,1)S(1)}, bf16[256,1536]{1,0:T(8,128)(2,1)S(1)}, u32[]{:S(2)}, u32[]{:S(2)}) collective-permute-start(bf16[256,1536]{1,0:T(8,128)(2,1)S(1)} %copy-done.13), channel_id=1, source_target_pairs={{0,31},{1,30},{2,29},{3,28},{4,27},{5,26},{6,25},{7,24},{8,23},{9,... | collective-permute-start | bytes 2359304 | tf_op jit(solution)/shard_map/ppermute | solution.py:34
  116.9 20.6 %collective-permute-done.16.rest_1_ = bf16[256,1536]{1,0:T(8,128)(2,1)S(1)} collective-permute-done((bf16[256,1536]{1,0:T(8,128)(2,1)S(1)}, bf16[256,1536]{1,0:T(8,128)(2,1)S(1)}, u32[]{:S(2)}, u32[]{:S(2)}) %collective-permute-start.16) | collective-permute-done | bytes 786464 | tf_op jit(solution)/shard_map/ppermute | solution.py:34
  137.5 17.0 %collective-permute-done.17.rest_15_ = bf16[336,1536]{1,0:T(8,128)(2,1)S(1)} collective-permute-done((bf16[336,1536]{1,0:T(8,128)(2,1)S(1)}, bf16[336,1536]{1,0:T(8,128)(2,1)S(1)}, u32[]{:S(2)}, u32[]{:S(2)}) %collective-permute-start.17) | collective-permute-done | bytes 1032224 | tf_op jit(solution)/shard_map/ppermute | solution.py:34
  154.5 0.0 collective-permute-done.18.rest_13_
  154.5 1.0 copy-done.12
  155.5 0.0 collective-permute-start.20
  155.5 2.8 %collective-permute-done.20.rest_17_ = bf16[336,1536]{1,0:T(8,128)(2,1)} collective-permute-done((bf16[336,1536]{1,0:T(8,128)(2,1)S(1)}, bf16[336,1536]{1,0:T(8,128)(2,1)}, u32[]{:S(2)}, u32[]{:S(2)}) %collective-permute-start.20) | collective-permute-done | bytes 1032224 | tf_op jit(solution)/shard_map/ppermute | solution.py:34
  158.3 47.3 %finish.1 = bf16[512,3840]{1,0:T(8,128)(2,1)} custom-call(s32[16]{0:T(128)} %stack.67.place, f32[1,1536]{1,0:T(1,128)} %broadcast_in_dim.12.sep_bias, f32[1,3840]{1,0:T(1,128)} %broadcast_in_dim.13.head_bias, s32[1,3840]{1,0:T(1,128)} %broadcast_in_dim.14.pair, bf16[512,1536]{1,0:T(8,128)(2,1)} %get-tuple-element.48.own_values, ...), custom_call_target="tpu_custom_call" | custom-call | flops 60397977600 | bytes 31457280 | tf_op jit(solution)/shard_map/finish/pallas_call | solution.py:194
  (42 shorter events, 0.1 us)
Async XLA Ops:
  0.0 30.0 %copy-start.5 = (f32[1536]{0:T(1024)S(1)}, f32[1536]{0:T(1024)}, u32[]{:S(2)}) copy-start(f32[1536]{0:T(1024)} %param.12) | copy-start | bytes 18436
  0.0 30.6 %copy-start.3 = (f32[3840]{0:T(1024)S(1)}, f32[3840]{0:T(1024)}, u32[]{:S(2)}) copy-start(f32[3840]{0:T(1024)} %param.14) | copy-start | bytes 46084
  0.0 31.3 %copy-start.4 = (s32[3840]{0:T(1024)S(1)}, s32[3840]{0:T(1024)}, u32[]{:S(2)}) copy-start(s32[3840]{0:T(1024)} %param.15) | copy-start | bytes 46084
  1.3 34.1 %copy-start.2 = (bf16[336,1536]{1,0:T(8,128)(2,1)}, bf16[336,1536]{1,0:T(8,128)(2,1)S(1)}, u32[]{:S(2)}) copy-start(bf16[336,1536]{1,0:T(8,128)(2,1)S(1)} %pad_maximum_fusion.rest_2_) | copy-start | bytes 3096580
  1.3 31.2 %collective-permute-start.3 = (bf16[336,1536]{1,0:T(8,128)(2,1)S(1)}, bf16[336,1536]{1,0:T(8,128)(2,1)S(1)}, u32[]{:S(2)}, u32[]{:S(2)}) collective-permute-start(bf16[336,1536]{1,0:T(8,128)(2,1)S(1)} %pad_maximum_fusion.rest_2_), channel_id=1, source_target_pairs={{0,2},{1,3},{2,0},{3,1},{4,6},{5,7},{6,4},{7,5},{8,10},{9,11},{10,... | collective-permute-start | bytes 3096584 | tf_op jit(solution)/shard_map/ppermute | solution.py:34
  1.8 30.7 %collective-permute-start.2 = (bf16[336,1536]{1,0:T(8,128)(2,1)S(1)}, bf16[336,1536]{1,0:T(8,128)(2,1)}, u32[]{:S(2)}, u32[]{:S(2)}) collective-permute-start(bf16[336,1536]{1,0:T(8,128)(2,1)S(1)} %pad_maximum_fusion.rest_2_), channel_id=1, source_target_pairs={{0,4},{1,5},{2,6},{3,7},{4,0},{5,1},{6,2},{7,3},{8,12},{9,13},{10,... | collective-permute-start | bytes 3096584 | tf_op jit(solution)/shard_map/ppermute | solution.py:34
  4.4 28.1 %collective-permute-start.1 = (bf16[336,1536]{1,0:T(8,128)(2,1)S(1)}, bf16[336,1536]{1,0:T(8,128)(2,1)S(1)}, u32[]{:S(2)}, u32[]{:S(2)}) collective-permute-start(bf16[336,1536]{1,0:T(8,128)(2,1)S(1)} %pad_maximum_fusion.rest_2_), channel_id=1, source_target_pairs={{8,16},{9,17},{10,18},{11,19},{12,20},{13,21},{14,22},{15,23},{16,... | collective-permute-start | bytes 3096584 | tf_op jit(solution)/shard_map/ppermute | solution.py:34
  5.1 28.4 %collective-permute-start = (bf16[336,1536]{1,0:T(8,128)(2,1)S(1)}, bf16[336,1536]{1,0:T(8,128)(2,1)}, u32[]{:S(2)}, u32[]{:S(2)}) collective-permute-start(bf16[336,1536]{1,0:T(8,128)(2,1)S(1)} %pad_maximum_fusion.rest_2_), channel_id=1, source_target_pairs={{0,8},{1,9},{2,10},{3,11},{4,12},{5,13},{6,14},{7,15},{8,0},{9,1},... | collective-permute-start | bytes 3096584 | tf_op jit(solution)/shard_map/ppermute | solution.py:34
  10.4 3.1 %collective-permute-start.5 = (bf16[1,1536]{1,0:T(2,128)(2,1)S(1)}, bf16[1,1536]{1,0:T(2,128)(2,1)S(1)}, u32[]{:S(2)}, u32[]{:S(2)}) collective-permute-start(bf16[1,1536]{1,0:T(2,128)(2,1)S(1)} %get-tuple-element.67), channel_id=1, source_target_pairs={{2,0},{3,1},{4,2},{5,3},{6,4},{7,5},{8,6},{9,7},{10,8},{11,9},{12,... | collective-permute-start | bytes 9224 | tf_op jit(solution)/shard_map/ppermute | solution.py:34
  13.4 28.3 %copy-start.17 = (bf16[1,1536]{1,0:T(2,128)(2,1)}, bf16[1,1536]{1,0:T(2,128)(2,1)S(1)}, u32[]{:S(2)}) copy-start(bf16[1,1536]{1,0:T(2,128)(2,1)S(1)} %collective-permute-done.5.bottom) | copy-start | bytes 9220
  13.4 19.1 %collective-permute-start.4 = (bf16[1,1536]{1,0:T(2,128)(2,1)S(1)}, bf16[1,1536]{1,0:T(2,128)(2,1)S(1)}, u32[]{:S(2)}, u32[]{:S(2)}) collective-permute-start(bf16[1,1536]{1,0:T(2,128)(2,1)S(1)} %get-tuple-element.68), channel_id=1, source_target_pairs={{0,2},{1,3},{2,4},{3,5},{4,6},{5,7},{6,8},{7,9},{8,10},{9,11},{10,... | collective-permute-start | bytes 9224 | tf_op jit(solution)/shard_map/ppermute | solution.py:34
  32.5 9.3 %copy-start.18 = (bf16[1,1536]{1,0:T(2,128)(2,1)}, bf16[1,1536]{1,0:T(2,128)(2,1)S(1)}, u32[]{:S(2)}) copy-start(bf16[1,1536]{1,0:T(2,128)(2,1)S(1)} %collective-permute-done.4.top) | copy-start | bytes 9220
  32.5 1.0 copy-start.6
  33.5 26.8 %collective-permute-start.8 = (bf16[336,1536]{1,0:T(8,128)(2,1)S(1)}, bf16[336,1536]{1,0:T(8,128)(2,1)S(1)}, u32[]{:S(2)}, u32[]{:S(2)}) collective-permute-start(bf16[336,1536]{1,0:T(8,128)(2,1)S(1)} %collective-permute-done.1), channel_id=1, source_target_pairs={{8,0},{9,1},{10,2},{11,3},{12,4},{13,5},{14,6},{15,7},{16,24},{17,... | collective-permute-start | bytes 3096584 | tf_op jit(solution)/shard_map/ppermute | solution.py:34
  34.8 25.5 %collective-permute-start.9 = (bf16[336,1536]{1,0:T(8,128)(2,1)}, bf16[336,1536]{1,0:T(8,128)(2,1)}, u32[]{:S(2)}, u32[]{:S(2)}) collective-permute-start(bf16[336,1536]{1,0:T(8,128)(2,1)} %collective-permute-done.2.rest_3_), channel_id=1, source_target_pairs={{0,2},{1,3},{2,0},{3,1},{4,6},{5,7},{6,4},{7,5},{8,10},{9,11},{10,... | collective-permute-start | bytes 3096584 | tf_op jit(solution)/shard_map/ppermute | solution.py:34
  34.9 25.4 %collective-permute-start.10 = (bf16[336,1536]{1,0:T(8,128)(2,1)}, bf16[336,1536]{1,0:T(8,128)(2,1)}, u32[]{:S(2)}, u32[]{:S(2)}) collective-permute-start(bf16[336,1536]{1,0:T(8,128)(2,1)} %collective-permute-done.rest_6_), channel_id=1, source_target_pairs={{0,2},{1,3},{2,0},{3,1},{4,6},{5,7},{6,4},{7,5},{8,10},{9,11},{10,... | collective-permute-start | bytes 3096584 | tf_op jit(solution)/shard_map/ppermute | solution.py:34
  35.4 29.0 %collective-permute-start.7 = (bf16[336,1536]{1,0:T(8,128)(2,1)}, bf16[336,1536]{1,0:T(8,128)(2,1)}, u32[]{:S(2)}, u32[]{:S(2)}) collective-permute-start(bf16[336,1536]{1,0:T(8,128)(2,1)} %collective-permute-done.rest_6_), channel_id=1, source_target_pairs={{0,4},{1,5},{2,6},{3,7},{4,0},{5,1},{6,2},{7,3},{8,12},{9,13},{10,... | collective-permute-start | bytes 3096584 | tf_op jit(solution)/shard_map/ppermute | solution.py:34
  41.0 23.4 %collective-permute-start.6 = (bf16[336,1536]{1,0:T(8,128)(2,1)}, bf16[336,1536]{1,0:T(8,128)(2,1)S(1)}, u32[]{:S(2)}, u32[]{:S(2)}) collective-permute-start(bf16[336,1536]{1,0:T(8,128)(2,1)} %collective-permute-done.rest_6_), channel_id=1, source_target_pairs={{8,16},{9,17},{10,18},{11,19},{12,20},{13,21},{14,22},{15,23},{16,... | collective-permute-start | bytes 3096584 | tf_op jit(solution)/shard_map/ppermute | solution.py:34
  48.6 19.3 %copy-start.15 = (bf16[256,1536]{1,0:T(8,128)(2,1)S(1)}, bf16[256,1536]{1,0:T(8,128)(2,1)}, u32[]{:S(2)}) copy-start(bf16[256,1536]{1,0:T(8,128)(2,1)} %get-tuple-element.49) | copy-start | bytes 2359300
  64.5 93.8 %copy-start = (bf16[336,1536]{1,0:T(8,128)(2,1)}, bf16[336,1536]{1,0:T(8,128)(2,1)S(1)}, u32[]{:S(2)}) copy-start(bf16[336,1536]{1,0:T(8,128)(2,1)S(1)} %broadcast_select_fusion.1.rest_10_) | copy-start | bytes 3096580
  64.5 49.8 %copy-start.13 = (bf16[256,1536]{1,0:T(8,128)(2,1)S(1)}, bf16[256,1536]{1,0:T(8,128)(2,1)}, u32[]{:S(2)}) copy-start(bf16[256,1536]{1,0:T(8,128)(2,1)} %get-tuple-element.55) | copy-start | bytes 2359300
  64.5 26.6 %collective-permute-start.15 = (bf16[336,1536]{1,0:T(8,128)(2,1)S(1)}, bf16[336,1536]{1,0:T(8,128)(2,1)S(1)}, u32[]{:S(2)}, u32[]{:S(2)}) collective-permute-start(bf16[336,1536]{1,0:T(8,128)(2,1)S(1)} %broadcast_select_fusion.1.rest_10_), channel_id=1, source_target_pairs={{0,2},{1,3},{2,0},{3,1},{4,6},{5,7},{6,4},{7,5},{8,10},{9,11},{10,... | collective-permute-start | bytes 3096584 | tf_op jit(solution)/shard_map/ppermute | solution.py:34
  64.6 42.1 %collective-permute-start.12 = (bf16[336,1536]{1,0:T(8,128)(2,1)S(1)}, bf16[336,1536]{1,0:T(8,128)(2,1)S(1)}, u32[]{:S(2)}, u32[]{:S(2)}) collective-permute-start(bf16[336,1536]{1,0:T(8,128)(2,1)S(1)} %broadcast_select_fusion.1.rest_10_), channel_id=1, source_target_pairs={{0,4},{1,5},{2,6},{3,7},{4,0},{5,1},{6,2},{7,3},{8,12},{9,13},{10,... | collective-permute-start | bytes 3096584 | tf_op jit(solution)/shard_map/ppermute | solution.py:34
  66.4 45.8 %collective-permute-start.13 = (bf16[336,1536]{1,0:T(8,128)(2,1)S(1)}, bf16[336,1536]{1,0:T(8,128)(2,1)S(1)}, u32[]{:S(2)}, u32[]{:S(2)}) collective-permute-start(bf16[336,1536]{1,0:T(8,128)(2,1)S(1)} %collective-permute-done.6), channel_id=1, source_target_pairs={{8,0},{9,1},{10,2},{11,3},{12,4},{13,5},{14,6},{15,7},{16,24},{17,... | collective-permute-start | bytes 3096584 | tf_op jit(solution)/shard_map/ppermute | solution.py:34
  67.7 44.5 %collective-permute-start.14 = (bf16[336,1536]{1,0:T(8,128)(2,1)}, bf16[336,1536]{1,0:T(8,128)(2,1)S(1)}, u32[]{:S(2)}, u32[]{:S(2)}) collective-permute-start(bf16[336,1536]{1,0:T(8,128)(2,1)} %collective-permute-done.7.rest_7_), channel_id=1, source_target_pairs={{0,2},{1,3},{2,0},{3,1},{4,6},{5,7},{6,4},{7,5},{8,10},{9,11},{10,... | collective-permute-start | bytes 3096584 | tf_op jit(solution)/shard_map/ppermute | solution.py:34
  67.9 23.2 %collective-permute-start.11 = (bf16[256,1536]{1,0:T(8,128)(2,1)S(1)}, bf16[256,1536]{1,0:T(8,128)(2,1)S(1)}, u32[]{:S(2)}, u32[]{:S(2)}) collective-permute-start(bf16[256,1536]{1,0:T(8,128)(2,1)S(1)} %copy-done.15), channel_id=1, source_target_pairs={{0,31},{1,30},{2,29},{3,28},{4,27},{5,26},{6,25},{7,24},{8,23},{9,... | collective-permute-start | bytes 2359304 | tf_op jit(solution)/shard_map/ppermute | solution.py:34
  91.1 21.1 %copy-start.14 = (bf16[256,1536]{1,0:T(8,128)(2,1)}, bf16[256,1536]{1,0:T(8,128)(2,1)S(1)}, u32[]{:S(2)}) copy-start(bf16[256,1536]{1,0:T(8,128)(2,1)S(1)} %collective-permute-done.11.rest_0_) | copy-start | bytes 2359300
  91.1 67.2 %copy-start.7 = (bf16[336,1536]{1,0:T(8,128)(2,1)}, bf16[336,1536]{1,0:T(8,128)(2,1)S(1)}, u32[]{:S(2)}) copy-start(bf16[336,1536]{1,0:T(8,128)(2,1)S(1)} %collective-permute-done.15.rest_12_) | copy-start | bytes 3096580
  106.7 51.6 %copy-start.8 = (bf16[336,1536]{1,0:T(8,128)(2,1)}, bf16[336,1536]{1,0:T(8,128)(2,1)S(1)}, u32[]{:S(2)}) copy-start(bf16[336,1536]{1,0:T(8,128)(2,1)S(1)} %collective-permute-done.12.rest_11_) | copy-start | bytes 3096580
  112.2 46.1 %copy-start.9 = (bf16[336,1536]{1,0:T(8,128)(2,1)}, bf16[336,1536]{1,0:T(8,128)(2,1)S(1)}, u32[]{:S(2)}) copy-start(bf16[336,1536]{1,0:T(8,128)(2,1)S(1)} %collective-permute-done.14.rest_9_) | copy-start | bytes 3096580
  112.3 46.0 %copy-start.1 = (bf16[336,1536]{1,0:T(8,128)(2,1)}, bf16[336,1536]{1,0:T(8,128)(2,1)S(1)}, u32[]{:S(2)}) copy-start(bf16[336,1536]{1,0:T(8,128)(2,1)S(1)} %broadcast_select_fusion.rest_14_) | copy-start | bytes 3096580
  112.3 25.2 %collective-permute-start.19 = (bf16[336,1536]{1,0:T(8,128)(2,1)S(1)}, bf16[336,1536]{1,0:T(8,128)(2,1)S(1)}, u32[]{:S(2)}, u32[]{:S(2)}) collective-permute-start(bf16[336,1536]{1,0:T(8,128)(2,1)S(1)} %broadcast_select_fusion.rest_14_), channel_id=1, source_target_pairs={{0,2},{1,3},{2,0},{3,1},{4,6},{5,7},{6,4},{7,5},{8,10},{9,11},{10,... | collective-permute-start | bytes 3096584 | tf_op jit(solution)/shard_map/ppermute | solution.py:34
  112.4 42.1 %collective-permute-start.17 = (bf16[336,1536]{1,0:T(8,128)(2,1)S(1)}, bf16[336,1536]{1,0:T(8,128)(2,1)S(1)}, u32[]{:S(2)}, u32[]{:S(2)}) collective-permute-start(bf16[336,1536]{1,0:T(8,128)(2,1)S(1)} %broadcast_select_fusion.rest_14_), channel_id=1, source_target_pairs={{0,4},{1,5},{2,6},{3,7},{4,0},{5,1},{6,2},{7,3},{8,12},{9,13},{10,... | collective-permute-start | bytes 3096584 | tf_op jit(solution)/shard_map/ppermute | solution.py:34
  114.2 40.3 %collective-permute-start.18 = (bf16[336,1536]{1,0:T(8,128)(2,1)S(1)}, bf16[336,1536]{1,0:T(8,128)(2,1)S(1)}, u32[]{:S(2)}, u32[]{:S(2)}) collective-permute-start(bf16[336,1536]{1,0:T(8,128)(2,1)S(1)} %collective-permute-done.12.rest_11_), channel_id=1, source_target_pairs={{0,2},{1,3},{2,0},{3,1},{4,6},{5,7},{6,4},{7,5},{8,10},{9,11},{10,... | collective-permute-start | bytes 3096584 | tf_op jit(solution)/shard_map/ppermute | solution.py:34
  114.4 23.1 %collective-permute-start.16 = (bf16[256,1536]{1,0:T(8,128)(2,1)S(1)}, bf16[256,1536]{1,0:T(8,128)(2,1)S(1)}, u32[]{:S(2)}, u32[]{:S(2)}) collective-permute-start(bf16[256,1536]{1,0:T(8,128)(2,1)S(1)} %copy-done.13), channel_id=1, source_target_pairs={{0,31},{1,30},{2,29},{3,28},{4,27},{5,26},{6,25},{7,24},{8,23},{9,... | collective-permute-start | bytes 2359304 | tf_op jit(solution)/shard_map/ppermute | solution.py:34
  137.5 18.0 %copy-start.16 = (bf16[256,1536]{1,0:T(8,128)(2,1)}, bf16[256,1536]{1,0:T(8,128)(2,1)S(1)}, u32[]{:S(2)}) copy-start(bf16[256,1536]{1,0:T(8,128)(2,1)S(1)} %collective-permute-done.16.rest_1_) | copy-start | bytes 2359300
  137.5 20.8 %copy-start.10 = (bf16[336,1536]{1,0:T(8,128)(2,1)}, bf16[336,1536]{1,0:T(8,128)(2,1)S(1)}, u32[]{:S(2)}) copy-start(bf16[336,1536]{1,0:T(8,128)(2,1)S(1)} %collective-permute-done.19.rest_16_) | copy-start | bytes 3096580
  154.5 3.8 %copy-start.11 = (bf16[336,1536]{1,0:T(8,128)(2,1)}, bf16[336,1536]{1,0:T(8,128)(2,1)S(1)}, u32[]{:S(2)}) copy-start(bf16[336,1536]{1,0:T(8,128)(2,1)S(1)} %collective-permute-done.17.rest_15_) | copy-start | bytes 3096580
  154.5 1.0 copy-start.12
  155.5 2.8 %collective-permute-start.20 = (bf16[336,1536]{1,0:T(8,128)(2,1)S(1)}, bf16[336,1536]{1,0:T(8,128)(2,1)}, u32[]{:S(2)}, u32[]{:S(2)}) collective-permute-start(bf16[336,1536]{1,0:T(8,128)(2,1)S(1)} %collective-permute-done.17.rest_15_), channel_id=1, source_target_pairs={{0,2},{1,3},{2,0},{3,1},{4,6},{5,7},{6,4},{7,5},{8,10},{9,11},{10,... | collective-permute-start | bytes 3096584 | tf_op jit(solution)/shard_map/ppermute | solution.py:34

commit v4 on v3

--- a/solution.py
+++ b/solution.py
@@ -93,39 +93,42 @@
     )
 
 
+def copies_of(blocks, place, pieces, weight, sems, first):
+    copies = []
+    for i, (piece, start, rows, slot) in enumerate(blocks):
+        target = pl.multiple_of(place[slot] * rows, rows)
+        copies.append(
+            pltpu.make_async_copy(
+                pieces[piece].at[pl.ds(start, rows), :],
+                weight.at[pl.ds(target, rows), :],
+                sems.at[first + i],
+            )
+        )
+    return copies
+
+
 def columns_of(j, step):
     return pl.ds(pl.multiple_of(j * step, step), step)
 
 
-def finish_kernel(place, sep_bias, head_bias, pair, own_values, *rest):
-    shards = place.shape[0]
-    parts = len(rest) - shards - 10
-    others, pieces = rest[:parts], rest[parts : parts + shards]
-    out, sep, head, inputs, values, own, other, chosen, result, sems = rest[parts + shards :]
-    bins, tracks = own.shape
-    width = values.shape[1]
-    depth = width // shards
-    share = tracks // shards
-    copies = []
-
-    def fetch(source, target):
-        copy = pltpu.make_async_copy(source, target, sems.at[len(copies)])
+def early_kernel(sep_blocks, near_blocks, place, sep_bias, head_bias, own_values, first, *rest):
+    *pieces, values, heads, sep, near, inputs, sems = rest
+    bins, part = own_values.shape[0], first.shape[0]
+    width, half_tracks = values.shape[1], heads.shape[1]
+    which = place[place.shape[0] - 1]
+    near_start = pl.multiple_of(which * half_tracks, 128)
+    copies = copies_of(sep_blocks, place, pieces, sep, sems, 0)
+    near_copies = copies_of(near_blocks, place, pieces, near, sems, len(sep_blocks))
+    base = len(sep_blocks) + len(near_blocks)
+    copies.append(
+        pltpu.make_async_copy(own_values, inputs.at[pl.ds(0, bins), :], sems.at[base])
+    )
+    copies.append(
+        pltpu.make_async_copy(first, inputs.at[pl.ds(bins, part), :], sems.at[base + 1])
+    )
+    for copy in copies + near_copies:
         copy.start()
-        copies.append(copy)
-
-    fetch(own_values, inputs.at[pl.ds(0, bins), :])
-    start = bins
-    for part in others:
-        fetch(part, inputs.at[pl.ds(start, part.shape[0]), :])
-        start += part.shape[0]
-    for i, piece in enumerate(pieces):
-        target = pl.multiple_of(place[i] * depth, depth)
-        fetch(piece.at[pl.ds(0, depth), :], sep.at[pl.ds(target, depth), :])
-    first = len(copies)
-    for i, piece in enumerate(pieces):
-        target = pl.multiple_of(place[i] * share, share)
-        fetch(piece.at[pl.ds(depth, share), :], head.at[pl.ds(target, share), :])
-    for copy in copies[:first]:
+    for copy in copies:
         copy.wait()
 
     @pl.loop(0, width // 256)
@@ -134,19 +137,116 @@
         product = jnp.dot(inputs[...], sep[:, columns], preferred_element_type=jnp.float32)
         values[:, columns] = gelu(product + sep_bias[:, columns]).astype(jnp.bfloat16)
 
-    for copy in copies[first:]:
+    for copy in near_copies:
         copy.wait()
-    step = 256
-
-    @pl.loop(0, tracks // step)
+    step = 384
+
+    @pl.loop(0, half_tracks // step)
     def _(j):
         columns = columns_of(j, step)
-        product = rows_by_rows(values[...], head[columns, :])
-        heads = softplus(product + head_bias[:, columns]).astype(jnp.bfloat16)
-        own[:, columns] = heads[:bins]
-        other[:, columns] = heads[bins:]
-
-    used = len(copies)
+        source = pl.ds(pl.multiple_of(near_start + j * step, 128), step)
+        product = rows_by_rows(values[...], near[columns, :])
+        heads[:, columns] = softplus(product + head_bias[:, source]).astype(jnp.bfloat16)
+
+
+def early(place, sep_bias, head_bias, own_values, first, pieces, sep_blocks, near_blocks):
+    rows, width = own_values.shape[0] + first.shape[0], own_values.shape[1]
+    half_tracks = head_bias.shape[1] // 2
+    vmem = pl.BlockSpec(memory_space=pltpu.VMEM)
+    shapes = [(rows, width), (rows, half_tracks)]
+    return pl.pallas_call(
+        functools.partial(early_kernel, sep_blocks, near_blocks),
+        in_specs=[pl.BlockSpec(memory_space=pltpu.SMEM)]
+        + [vmem] * 2
+        + [pl.BlockSpec(memory_space=pl.ANY)] * (2 + len(pieces)),
+        out_specs=[vmem] * 2,
+        out_shape=[jax.ShapeDtypeStruct(shape, jnp.bfloat16) for shape in shapes],
+        scratch_shapes=[
+            pltpu.VMEM((width, width), jnp.bfloat16),
+            pltpu.VMEM((half_tracks, width), jnp.bfloat16),
+            pltpu.VMEM((rows, width), jnp.bfloat16),
+            pltpu.SemaphoreType.DMA((2 + len(sep_blocks) + len(near_blocks),)),
+        ],
+        compiler_params=params(),
+        cost_estimate=cost(2 * rows * width * (width + half_tracks), 4 * width * width),
+        name="early",
+    )(place, sep_bias, head_bias, own_values, first, *pieces)
+
+
+def finish_kernel(sep_blocks, near_blocks, far_blocks, place, sep_bias, head_bias, pair, *rest):
+    early_values, later, near_heads, *pieces = rest[:-11]
+    out, sep, near, far, last_values, values, own, other, chosen, result, sems = rest[-11:]
+    bins, tracks = own.shape
+    part = early_values.shape[0] - bins
+    width = values.shape[1]
+    half_tracks = tracks // 2
+    which = place[place.shape[0] - 1]
+    near_start = pl.multiple_of(which * half_tracks, 128)
+    far_start = pl.multiple_of((1 - which) * half_tracks, 128)
+    near_columns = pl.ds(near_start, half_tracks)
+    near_first = len(sep_blocks)
+    far_first = near_first + len(near_blocks)
+    base = far_first + len(far_blocks)
+
+    def fetch(source, target, number):
+        copy = pltpu.make_async_copy(source, target, sems.at[base + number])
+        copy.start()
+        return copy
+
+    later_copy = fetch(later, last_values, 0)
+    sep_copies = copies_of(sep_blocks, place, pieces, sep, sems, 0)
+    near_copies = copies_of(near_blocks, place, pieces, near, sems, near_first)
+    far_copies = copies_of(far_blocks, place, pieces, far, sems, far_first)
+    for copy in sep_copies + near_copies:
+        copy.start()
+    values_copy = fetch(early_values, values.at[pl.ds(0, bins + part), :], 1)
+    for copy in far_copies:
+        copy.start()
+    own_near_copy = fetch(near_heads.at[pl.ds(0, bins), :], own.at[:, near_columns], 2)
+    first_near_copy = fetch(
+        near_heads.at[pl.ds(bins, part), :], other.at[pl.ds(0, part), near_columns], 3
+    )
+    later_copy.wait()
+    for copy in sep_copies:
+        copy.wait()
+
+    @pl.loop(0, width // 256)
+    def _(j):
+        columns = columns_of(j, 256)
+        product = jnp.dot(
+            last_values[...], sep[:, columns], preferred_element_type=jnp.float32
+        )
+        values[bins + part :, columns] = gelu(product + sep_bias[:, columns]).astype(
+            jnp.bfloat16
+        )
+
+    step = 384
+    for copy in near_copies:
+        copy.wait()
+
+    @pl.loop(0, half_tracks // step)
+    def _(j):
+        columns = columns_of(j, step)
+        target = pl.ds(pl.multiple_of(near_start + j * step, 128), step)
+        product = rows_by_rows(values[bins + part :, :], near[columns, :])
+        other[part:, target] = softplus(product + head_bias[:, target]).astype(jnp.bfloat16)
+
+    values_copy.wait()
+    for copy in far_copies:
+        copy.wait()
+
+    @pl.loop(0, half_tracks // step)
+    def _(j):
+        columns = columns_of(j, step)
+        target = pl.ds(pl.multiple_of(far_start + j * step, 128), step)
+        product = rows_by_rows(values[...], far[columns, :])
+        heads = softplus(product + head_bias[:, target]).astype(jnp.bfloat16)
+        own[:, target] = heads[:bins]
+        other[:, target] = heads[bins:]
+
+    own_near_copy.wait()
+    first_near_copy.wait()
+    step = 256
 
     def choose(j, slot):
         rows = lax.broadcasted_iota(jnp.int32, (tracks, step), 0)
@@ -156,7 +256,7 @@
     def result_copy(j):
         columns = columns_of(j, step)
         return pltpu.make_async_copy(
-            result.at[:, columns], out.at[:, columns], sems.at[used + j]
+            result.at[:, columns], out.at[:, columns], sems.at[base + 4 + j]
         )
 
     def combine(j, slot):
@@ -184,24 +284,26 @@
         result_copy(j).wait()
 
 
-def finish(place, sep_bias, head_bias, pair, own_values, others, pieces):
-    bins, width = own_values.shape
+def finish(place, sep_bias, head_bias, pair, arrays, pieces, sep_blocks, near_blocks, far_blocks):
+    last, width = arrays[1].shape
+    bins = (arrays[0].shape[0] + last) // 2
     tracks = head_bias.shape[1]
     vmem = pl.BlockSpec(memory_space=pltpu.VMEM)
     anywhere = pl.BlockSpec(memory_space=pl.ANY)
     bf16 = lambda *shape: pltpu.VMEM(shape, jnp.bfloat16)
-    count = 1 + len(others) + 2 * len(pieces) + tracks // 256
+    count = len(sep_blocks) + len(near_blocks) + len(far_blocks) + 4 + tracks // 256
     return pl.pallas_call(
-        finish_kernel,
+        functools.partial(finish_kernel, sep_blocks, near_blocks, far_blocks),
         in_specs=[pl.BlockSpec(memory_space=pltpu.SMEM)]
         + [vmem] * 3
-        + [anywhere] * (1 + len(others) + len(pieces)),
+        + [anywhere] * (len(arrays) + len(pieces)),
         out_specs=anywhere,
         out_shape=jax.ShapeDtypeStruct((bins, tracks), jnp.bfloat16),
         scratch_shapes=[
             bf16(width, width),
-            bf16(tracks, width),
-            bf16(2 * bins, width),
+            bf16(tracks // 2, width),
+            bf16(tracks // 2, width),
+            bf16(last, width),
             bf16(2 * bins, width),
             bf16(bins, tracks),
             bf16(bins, tracks),
@@ -212,7 +314,7 @@
         compiler_params=params(),
         cost_estimate=cost(8 * bins * tracks * tracks, 16 * bins * tracks),
         name="finish",
-    )(place, sep_bias, head_bias, pair, own_values, *others, *pieces)
+    )(place, sep_bias, head_bias, pair, *arrays, *pieces)
 
 
 def along_line(s, b):
@@ -233,18 +335,23 @@
 
 def across_cores(s, b):
     return s ^ 1, b
+
+
+def blocks_of(rows, starts, first):
+    return [(i, start, rows, first + i) for i, start in enumerate(starts)]
 
 
 def places():
     s = lax.axis_index("seq")
     z, y, c = s // 4, (s // 2) % 2, s % 2
     inner = jnp.where(z < 2, 2, 1)
-    result = []
+    within, among = [], []
     for zz in (z, z ^ 1, inner, inner ^ 1):
         for core in (c, 1 - c):
             for yy in (y, 1 - y):
-                result.append(zz * 4 + yy * 2 + core)
-    return jnp.stack(result).astype(jnp.int32)
+                within.append((zz % 2) * 4 + yy * 2 + core)
+                among.append(zz * 4 + yy * 2 + core)
+    return jnp.stack(within + among + [s // 8]).astype(jnp.int32)
 
 
 def edge(coarse_row, skip_row):
@@ -274,21 +381,23 @@
     q0 = send(own, across_middle)
     y0 = send(own, across_pair)
     k_own = send(own, across_cores)
-    small = (sep_bias[None], head_bias[None], strand_pair[None], places())
+    small = (sep_bias, head_bias, strand_pair, places())
     edges = (top, bottom)
     near, q0, y0, k_own, edges, small = tied(near, q0, y0, k_own, edges, small)
     sep_bias, head_bias, strand_pair, place = small
 
     top, bottom = edges
-    own_values, *flipped = conv(coarse, skip, top, bottom, depth_kernel, (skip.shape[0] // 2,))
+    own_values, *flipped = conv(coarse, skip, top, bottom, depth_kernel, (5 * skip.shape[0] // 8,))
     q1 = send(near, across_middle)
     y1 = send(near, across_pair)
     s0 = send(q0, to_line_ends)
     k_y0 = send(y0, across_cores)
     k_near = send(near, across_cores)
-    q1, y1, s0, k_y0, k_near, flipped, own_values = tied(
-        q1, y1, s0, k_y0, k_near, flipped, own_values
-    )
+    small = (sep_bias[None], head_bias[None], strand_pair[None], place)
+    q1, y1, s0, k_y0, k_near, flipped, own_values, small = tied(
+        q1, y1, s0, k_y0, k_near, flipped, own_values, small
+    )
+    sep_bias, head_bias, strand_pair, place = small
 
     m0 = send(flipped[0], to_mirror)
     o0 = pick(q0, s0)
@@ -298,17 +407,48 @@
     k_o0 = send(o0, across_cores)
     m0, y2, s1, k_y1, k_o0, flipped = tied(m0, y2, s1, k_y1, k_o0, flipped)
 
-    m1 = send(flipped[1], to_mirror)
-    o1 = pick(q1, s1)
-    y3 = send(o1, across_pair)
+    depth = sep_weight.shape[0]
+    o1_sep, o1_head = pick(q1[:depth], s1[:depth]), pick(q1[depth:], s1[depth:])
+    y3_sep = send(o1_sep, across_pair)
     k_y2 = send(y2, across_cores)
-    k_o1 = send(o1, across_cores)
-    m1, y3, k_y2, k_o1 = tied(m1, y3, k_y2, k_o1)
+    k_o1_sep = send(o1_sep, across_cores)
+    y3_sep, o1_head, last_part = tied(y3_sep, o1_head, flipped[1])
+
+    m1 = send(last_part, to_mirror)
+    y3 = send(o1_head, across_pair)
+    k_y3_sep = send(y3_sep, across_cores)
+    k_o1 = send(o1_head, across_cores)
+    near_pieces = [own, y0, k_own, k_y0, near, y1, k_near, k_y1]
+    far_pieces = [o0, y2, k_o0, k_y2]
+    rows = own.shape[0] - depth
+    near_blocks = blocks_of(rows, [depth] * 8, 0)
+    sep_only = [o1_sep, y3_sep, k_o1_sep, k_y3_sep]
+    sep_blocks = blocks_of(depth, [0] * 16, 16)
+    values, near_heads = early(
+        place,
+        sep_bias,
+        head_bias,
+        own_values,
+        m0,
+        near_pieces + far_pieces + sep_only,
+        sep_blocks,
+        near_blocks,
+    )
+    m1, y3, k_o1, values, near_heads = tied(m1, y3, k_o1, values, near_heads)
 
     k_y3 = send(y3, across_cores)
-    pieces = [own, y0, k_own, k_y0, near, y1, k_near, k_y1]
-    pieces += [o0, y2, k_o0, k_y2, o1, y3, k_o1, k_y3]
-    return finish(place, sep_bias, head_bias, strand_pair, own_values, [m0, m1], pieces)[None]
+    far_blocks = blocks_of(rows, [depth] * 4 + [0] * 4, 8)
+    return finish(
+        place,
+        sep_bias,
+        head_bias,
+        strand_pair,
+        [values, m1, near_heads],
+        near_pieces + far_pieces + sep_only + [o1_head, y3, k_o1, k_y3],
+        sep_blocks,
+        near_blocks,
+        [(i + 8 if i < 4 else i + 12, *block) for i, *block in far_blocks],
+    )[None]
 
 
 def plain_features_kernel(own, other, weight, bias, out):

time: 206 us -> 197 us (0.956)
  waiting for transfers between devices: 98.9 us -> 76.2 us
  Pallas kernels: 54.1 us -> 65 us
  starting transfers between devices: 45.5 us -> 48.4 us
    ppermute x21 -> x24, waiting for transfers between devices: 98.9 us -> 76.2 us  [send(): return lax.ppermute(array, BOTH, route(seq, batch, move))]
    pallas_call x1 -> x2, Pallas kernels: 47.3 us -> 58.2 us  [the longest x1 37.8 us: finish(): pl.pallas_call(functools.partial(finish_kernel, sep_blocks, near_blocks,...]
    ppermute x21 -> x24, starting transfers between devices: 45.5 us -> 48.4 us  [send(): return lax.ppermute(array, BOTH, route(seq, batch, move))]
  transfers between devices with their start and end apart: 21 -> 24, of which waited for: 9 -> 11; matrix products, arithmetic and copies ran while one was open for 2% -> 2% of each run, Pallas kernels for 3% -> 14%
where the time goes in v4:
time: 197 us; the launch traced here: 196 us
  waiting for transfers between devices  76.2 us (39%)
  Pallas kernels  65 us (33%)
  starting transfers between devices  48.4 us (25%)
  local copies, waits for them, and re-layouts  4.03 us (2%)
  other arithmetic  2.32 us (1%)
    ppermute x24, waiting for transfers between devices, send(): return lax.ppermute(array, BOTH, route(seq, batch, move))  76.2 us
    ppermute x24, starting transfers between devices, send(): return lax.ppermute(array, BOTH, route(seq, batch, move))  48.4 us
    pallas_call x1, Pallas kernels, finish(): pl.pallas_call(functools.partial(finish_kernel, sep_blocks, near_blocks,...  37.8 us
    pallas_call x1, Pallas kernels, early(): pl.pallas_call(functools.partial(early_kernel, sep_blocks, near_blocks),...  20.4 us
    pallas_call x1, Pallas kernels, conv(): pl.pallas_call(conv_kernel, grid=(width // step,), in_specs=[column(coars...  6.76 us
  transfers between devices with their start and end apart: 24, of which 11 were waited for; matrix products, arithmetic and copies ran while one was open for 2% of the time, Pallas kernels for 14%

profile of v4, /device:TPU:0, one launch (start us, length us, event | category | flops | bytes accessed | tf_op | source)
XLA Modules:
  0.0 196.3 jit_solution(6423448851511386942)
XLA Ops:
  0.0 1.3 pad_maximum_fusion.rest_0_.rest_3_
  1.3 0.5 collective-permute-start.3
  1.8 2.6 %collective-permute-start.2 = (bf16[336,1536]{1,0:T(8,128)(2,1)S(1)}, bf16[336,1536]{1,0:T(8,128)(2,1)}, u32[]{:S(2)}, u32[]{:S(2)}) collective-permute-start(bf16[336,1536]{1,0:T(8,128)(2,1)S(1)} %pad_maximum_fusion.rest_0_.rest_3_), channel_id=1, source_target_pairs={{0,4},{1,5},{2,6},{3,7},{4,0},{5,1},{6,2},{7,3},{8,12},{9,13},{10,... | collective-permute-start | bytes 3096584 | tf_op jit(solution)/shard_map/ppermute | solution.py:34
  4.4 0.7 collective-permute-start.1
  5.1 4.4 %collective-permute-start = (bf16[336,1536]{1,0:T(8,128)(2,1)S(1)}, bf16[336,1536]{1,0:T(8,128)(2,1)}, u32[]{:S(2)}, u32[]{:S(2)}) collective-permute-start(bf16[336,1536]{1,0:T(8,128)(2,1)S(1)} %pad_maximum_fusion.rest_0_.rest_3_), channel_id=1, source_target_pairs={{0,8},{1,9},{2,10},{3,11},{4,12},{5,13},{6,14},{7,15},{8,0},{9,1},... | collective-permute-start | bytes 3096584 | tf_op jit(solution)/shard_map/ppermute | solution.py:34
  9.5 0.8 convert_bitcast_fusion
  10.4 1.3 collective-permute-start.5
  11.8 1.7 collective-permute-done.5.bottom
  13.4 16.6 %collective-permute-start.4 = (bf16[1,1536]{1,0:T(2,128)(2,1)S(1)}, bf16[1,1536]{1,0:T(2,128)(2,1)S(1)}, u32[]{:S(2)}, u32[]{:S(2)}) collective-permute-start(bf16[1,1536]{1,0:T(2,128)(2,1)S(1)} %get-tuple-element.88), channel_id=1, source_target_pairs={{0,2},{1,3},{2,4},{3,5},{4,6},{5,7},{6,8},{7,9},{8,10},{9,11},{10,... | collective-permute-start | bytes 9224 | tf_op jit(solution)/shard_map/ppermute | solution.py:34
  30.0 0.6 stack.135.place
  30.6 0.2 collective-permute-done.4.top
  30.8 0.0 collective-permute-done.2.rest_1_.rest_4_
  30.8 0.0 collective-permute-done.1
  30.8 1.7 collective-permute-done.rest_4_.rest_7_
  32.5 1.3 collective-permute-start.8
  33.8 0.1 collective-permute-start.9
  33.9 0.5 collective-permute-start.10
  34.4 4.0 %collective-permute-start.7 = (bf16[336,1536]{1,0:T(8,128)(2,1)}, bf16[336,1536]{1,0:T(8,128)(2,1)}, u32[]{:S(2)}, u32[]{:S(2)}) collective-permute-start(bf16[336,1536]{1,0:T(8,128)(2,1)} %collective-permute-done.rest_4_.rest_7_), channel_id=1, source_target_pairs={{0,4},{1,5},{2,6},{3,7},{4,0},{5,1},{6,2},{7,3},{8,12},{9,13},{10,... | collective-permute-start | bytes 3096584 | tf_op jit(solution)/shard_map/ppermute | solution.py:34
  38.4 0.7 collective-permute-start.6
  39.1 0.6 broadcast_in_dim.12.sep_bias
  39.7 0.6 broadcast_in_dim.13.head_bias
  40.3 0.6 broadcast_in_dim.14.pair
  40.9 6.8 %conv.1 = (bf16[512,1536]{1,0:T(8,128)(2,1)}, bf16[320,1536]{1,0:T(8,128)(2,1)}, bf16[192,1536]{1,0:T(8,128)(2,1)}) custom-call(bf16[256,1536]{1,0:T(8,128)(2,1)} %bitcast.42, bf16[512,1536]{1,0:T(8,128)(2,1)} %bitcast.43, bf16[1,1536]{1,0:T(2,128)(2,1)} %copy-done.20, bf16[1,1536]{1,0:T(2,128)(2,1)} %copy-done.19, f32[3,1536]{1,0:T(4,128)} %taps.1), custom_call_target="tpu_custom_call" | custom-call | flops 805306368 | bytes 4718592 | tf_op jit(solution)/shard_map/conv/pallas_call | solution.py:69
  47.7 11.7 %collective-permute-done.8 = bf16[336,1536]{1,0:T(8,128)(2,1)S(1)} collective-permute-done((bf16[336,1536]{1,0:T(8,128)(2,1)S(1)}, bf16[336,1536]{1,0:T(8,128)(2,1)S(1)}, u32[]{:S(2)}, u32[]{:S(2)}) %collective-permute-start.8) | collective-permute-done | bytes 1032224 | tf_op jit(solution)/shard_map/ppermute | solution.py:34
  59.4 2.6 %collective-permute-done.7.rest_5_.rest_8_ = bf16[336,1536]{1,0:T(8,128)(2,1)} collective-permute-done((bf16[336,1536]{1,0:T(8,128)(2,1)}, bf16[336,1536]{1,0:T(8,128)(2,1)}, u32[]{:S(2)}, u32[]{:S(2)}) %collective-permute-start.7) | collective-permute-done | bytes 1032224 | tf_op jit(solution)/shard_map/ppermute | solution.py:34
  62.0 0.1 broadcast_select_fusion.rest_8_.rest_11_
  62.1 0.1 collective-permute-start.15
  62.2 1.8 collective-permute-start.12
  64.0 1.3 collective-permute-start.13
  65.3 0.2 collective-permute-start.14
  65.5 4.7 %collective-permute-start.11 = (bf16[320,1536]{1,0:T(8,128)(2,1)S(1)}, bf16[320,1536]{1,0:T(8,128)(2,1)S(1)}, u32[]{:S(2)}, u32[]{:S(2)}) collective-permute-start(bf16[320,1536]{1,0:T(8,128)(2,1)S(1)} %copy-done.11), channel_id=1, source_target_pairs={{0,31},{1,30},{2,29},{3,28},{4,27},{5,26},{6,25},{7,24},{8,23},{9,... | collective-permute-start | bytes 2949128 | tf_op jit(solution)/shard_map/ppermute | solution.py:34
  70.2 22.7 %collective-permute-done.11.first = bf16[320,1536]{1,0:T(8,128)(2,1)S(1)} collective-permute-done((bf16[320,1536]{1,0:T(8,128)(2,1)S(1)}, bf16[320,1536]{1,0:T(8,128)(2,1)S(1)}, u32[]{:S(2)}, u32[]{:S(2)}) %collective-permute-start.11) | collective-permute-done | bytes 983072 | tf_op jit(solution)/shard_map/ppermute | solution.py:34
  93.0 15.5 %collective-permute-done.12.rest_9_.rest_12_ = bf16[336,1536]{1,0:T(8,128)(2,1)S(1)} collective-permute-done((bf16[336,1536]{1,0:T(8,128)(2,1)S(1)}, bf16[336,1536]{1,0:T(8,128)(2,1)S(1)}, u32[]{:S(2)}, u32[]{:S(2)}) %collective-permute-start.12) | collective-permute-done | bytes 1032224 | tf_op jit(solution)/shard_map/ppermute | solution.py:34
  108.5 5.7 %collective-permute-done.13 = bf16[336,1536]{1,0:T(8,128)(2,1)S(1)} collective-permute-done((bf16[336,1536]{1,0:T(8,128)(2,1)S(1)}, bf16[336,1536]{1,0:T(8,128)(2,1)S(1)}, u32[]{:S(2)}, u32[]{:S(2)}) %collective-permute-start.13) | collective-permute-done | bytes 1032224 | tf_op jit(solution)/shard_map/ppermute | solution.py:34
  114.2 0.1 collective-permute-start.20
  114.3 0.5 collective-permute-start.21
  114.9 1.6 collective-permute-start.16
  116.4 0.1 slice_select_fusion.rest_19_
  116.5 7.3 %collective-permute-done.16.rest_13_.rest_16_ = bf16[96,1536]{1,0:T(8,128)(2,1)S(1)} collective-permute-done((bf16[96,1536]{1,0:T(8,128)(2,1)S(1)}, bf16[96,1536]{1,0:T(8,128)(2,1)S(1)}, u32[]{:S(2)}, u32[]{:S(2)}) %collective-permute-start.16) | collective-permute-done | bytes 294944 | tf_op jit(solution)/shard_map/ppermute | solution.py:34
  123.9 0.5 collective-permute-start.19
  124.4 1.6 collective-permute-start.18
  125.9 3.4 %collective-permute-start.17 = (bf16[192,1536]{1,0:T(8,128)(2,1)}, bf16[192,1536]{1,0:T(8,128)(2,1)S(1)}, u32[]{:S(2)}, u32[]{:S(2)}) collective-permute-start(bf16[192,1536]{1,0:T(8,128)(2,1)} %get-tuple-element.69), channel_id=1, source_target_pairs={{0,31},{1,30},{2,29},{3,28},{4,27},{5,26},{6,25},{7,24},{8,23},{9,... | collective-permute-start | bytes 1769480 | tf_op jit(solution)/shard_map/ppermute | solution.py:34
  129.4 0.7 copy-done.18
  130.0 20.4 %early.1 = (bf16[832,1536]{1,0:T(8,128)(2,1)}, bf16[832,1920]{1,0:T(8,128)(2,1)}) custom-call(s32[33]{0:T(128)} %stack.135.place, f32[1,1536]{1,0:T(1,128)} %broadcast_in_dim.12.sep_bias, f32[1,3840]{1,0:T(1,128)} %broadcast_in_dim.13.head_bias, bf16[512,1536]{1,0:T(8,128)(2,1)} %get-tuple-element.71.own_values, bf16[320,1536]{1,0:T(8,128)(2,1)} %copy-done.10, ...), custom_call_target="tpu_custom_call" | custom-call | flops 8833204224 | bytes 9437184 | tf_op jit(solution)/shard_map/early/pallas_call | solution.py:157
  150.5 4.9 %collective-permute-done.18.rest_20_ = bf16[240,1536]{1,0:T(8,128)(2,1)S(1)} collective-permute-done((bf16[240,1536]{1,0:T(8,128)(2,1)S(1)}, bf16[240,1536]{1,0:T(8,128)(2,1)S(1)}, u32[]{:S(2)}, u32[]{:S(2)}) %collective-permute-start.18) | collective-permute-done | bytes 737312 | tf_op jit(solution)/shard_map/ppermute | solution.py:34
  155.4 2.2 %collective-permute-done.23.rest_22_ = bf16[240,1536]{1,0:T(8,128)(2,1)S(1)} collective-permute-done((bf16[240,1536]{1,0:T(8,128)(2,1)S(1)}, bf16[240,1536]{1,0:T(8,128)(2,1)S(1)}, u32[]{:S(2)}, u32[]{:S(2)}) %collective-permute-start.23) | collective-permute-done | bytes 737312 | tf_op jit(solution)/shard_map/ppermute | solution.py:34
  157.6 0.9 copy-done.14
  158.5 37.8 %finish.1 = bf16[512,3840]{1,0:T(8,128)(2,1)} custom-call(s32[33]{0:T(128)} %stack.135.place, f32[1,1536]{1,0:T(1,128)} %broadcast_in_dim.12.sep_bias, f32[1,3840]{1,0:T(1,128)} %broadcast_in_dim.13.head_bias, s32[1,3840]{1,0:T(1,128)} %broadcast_in_dim.14.pair, bf16[832,1536]{1,0:T(8,128)(2,1)} %get-tuple-element.82.rest_0_, bf16[192,1536]{1,0:T(8,128)(2,1)} %copy-done.15, ...), custom_call_target="tpu_custom_call" | custom-call | flops 60397977600 | bytes 31457280 | tf_op jit(solution)/shard_map/finish/pallas_call | solution.py:295
  (54 shorter events, 0.1 us)
Async XLA Ops:
  0.0 40.3 %copy-start.5 = (s32[3840]{0:T(1024)S(1)}, s32[3840]{0:T(1024)}, u32[]{:S(2)}) copy-start(s32[3840]{0:T(1024)} %param.15) | copy-start | bytes 46084
  0.0 39.7 %copy-start.4 = (f32[3840]{0:T(1024)S(1)}, f32[3840]{0:T(1024)}, u32[]{:S(2)}) copy-start(f32[3840]{0:T(1024)} %param.14) | copy-start | bytes 46084
  0.0 39.1 %copy-start.6 = (f32[1536]{0:T(1024)S(1)}, f32[1536]{0:T(1024)}, u32[]{:S(2)}) copy-start(f32[1536]{0:T(1024)} %param.12) | copy-start | bytes 18436
  1.3 33.1 %copy-start.1 = (bf16[336,1536]{1,0:T(8,128)(2,1)}, bf16[336,1536]{1,0:T(8,128)(2,1)S(1)}, u32[]{:S(2)}) copy-start(bf16[336,1536]{1,0:T(8,128)(2,1)S(1)} %pad_maximum_fusion.rest_0_.rest_3_) | copy-start | bytes 3096580
  1.3 29.5 %collective-permute-start.3 = (bf16[336,1536]{1,0:T(8,128)(2,1)S(1)}, bf16[336,1536]{1,0:T(8,128)(2,1)}, u32[]{:S(2)}, u32[]{:S(2)}) collective-permute-start(bf16[336,1536]{1,0:T(8,128)(2,1)S(1)} %pad_maximum_fusion.rest_0_.rest_3_), channel_id=1, source_target_pairs={{0,2},{1,3},{2,0},{3,1},{4,6},{5,7},{6,4},{7,5},{8,10},{9,11},{10,... | collective-permute-start | bytes 3096584 | tf_op jit(solution)/shard_map/ppermute | solution.py:34
  1.8 29.0 %collective-permute-start.2 = (bf16[336,1536]{1,0:T(8,128)(2,1)S(1)}, bf16[336,1536]{1,0:T(8,128)(2,1)}, u32[]{:S(2)}, u32[]{:S(2)}) collective-permute-start(bf16[336,1536]{1,0:T(8,128)(2,1)S(1)} %pad_maximum_fusion.rest_0_.rest_3_), channel_id=1, source_target_pairs={{0,4},{1,5},{2,6},{3,7},{4,0},{5,1},{6,2},{7,3},{8,12},{9,13},{10,... | collective-permute-start | bytes 3096584 | tf_op jit(solution)/shard_map/ppermute | solution.py:34
  4.4 26.4 %collective-permute-start.1 = (bf16[336,1536]{1,0:T(8,128)(2,1)S(1)}, bf16[336,1536]{1,0:T(8,128)(2,1)S(1)}, u32[]{:S(2)}, u32[]{:S(2)}) collective-permute-start(bf16[336,1536]{1,0:T(8,128)(2,1)S(1)} %pad_maximum_fusion.rest_0_.rest_3_), channel_id=1, source_target_pairs={{8,16},{9,17},{10,18},{11,19},{12,20},{13,21},{14,22},{15,23},{16,... | collective-permute-start | bytes 3096584 | tf_op jit(solution)/shard_map/ppermute | solution.py:34
  5.1 27.4 %collective-permute-start = (bf16[336,1536]{1,0:T(8,128)(2,1)S(1)}, bf16[336,1536]{1,0:T(8,128)(2,1)}, u32[]{:S(2)}, u32[]{:S(2)}) collective-permute-start(bf16[336,1536]{1,0:T(8,128)(2,1)S(1)} %pad_maximum_fusion.rest_0_.rest_3_), channel_id=1, source_target_pairs={{0,8},{1,9},{2,10},{3,11},{4,12},{5,13},{6,14},{7,15},{8,0},{9,1},... | collective-permute-start | bytes 3096584 | tf_op jit(solution)/shard_map/ppermute | solution.py:34
  10.4 3.1 %collective-permute-start.5 = (bf16[1,1536]{1,0:T(2,128)(2,1)S(1)}, bf16[1,1536]{1,0:T(2,128)(2,1)S(1)}, u32[]{:S(2)}, u32[]{:S(2)}) collective-permute-start(bf16[1,1536]{1,0:T(2,128)(2,1)S(1)} %get-tuple-element.87), channel_id=1, source_target_pairs={{2,0},{3,1},{4,2},{5,3},{6,4},{7,5},{8,6},{9,7},{10,8},{11,9},{12,... | collective-permute-start | bytes 9224 | tf_op jit(solution)/shard_map/ppermute | solution.py:34
  13.4 27.5 %copy-start.19 = (bf16[1,1536]{1,0:T(2,128)(2,1)}, bf16[1,1536]{1,0:T(2,128)(2,1)S(1)}, u32[]{:S(2)}) copy-start(bf16[1,1536]{1,0:T(2,128)(2,1)S(1)} %collective-permute-done.5.bottom) | copy-start | bytes 9220
  13.4 17.4 %collective-permute-start.4 = (bf16[1,1536]{1,0:T(2,128)(2,1)S(1)}, bf16[1,1536]{1,0:T(2,128)(2,1)S(1)}, u32[]{:S(2)}, u32[]{:S(2)}) collective-permute-start(bf16[1,1536]{1,0:T(2,128)(2,1)S(1)} %get-tuple-element.88), channel_id=1, source_target_pairs={{0,2},{1,3},{2,4},{3,5},{4,6},{5,7},{6,8},{7,9},{8,10},{9,11},{10,... | collective-permute-start | bytes 9224 | tf_op jit(solution)/shard_map/ppermute | solution.py:34
  30.8 10.1 %copy-start.20 = (bf16[1,1536]{1,0:T(2,128)(2,1)}, bf16[1,1536]{1,0:T(2,128)(2,1)S(1)}, u32[]{:S(2)}) copy-start(bf16[1,1536]{1,0:T(2,128)(2,1)S(1)} %collective-permute-done.4.top) | copy-start | bytes 9220
  32.5 26.9 %collective-permute-start.8 = (bf16[336,1536]{1,0:T(8,128)(2,1)S(1)}, bf16[336,1536]{1,0:T(8,128)(2,1)S(1)}, u32[]{:S(2)}, u32[]{:S(2)}) collective-permute-start(bf16[336,1536]{1,0:T(8,128)(2,1)S(1)} %collective-permute-done.1), channel_id=1, source_target_pairs={{8,0},{9,1},{10,2},{11,3},{12,4},{13,5},{14,6},{15,7},{16,24},{17,... | collective-permute-start | bytes 3096584 | tf_op jit(solution)/shard_map/ppermute | solution.py:34
  33.8 25.6 %collective-permute-start.9 = (bf16[336,1536]{1,0:T(8,128)(2,1)}, bf16[336,1536]{1,0:T(8,128)(2,1)}, u32[]{:S(2)}, u32[]{:S(2)}) collective-permute-start(bf16[336,1536]{1,0:T(8,128)(2,1)} %collective-permute-done.2.rest_1_.rest_4_), channel_id=1, source_target_pairs={{0,2},{1,3},{2,0},{3,1},{4,6},{5,7},{6,4},{7,5},{8,10},{9,11},{10,... | collective-permute-start | bytes 3096584 | tf_op jit(solution)/shard_map/ppermute | solution.py:34
  33.9 25.5 %collective-permute-start.10 = (bf16[336,1536]{1,0:T(8,128)(2,1)}, bf16[336,1536]{1,0:T(8,128)(2,1)}, u32[]{:S(2)}, u32[]{:S(2)}) collective-permute-start(bf16[336,1536]{1,0:T(8,128)(2,1)} %collective-permute-done.rest_4_.rest_7_), channel_id=1, source_target_pairs={{0,2},{1,3},{2,0},{3,1},{4,6},{5,7},{6,4},{7,5},{8,10},{9,11},{10,... | collective-permute-start | bytes 3096584 | tf_op jit(solution)/shard_map/ppermute | solution.py:34
  34.4 27.6 %collective-permute-start.7 = (bf16[336,1536]{1,0:T(8,128)(2,1)}, bf16[336,1536]{1,0:T(8,128)(2,1)}, u32[]{:S(2)}, u32[]{:S(2)}) collective-permute-start(bf16[336,1536]{1,0:T(8,128)(2,1)} %collective-permute-done.rest_4_.rest_7_), channel_id=1, source_target_pairs={{0,4},{1,5},{2,6},{3,7},{4,0},{5,1},{6,2},{7,3},{8,12},{9,13},{10,... | collective-permute-start | bytes 3096584 | tf_op jit(solution)/shard_map/ppermute | solution.py:34
  38.4 23.6 %collective-permute-start.6 = (bf16[336,1536]{1,0:T(8,128)(2,1)}, bf16[336,1536]{1,0:T(8,128)(2,1)S(1)}, u32[]{:S(2)}, u32[]{:S(2)}) collective-permute-start(bf16[336,1536]{1,0:T(8,128)(2,1)} %collective-permute-done.rest_4_.rest_7_), channel_id=1, source_target_pairs={{8,16},{9,17},{10,18},{11,19},{12,20},{13,21},{14,22},{15,23},{16,... | collective-permute-start | bytes 3096584 | tf_op jit(solution)/shard_map/ppermute | solution.py:34
  47.7 17.8 %copy-start.11 = (bf16[320,1536]{1,0:T(8,128)(2,1)S(1)}, bf16[320,1536]{1,0:T(8,128)(2,1)}, u32[]{:S(2)}) copy-start(bf16[320,1536]{1,0:T(8,128)(2,1)} %get-tuple-element.63) | copy-start | bytes 2949124
  62.1 67.2 %copy-start = (bf16[336,1536]{1,0:T(8,128)(2,1)}, bf16[336,1536]{1,0:T(8,128)(2,1)S(1)}, u32[]{:S(2)}) copy-start(bf16[336,1536]{1,0:T(8,128)(2,1)S(1)} %broadcast_select_fusion.rest_8_.rest_11_) | copy-start | bytes 3096580
  62.1 30.9 %collective-permute-start.15 = (bf16[336,1536]{1,0:T(8,128)(2,1)S(1)}, bf16[336,1536]{1,0:T(8,128)(2,1)S(1)}, u32[]{:S(2)}, u32[]{:S(2)}) collective-permute-start(bf16[336,1536]{1,0:T(8,128)(2,1)S(1)} %broadcast_select_fusion.rest_8_.rest_11_), channel_id=1, source_target_pairs={{0,2},{1,3},{2,0},{3,1},{4,6},{5,7},{6,4},{7,5},{8,10},{9,11},{10,... | collective-permute-start | bytes 3096584 | tf_op jit(solution)/shard_map/ppermute | solution.py:34
  62.2 46.3 %collective-permute-start.12 = (bf16[336,1536]{1,0:T(8,128)(2,1)S(1)}, bf16[336,1536]{1,0:T(8,128)(2,1)S(1)}, u32[]{:S(2)}, u32[]{:S(2)}) collective-permute-start(bf16[336,1536]{1,0:T(8,128)(2,1)S(1)} %broadcast_select_fusion.rest_8_.rest_11_), channel_id=1, source_target_pairs={{0,4},{1,5},{2,6},{3,7},{4,0},{5,1},{6,2},{7,3},{8,12},{9,13},{10,... | collective-permute-start | bytes 3096584 | tf_op jit(solution)/shard_map/ppermute | solution.py:34
  64.0 50.1 %collective-permute-start.13 = (bf16[336,1536]{1,0:T(8,128)(2,1)S(1)}, bf16[336,1536]{1,0:T(8,128)(2,1)S(1)}, u32[]{:S(2)}, u32[]{:S(2)}) collective-permute-start(bf16[336,1536]{1,0:T(8,128)(2,1)S(1)} %collective-permute-done.6), channel_id=1, source_target_pairs={{8,0},{9,1},{10,2},{11,3},{12,4},{13,5},{14,6},{15,7},{16,24},{17,... | collective-permute-start | bytes 3096584 | tf_op jit(solution)/shard_map/ppermute | solution.py:34
  65.3 48.9 %collective-permute-start.14 = (bf16[336,1536]{1,0:T(8,128)(2,1)}, bf16[336,1536]{1,0:T(8,128)(2,1)S(1)}, u32[]{:S(2)}, u32[]{:S(2)}) collective-permute-start(bf16[336,1536]{1,0:T(8,128)(2,1)} %collective-permute-done.7.rest_5_.rest_8_), channel_id=1, source_target_pairs={{0,2},{1,3},{2,0},{3,1},{4,6},{5,7},{6,4},{7,5},{8,10},{9,11},{10,... | collective-permute-start | bytes 3096584 | tf_op jit(solution)/shard_map/ppermute | solution.py:34
  65.5 27.4 %collective-permute-start.11 = (bf16[320,1536]{1,0:T(8,128)(2,1)S(1)}, bf16[320,1536]{1,0:T(8,128)(2,1)S(1)}, u32[]{:S(2)}, u32[]{:S(2)}) collective-permute-start(bf16[320,1536]{1,0:T(8,128)(2,1)S(1)} %copy-done.11), channel_id=1, source_target_pairs={{0,31},{1,30},{2,29},{3,28},{4,27},{5,26},{6,25},{7,24},{8,23},{9,... | collective-permute-start | bytes 2949128 | tf_op jit(solution)/shard_map/ppermute | solution.py:34
  93.0 21.2 %copy-start.10 = (bf16[320,1536]{1,0:T(8,128)(2,1)}, bf16[320,1536]{1,0:T(8,128)(2,1)S(1)}, u32[]{:S(2)}) copy-start(bf16[320,1536]{1,0:T(8,128)(2,1)S(1)} %collective-permute-done.11.first) | copy-start | bytes 2949124
  93.0 36.3 %copy-start.7 = (bf16[336,1536]{1,0:T(8,128)(2,1)}, bf16[336,1536]{1,0:T(8,128)(2,1)S(1)}, u32[]{:S(2)}) copy-start(bf16[336,1536]{1,0:T(8,128)(2,1)S(1)} %collective-permute-done.15.rest_10_.rest_13_) | copy-start | bytes 3096580
  108.5 20.8 %copy-start.8 = (bf16[336,1536]{1,0:T(8,128)(2,1)}, bf16[336,1536]{1,0:T(8,128)(2,1)S(1)}, u32[]{:S(2)}) copy-start(bf16[336,1536]{1,0:T(8,128)(2,1)S(1)} %collective-permute-done.12.rest_9_.rest_12_) | copy-start | bytes 3096580
  114.2 15.2 %copy-start.9 = (bf16[336,1536]{1,0:T(8,128)(2,1)}, bf16[336,1536]{1,0:T(8,128)(2,1)S(1)}, u32[]{:S(2)}) copy-start(bf16[336,1536]{1,0:T(8,128)(2,1)S(1)} %collective-permute-done.14.rest_7_.rest_10_) | copy-start | bytes 3096580
  114.2 15.1 %collective-permute-start.20 = (bf16[336,1536]{1,0:T(8,128)(2,1)S(1)}, bf16[336,1536]{1,0:T(8,128)(2,1)}, u32[]{:S(2)}, u32[]{:S(2)}) collective-permute-start(bf16[336,1536]{1,0:T(8,128)(2,1)S(1)} %collective-permute-done.12.rest_9_.rest_12_), channel_id=1, source_target_pairs={{0,2},{1,3},{2,0},{3,1},{4,6},{5,7},{6,4},{7,5},{8,10},{9,11},{10,... | collective-permute-start | bytes 3096584 | tf_op jit(solution)/shard_map/ppermute | solution.py:34
  114.3 15.0 %copy-start.3 = (bf16[96,1536]{1,0:T(8,128)(2,1)}, bf16[96,1536]{1,0:T(8,128)(2,1)S(1)}, u32[]{:S(2)}) copy-start(bf16[96,1536]{1,0:T(8,128)(2,1)S(1)} %slice_select_fusion.1.rest_12_.rest_15_) | copy-start | bytes 884740
  114.3 11.6 %collective-permute-start.21 = (bf16[96,1536]{1,0:T(8,128)(2,1)S(1)}, bf16[96,1536]{1,0:T(8,128)(2,1)S(1)}, u32[]{:S(2)}, u32[]{:S(2)}) collective-permute-start(bf16[96,1536]{1,0:T(8,128)(2,1)S(1)} %slice_select_fusion.1.rest_12_.rest_15_), channel_id=1, source_target_pairs={{0,2},{1,3},{2,0},{3,1},{4,6},{5,7},{6,4},{7,5},{8,10},{9,11},{10,... | collective-permute-start | bytes 884744 | tf_op jit(solution)/shard_map/ppermute | solution.py:34
  114.9 9.0 %collective-permute-start.16 = (bf16[96,1536]{1,0:T(8,128)(2,1)S(1)}, bf16[96,1536]{1,0:T(8,128)(2,1)S(1)}, u32[]{:S(2)}, u32[]{:S(2)}) collective-permute-start(bf16[96,1536]{1,0:T(8,128)(2,1)S(1)} %slice_select_fusion.1.rest_12_.rest_15_), channel_id=1, source_target_pairs={{0,4},{1,5},{2,6},{3,7},{4,0},{5,1},{6,2},{7,3},{8,12},{9,13},{10,... | collective-permute-start | bytes 884744 | tf_op jit(solution)/shard_map/ppermute | solution.py:34
  116.5 33.9 %copy-start.2 = (bf16[240,1536]{1,0:T(8,128)(2,1)}, bf16[240,1536]{1,0:T(8,128)(2,1)S(1)}, u32[]{:S(2)}) copy-start(bf16[240,1536]{1,0:T(8,128)(2,1)S(1)} %slice_select_fusion.rest_19_) | copy-start | bytes 2211844
  123.8 2.1 %copy-start.17 = (bf16[96,1536]{1,0:T(8,128)(2,1)}, bf16[96,1536]{1,0:T(8,128)(2,1)S(1)}, u32[]{:S(2)}) copy-start(bf16[96,1536]{1,0:T(8,128)(2,1)S(1)} %collective-permute-done.16.rest_13_.rest_16_) | copy-start | bytes 884740
  123.8 5.4 %collective-permute-start.22 = (bf16[96,1536]{1,0:T(8,128)(2,1)S(1)}, bf16[96,1536]{1,0:T(8,128)(2,1)S(1)}, u32[]{:S(2)}, u32[]{:S(2)}) collective-permute-start(bf16[96,1536]{1,0:T(8,128)(2,1)S(1)} %collective-permute-done.16.rest_13_.rest_16_), channel_id=1, source_target_pairs={{0,2},{1,3},{2,0},{3,1},{4,6},{5,7},{6,4},{7,5},{8,10},{9,11},{10,... | collective-permute-start | bytes 884744 | tf_op jit(solution)/shard_map/ppermute | solution.py:34
  123.9 26.6 %collective-permute-start.19 = (bf16[240,1536]{1,0:T(8,128)(2,1)S(1)}, bf16[240,1536]{1,0:T(8,128)(2,1)S(1)}, u32[]{:S(2)}, u32[]{:S(2)}) collective-permute-start(bf16[240,1536]{1,0:T(8,128)(2,1)S(1)} %slice_select_fusion.rest_19_), channel_id=1, source_target_pairs={{0,2},{1,3},{2,0},{3,1},{4,6},{5,7},{6,4},{7,5},{8,10},{9,11},{10,... | collective-permute-start | bytes 2211848 | tf_op jit(solution)/shard_map/ppermute | solution.py:34
  124.4 31.0 %collective-permute-start.18 = (bf16[240,1536]{1,0:T(8,128)(2,1)S(1)}, bf16[240,1536]{1,0:T(8,128)(2,1)S(1)}, u32[]{:S(2)}, u32[]{:S(2)}) collective-permute-start(bf16[240,1536]{1,0:T(8,128)(2,1)S(1)} %slice_select_fusion.rest_19_), channel_id=1, source_target_pairs={{0,4},{1,5},{2,6},{3,7},{4,0},{5,1},{6,2},{7,3},{8,12},{9,13},{10,... | collective-permute-start | bytes 2211848 | tf_op jit(solution)/shard_map/ppermute | solution.py:34
  125.9 3.4 %copy-start.16 = (bf16[96,1536]{1,0:T(8,128)(2,1)}, bf16[96,1536]{1,0:T(8,128)(2,1)S(1)}, u32[]{:S(2)}) copy-start(bf16[96,1536]{1,0:T(8,128)(2,1)S(1)} %collective-permute-done.21.rest_14_.rest_17_) | copy-start | bytes 884740
  125.9 24.5 %collective-permute-start.17 = (bf16[192,1536]{1,0:T(8,128)(2,1)}, bf16[192,1536]{1,0:T(8,128)(2,1)S(1)}, u32[]{:S(2)}, u32[]{:S(2)}) collective-permute-start(bf16[192,1536]{1,0:T(8,128)(2,1)} %get-tuple-element.69), channel_id=1, source_target_pairs={{0,31},{1,30},{2,29},{3,28},{4,27},{5,26},{6,25},{7,24},{8,23},{9,... | collective-permute-start | bytes 1769480 | tf_op jit(solution)/shard_map/ppermute | solution.py:34
  129.3 0.7 copy-start.18
  150.5 7.2 %copy-start.15 = (bf16[192,1536]{1,0:T(8,128)(2,1)}, bf16[192,1536]{1,0:T(8,128)(2,1)S(1)}, u32[]{:S(2)}) copy-start(bf16[192,1536]{1,0:T(8,128)(2,1)S(1)} %collective-permute-done.17.rest_1_) | copy-start | bytes 1769476
  150.5 7.1 %copy-start.12 = (bf16[240,1536]{1,0:T(8,128)(2,1)}, bf16[240,1536]{1,0:T(8,128)(2,1)S(1)}, u32[]{:S(2)}) copy-start(bf16[240,1536]{1,0:T(8,128)(2,1)S(1)} %collective-permute-done.19.rest_21_) | copy-start | bytes 2211844
  155.4 2.2 %copy-start.13 = (bf16[240,1536]{1,0:T(8,128)(2,1)}, bf16[240,1536]{1,0:T(8,128)(2,1)S(1)}, u32[]{:S(2)}) copy-start(bf16[240,1536]{1,0:T(8,128)(2,1)S(1)} %collective-permute-done.18.rest_20_) | copy-start | bytes 2211844
  155.4 2.2 %collective-permute-start.23 = (bf16[240,1536]{1,0:T(8,128)(2,1)S(1)}, bf16[240,1536]{1,0:T(8,128)(2,1)S(1)}, u32[]{:S(2)}, u32[]{:S(2)}) collective-permute-start(bf16[240,1536]{1,0:T(8,128)(2,1)S(1)} %collective-permute-done.18.rest_20_), channel_id=1, source_target_pairs={{0,2},{1,3},{2,0},{3,1},{4,6},{5,7},{6,4},{7,5},{8,10},{9,11},{10,... | collective-permute-start | bytes 2211848 | tf_op jit(solution)/shard_map/ppermute | solution.py:34
  157.6 0.9 copy-start.14

commit v5 on v4

--- a/solution.py
+++ b/solution.py
@@ -370,8 +370,12 @@
     coarse, skip = coarse[0], skip[0]
     first = edge(coarse[:1], skip[:1])
     last = edge(coarse[-1:], skip[-1:])
-    top = send(last, lambda s, b: (s + 1, b) if s + 1 < seq else None)
-    bottom = send(first, lambda s, b: (s - 1, b) if s > 0 else None)
+    even = lax.axis_index("seq") % 2 == 0
+    inside = send(jnp.where(even, last, first), across_cores)
+    outside = send(
+        jnp.where(even, first, last),
+        lambda s, b: (s + 2 * (s % 2) - 1, b) if 0 <= s + 2 * (s % 2) - 1 < seq else None,
+    )
     to_mirror = lambda s, b: (seq - 1 - s, (b + batch // 2) % batch)
     z = lax.axis_index("seq") // 4
     pick = lambda a, c: jnp.where((z == 1) | (z == 2), a, c)
@@ -381,19 +385,20 @@
     q0 = send(own, across_middle)
     y0 = send(own, across_pair)
     k_own = send(own, across_cores)
-    small = (sep_bias, head_bias, strand_pair, places())
-    edges = (top, bottom)
+    small = (sep_bias, head_bias, strand_pair)
+    edges = (inside, outside)
     near, q0, y0, k_own, edges, small = tied(near, q0, y0, k_own, edges, small)
-    sep_bias, head_bias, strand_pair, place = small
-
-    top, bottom = edges
+    sep_bias, head_bias, strand_pair = small
+
+    inside, outside = edges
+    top, bottom = jnp.where(even, outside, inside), jnp.where(even, inside, outside)
     own_values, *flipped = conv(coarse, skip, top, bottom, depth_kernel, (5 * skip.shape[0] // 8,))
     q1 = send(near, across_middle)
     y1 = send(near, across_pair)
     s0 = send(q0, to_line_ends)
     k_y0 = send(y0, across_cores)
     k_near = send(near, across_cores)
-    small = (sep_bias[None], head_bias[None], strand_pair[None], place)
+    small = (sep_bias[None], head_bias[None], strand_pair[None], places())
     q1, y1, s0, k_y0, k_near, flipped, own_values, small = tied(
         q1, y1, s0, k_y0, k_near, flipped, own_values, small
     )

time: 197 us -> 194 us (0.985)
  starting transfers between devices: 48.4 us -> 41.2 us
  waiting for transfers between devices: 76.2 us -> 79.3 us
    ppermute x24, starting transfers between devices: 48.4 us -> 41.2 us  [send(): return lax.ppermute(array, BOTH, route(seq, batch, move))]
    ppermute x24, waiting for transfers between devices: 76.2 us -> 79.3 us  [send(): return lax.ppermute(array, BOTH, route(seq, batch, move))]
  transfers between devices with their start and end apart: 24 -> 24, of which waited for: 11 -> 10; matrix products, arithmetic and copies ran while one was open for 2% -> 2% of each run, Pallas kernels for 14% -> 14%
where the time goes in v5:
time: 194 us
  waiting for transfers between devices  79.3 us (41%)
  Pallas kernels  65 us (34%)
  starting transfers between devices  41.2 us (21%)
  local copies, waits for them, and re-layouts  5.2 us (3%)
  other arithmetic  2.98 us (2%)
    ppermute x24, waiting for transfers between devices, send(): return lax.ppermute(array, BOTH, route(seq, batch, move))  79.3 us
    ppermute x24, starting transfers between devices, send(): return lax.ppermute(array, BOTH, route(seq, batch, move))  41.2 us
    pallas_call x1, Pallas kernels, finish(): pl.pallas_call(functools.partial(finish_kernel, sep_blocks, near_blocks,...  37.8 us
    pallas_call x1, Pallas kernels, early(): pl.pallas_call(functools.partial(early_kernel, sep_blocks, near_blocks),...  20.4 us
    pallas_call x1, Pallas kernels, conv(): pl.pallas_call(conv_kernel, grid=(width // step,), in_specs=[column(coars...  6.79 us
  transfers between devices with their start and end apart: 24, of which 10 were waited for; matrix products, arithmetic and copies ran while one was open for 2% of the time, Pallas kernels for 14%

profile of v5, /device:TPU:0, one launch (start us, length us, event | category | flops | bytes accessed | tf_op | source)
XLA Modules:
  0.0 194.0 jit_solution(2795055361359238857)
XLA Ops:
  0.0 1.3 pad_maximum_fusion.rest_0_.rest_3_
  1.3 0.5 collective-permute-start.3
  1.8 2.6 %collective-permute-start.2 = (bf16[336,1536]{1,0:T(8,128)(2,1)S(1)}, bf16[336,1536]{1,0:T(8,128)(2,1)}, u32[]{:S(2)}, u32[]{:S(2)}) collective-permute-start(bf16[336,1536]{1,0:T(8,128)(2,1)S(1)} %pad_maximum_fusion.rest_0_.rest_3_), channel_id=1, source_target_pairs={{0,4},{1,5},{2,6},{3,7},{4,0},{5,1},{6,2},{7,3},{8,12},{9,13},{10,... | collective-permute-start | bytes 3096584 | tf_op jit(solution)/shard_map/ppermute | solution.py:34
  4.4 0.7 collective-permute-start.1
  5.1 4.4 %collective-permute-start = (bf16[336,1536]{1,0:T(8,128)(2,1)S(1)}, bf16[336,1536]{1,0:T(8,128)(2,1)}, u32[]{:S(2)}, u32[]{:S(2)}) collective-permute-start(bf16[336,1536]{1,0:T(8,128)(2,1)S(1)} %pad_maximum_fusion.rest_0_.rest_3_), channel_id=1, source_target_pairs={{0,8},{1,9},{2,10},{3,11},{4,12},{5,13},{6,14},{7,15},{8,0},{9,1},... | collective-permute-start | bytes 3096584 | tf_op jit(solution)/shard_map/ppermute | solution.py:34
  9.5 0.8 fusion.1
  10.4 0.7 collective-permute-start.5
  11.0 17.1 %collective-permute-start.4 = (bf16[1,1536]{1,0:T(2,128)(2,1)S(1)}, bf16[1,1536]{1,0:T(2,128)(2,1)S(1)}, u32[]{:S(2)}, u32[]{:S(2)}) collective-permute-start(bf16[1,1536]{1,0:T(2,128)(2,1)S(1)} %get-tuple-element.86), channel_id=1, source_target_pairs={{0,2},{1,3},{2,0},{3,1},{4,6},{5,7},{6,4},{7,5},{8,10},{9,11},{10,... | collective-permute-start | bytes 9224 | tf_op jit(solution)/shard_map/ppermute | solution.py:34
  28.1 0.8 collective-permute-done.4
  28.9 0.0 collective-permute-done.2.rest_1_.rest_4_
  28.9 3.6 %collective-permute-done.rest_4_.rest_7_ = bf16[336,1536]{1,0:T(8,128)(2,1)} collective-permute-done((bf16[336,1536]{1,0:T(8,128)(2,1)S(1)}, bf16[336,1536]{1,0:T(8,128)(2,1)}, u32[]{:S(2)}, u32[]{:S(2)}) %collective-permute-start) | collective-permute-done | bytes 1032224 | tf_op jit(solution)/shard_map/ppermute | solution.py:34
  32.5 1.3 collective-permute-start.8
  33.8 0.1 collective-permute-start.9
  33.9 0.5 collective-permute-start.10
  34.4 2.1 %collective-permute-start.7 = (bf16[336,1536]{1,0:T(8,128)(2,1)}, bf16[336,1536]{1,0:T(8,128)(2,1)}, u32[]{:S(2)}, u32[]{:S(2)}) collective-permute-start(bf16[336,1536]{1,0:T(8,128)(2,1)} %collective-permute-done.rest_4_.rest_7_), channel_id=1, source_target_pairs={{0,4},{1,5},{2,6},{3,7},{4,0},{5,1},{6,2},{7,3},{8,12},{9,13},{10,... | collective-permute-start | bytes 3096584 | tf_op jit(solution)/shard_map/ppermute | solution.py:34
  36.5 0.7 collective-permute-start.6
  37.3 0.7 stack.135.place
  38.0 0.6 broadcast_in_dim.12.sep_bias
  38.6 0.6 broadcast_in_dim.13.head_bias
  39.3 0.6 broadcast_in_dim.14.pair
  39.9 0.6 broadcast_select_fusion.1
  40.5 6.8 %conv.1 = (bf16[512,1536]{1,0:T(8,128)(2,1)}, bf16[320,1536]{1,0:T(8,128)(2,1)}, bf16[192,1536]{1,0:T(8,128)(2,1)}) custom-call(bf16[256,1536]{1,0:T(8,128)(2,1)} %bitcast.42, bf16[512,1536]{1,0:T(8,128)(2,1)} %bitcast.43, bf16[1,1536]{1,0:T(2,128)(2,1)} %get-tuple-element.88.top, bf16[1,1536]{1,0:T(2,128)(2,1)} %get-tuple-element.87.bottom, f32[3,1536]{1,0:T(4,128)} %taps.1), custom_call_target="tpu_custom_call" | custom-call | flops 805306368 | bytes 4718592 | tf_op jit(solution)/shard_map/conv/pallas_call | solution.py:69
  47.3 11.4 %collective-permute-done.8 = bf16[336,1536]{1,0:T(8,128)(2,1)S(1)} collective-permute-done((bf16[336,1536]{1,0:T(8,128)(2,1)S(1)}, bf16[336,1536]{1,0:T(8,128)(2,1)S(1)}, u32[]{:S(2)}, u32[]{:S(2)}) %collective-permute-start.8) | collective-permute-done | bytes 1032224 | tf_op jit(solution)/shard_map/ppermute | solution.py:34
  58.7 1.4 collective-permute-done.7.rest_5_.rest_8_
  60.1 0.1 broadcast_select_fusion.rest_8_.rest_11_
  60.3 0.1 collective-permute-start.15
  60.3 1.8 collective-permute-start.12
  62.1 1.3 collective-permute-start.13
  63.4 0.2 collective-permute-start.14
  63.7 1.8 collective-permute-start.11
  65.5 25.6 %collective-permute-done.11.first = bf16[320,1536]{1,0:T(8,128)(2,1)S(1)} collective-permute-done((bf16[320,1536]{1,0:T(8,128)(2,1)S(1)}, bf16[320,1536]{1,0:T(8,128)(2,1)S(1)}, u32[]{:S(2)}, u32[]{:S(2)}) %collective-permute-start.11) | collective-permute-done | bytes 983072 | tf_op jit(solution)/shard_map/ppermute | solution.py:34
  91.1 15.6 %collective-permute-done.12.rest_9_.rest_12_ = bf16[336,1536]{1,0:T(8,128)(2,1)S(1)} collective-permute-done((bf16[336,1536]{1,0:T(8,128)(2,1)S(1)}, bf16[336,1536]{1,0:T(8,128)(2,1)S(1)}, u32[]{:S(2)}, u32[]{:S(2)}) %collective-permute-start.12) | collective-permute-done | bytes 1032224 | tf_op jit(solution)/shard_map/ppermute | solution.py:34
  106.6 5.2 %collective-permute-done.13 = bf16[336,1536]{1,0:T(8,128)(2,1)S(1)} collective-permute-done((bf16[336,1536]{1,0:T(8,128)(2,1)S(1)}, bf16[336,1536]{1,0:T(8,128)(2,1)S(1)}, u32[]{:S(2)}, u32[]{:S(2)}) %collective-permute-start.13) | collective-permute-done | bytes 1032224 | tf_op jit(solution)/shard_map/ppermute | solution.py:34
  111.8 0.1 collective-permute-start.20
  112.0 0.6 collective-permute-start.21
  112.5 1.7 collective-permute-start.16
  114.3 0.1 slice_select_fusion.rest_19_
  114.4 7.2 %collective-permute-done.16.rest_13_.rest_16_ = bf16[96,1536]{1,0:T(8,128)(2,1)S(1)} collective-permute-done((bf16[96,1536]{1,0:T(8,128)(2,1)S(1)}, bf16[96,1536]{1,0:T(8,128)(2,1)S(1)}, u32[]{:S(2)}, u32[]{:S(2)}) %collective-permute-start.16) | collective-permute-done | bytes 294944 | tf_op jit(solution)/shard_map/ppermute | solution.py:34
  121.5 0.5 collective-permute-start.19
  122.0 1.7 collective-permute-start.18
  123.8 0.7 collective-permute-start.17
  124.5 0.7 copy-done.19
  125.3 1.0 copy-done.10
  126.3 20.4 %early.1 = (bf16[832,1536]{1,0:T(8,128)(2,1)}, bf16[832,1920]{1,0:T(8,128)(2,1)}) custom-call(s32[33]{0:T(128)} %stack.135.place, f32[1,1536]{1,0:T(1,128)} %broadcast_in_dim.12.sep_bias, f32[1,3840]{1,0:T(1,128)} %broadcast_in_dim.13.head_bias, bf16[512,1536]{1,0:T(8,128)(2,1)} %get-tuple-element.69.own_values, bf16[320,1536]{1,0:T(8,128)(2,1)} %copy-done.11, ...), custom_call_target="tpu_custom_call" | custom-call | flops 8833204224 | bytes 9437184 | tf_op jit(solution)/shard_map/early/pallas_call | solution.py:157
  146.7 6.3 %collective-permute-done.18.rest_20_ = bf16[240,1536]{1,0:T(8,128)(2,1)S(1)} collective-permute-done((bf16[240,1536]{1,0:T(8,128)(2,1)S(1)}, bf16[240,1536]{1,0:T(8,128)(2,1)S(1)}, u32[]{:S(2)}, u32[]{:S(2)}) %collective-permute-start.18) | collective-permute-done | bytes 737312 | tf_op jit(solution)/shard_map/ppermute | solution.py:34
  153.1 2.2 %collective-permute-done.23.rest_22_ = bf16[240,1536]{1,0:T(8,128)(2,1)S(1)} collective-permute-done((bf16[240,1536]{1,0:T(8,128)(2,1)S(1)}, bf16[240,1536]{1,0:T(8,128)(2,1)S(1)}, u32[]{:S(2)}, u32[]{:S(2)}) %collective-permute-start.23) | collective-permute-done | bytes 737312 | tf_op jit(solution)/shard_map/ppermute | solution.py:34
  155.3 0.9 copy-done.15
  156.2 37.8 %finish.1 = bf16[512,3840]{1,0:T(8,128)(2,1)} custom-call(s32[33]{0:T(128)} %stack.135.place, f32[1,1536]{1,0:T(1,128)} %broadcast_in_dim.12.sep_bias, f32[1,3840]{1,0:T(1,128)} %broadcast_in_dim.13.head_bias, s32[1,3840]{1,0:T(1,128)} %broadcast_in_dim.14.pair, bf16[832,1536]{1,0:T(8,128)(2,1)} %get-tuple-element.80.rest_0_, bf16[192,1536]{1,0:T(8,128)(2,1)} %copy-done.16, ...), custom_call_target="tpu_custom_call" | custom-call | flops 60397977600 | bytes 31457280 | tf_op jit(solution)/shard_map/finish/pallas_call | solution.py:295
  (53 shorter events, 0.1 us)
Async XLA Ops:
  0.0 39.3 %copy-start.5 = (s32[3840]{0:T(1024)S(1)}, s32[3840]{0:T(1024)}, u32[]{:S(2)}) copy-start(s32[3840]{0:T(1024)} %param.15) | copy-start | bytes 46084
  0.0 38.6 %copy-start.4 = (f32[3840]{0:T(1024)S(1)}, f32[3840]{0:T(1024)}, u32[]{:S(2)}) copy-start(f32[3840]{0:T(1024)} %param.14) | copy-start | bytes 46084
  0.0 38.0 %copy-start.6 = (f32[1536]{0:T(1024)S(1)}, f32[1536]{0:T(1024)}, u32[]{:S(2)}) copy-start(f32[1536]{0:T(1024)} %param.12) | copy-start | bytes 18436
  1.3 33.1 %copy-start.1 = (bf16[336,1536]{1,0:T(8,128)(2,1)}, bf16[336,1536]{1,0:T(8,128)(2,1)S(1)}, u32[]{:S(2)}) copy-start(bf16[336,1536]{1,0:T(8,128)(2,1)S(1)} %pad_maximum_fusion.rest_0_.rest_3_) | copy-start | bytes 3096580
  1.3 27.6 %collective-permute-start.3 = (bf16[336,1536]{1,0:T(8,128)(2,1)S(1)}, bf16[336,1536]{1,0:T(8,128)(2,1)}, u32[]{:S(2)}, u32[]{:S(2)}) collective-permute-start(bf16[336,1536]{1,0:T(8,128)(2,1)S(1)} %pad_maximum_fusion.rest_0_.rest_3_), channel_id=1, source_target_pairs={{0,2},{1,3},{2,0},{3,1},{4,6},{5,7},{6,4},{7,5},{8,10},{9,11},{10,... | collective-permute-start | bytes 3096584 | tf_op jit(solution)/shard_map/ppermute | solution.py:34
  1.8 27.1 %collective-permute-start.2 = (bf16[336,1536]{1,0:T(8,128)(2,1)S(1)}, bf16[336,1536]{1,0:T(8,128)(2,1)}, u32[]{:S(2)}, u32[]{:S(2)}) collective-permute-start(bf16[336,1536]{1,0:T(8,128)(2,1)S(1)} %pad_maximum_fusion.rest_0_.rest_3_), channel_id=1, source_target_pairs={{0,4},{1,5},{2,6},{3,7},{4,0},{5,1},{6,2},{7,3},{8,12},{9,13},{10,... | collective-permute-start | bytes 3096584 | tf_op jit(solution)/shard_map/ppermute | solution.py:34
  4.4 24.5 %collective-permute-start.1 = (bf16[336,1536]{1,0:T(8,128)(2,1)S(1)}, bf16[336,1536]{1,0:T(8,128)(2,1)S(1)}, u32[]{:S(2)}, u32[]{:S(2)}) collective-permute-start(bf16[336,1536]{1,0:T(8,128)(2,1)S(1)} %pad_maximum_fusion.rest_0_.rest_3_), channel_id=1, source_target_pairs={{8,16},{9,17},{10,18},{11,19},{12,20},{13,21},{14,22},{15,23},{16,... | collective-permute-start | bytes 3096584 | tf_op jit(solution)/shard_map/ppermute | solution.py:34
  5.1 27.4 %collective-permute-start = (bf16[336,1536]{1,0:T(8,128)(2,1)S(1)}, bf16[336,1536]{1,0:T(8,128)(2,1)}, u32[]{:S(2)}, u32[]{:S(2)}) collective-permute-start(bf16[336,1536]{1,0:T(8,128)(2,1)S(1)} %pad_maximum_fusion.rest_0_.rest_3_), channel_id=1, source_target_pairs={{0,8},{1,9},{2,10},{3,11},{4,12},{5,13},{6,14},{7,15},{8,0},{9,1},... | collective-permute-start | bytes 3096584 | tf_op jit(solution)/shard_map/ppermute | solution.py:34
  10.4 0.7 collective-permute-start.5
  11.0 17.9 %collective-permute-start.4 = (bf16[1,1536]{1,0:T(2,128)(2,1)S(1)}, bf16[1,1536]{1,0:T(2,128)(2,1)S(1)}, u32[]{:S(2)}, u32[]{:S(2)}) collective-permute-start(bf16[1,1536]{1,0:T(2,128)(2,1)S(1)} %get-tuple-element.86), channel_id=1, source_target_pairs={{0,2},{1,3},{2,0},{3,1},{4,6},{5,7},{6,4},{7,5},{8,10},{9,11},{10,... | collective-permute-start | bytes 9224 | tf_op jit(solution)/shard_map/ppermute | solution.py:34
  32.5 26.2 %collective-permute-start.8 = (bf16[336,1536]{1,0:T(8,128)(2,1)S(1)}, bf16[336,1536]{1,0:T(8,128)(2,1)S(1)}, u32[]{:S(2)}, u32[]{:S(2)}) collective-permute-start(bf16[336,1536]{1,0:T(8,128)(2,1)S(1)} %collective-permute-done.1), channel_id=1, source_target_pairs={{8,0},{9,1},{10,2},{11,3},{12,4},{13,5},{14,6},{15,7},{16,24},{17,... | collective-permute-start | bytes 3096584 | tf_op jit(solution)/shard_map/ppermute | solution.py:34
  33.8 24.9 %collective-permute-start.9 = (bf16[336,1536]{1,0:T(8,128)(2,1)}, bf16[336,1536]{1,0:T(8,128)(2,1)}, u32[]{:S(2)}, u32[]{:S(2)}) collective-permute-start(bf16[336,1536]{1,0:T(8,128)(2,1)} %collective-permute-done.2.rest_1_.rest_4_), channel_id=1, source_target_pairs={{0,2},{1,3},{2,0},{3,1},{4,6},{5,7},{6,4},{7,5},{8,10},{9,11},{10,... | collective-permute-start | bytes 3096584 | tf_op jit(solution)/shard_map/ppermute | solution.py:34
  33.9 24.9 %collective-permute-start.10 = (bf16[336,1536]{1,0:T(8,128)(2,1)}, bf16[336,1536]{1,0:T(8,128)(2,1)}, u32[]{:S(2)}, u32[]{:S(2)}) collective-permute-start(bf16[336,1536]{1,0:T(8,128)(2,1)} %collective-permute-done.rest_4_.rest_7_), channel_id=1, source_target_pairs={{0,2},{1,3},{2,0},{3,1},{4,6},{5,7},{6,4},{7,5},{8,10},{9,11},{10,... | collective-permute-start | bytes 3096584 | tf_op jit(solution)/shard_map/ppermute | solution.py:34
  34.4 25.7 %collective-permute-start.7 = (bf16[336,1536]{1,0:T(8,128)(2,1)}, bf16[336,1536]{1,0:T(8,128)(2,1)}, u32[]{:S(2)}, u32[]{:S(2)}) collective-permute-start(bf16[336,1536]{1,0:T(8,128)(2,1)} %collective-permute-done.rest_4_.rest_7_), channel_id=1, source_target_pairs={{0,4},{1,5},{2,6},{3,7},{4,0},{5,1},{6,2},{7,3},{8,12},{9,13},{10,... | collective-permute-start | bytes 3096584 | tf_op jit(solution)/shard_map/ppermute | solution.py:34
  36.5 23.6 %collective-permute-start.6 = (bf16[336,1536]{1,0:T(8,128)(2,1)}, bf16[336,1536]{1,0:T(8,128)(2,1)S(1)}, u32[]{:S(2)}, u32[]{:S(2)}) collective-permute-start(bf16[336,1536]{1,0:T(8,128)(2,1)} %collective-permute-done.rest_4_.rest_7_), channel_id=1, source_target_pairs={{8,16},{9,17},{10,18},{11,19},{12,20},{13,21},{14,22},{15,23},{16,... | collective-permute-start | bytes 3096584 | tf_op jit(solution)/shard_map/ppermute | solution.py:34
  47.3 16.4 %copy-start.12 = (bf16[320,1536]{1,0:T(8,128)(2,1)S(1)}, bf16[320,1536]{1,0:T(8,128)(2,1)}, u32[]{:S(2)}) copy-start(bf16[320,1536]{1,0:T(8,128)(2,1)} %get-tuple-element.61) | copy-start | bytes 2949124
  60.2 65.0 %copy-start = (bf16[336,1536]{1,0:T(8,128)(2,1)}, bf16[336,1536]{1,0:T(8,128)(2,1)S(1)}, u32[]{:S(2)}) copy-start(bf16[336,1536]{1,0:T(8,128)(2,1)S(1)} %broadcast_select_fusion.rest_8_.rest_11_) | copy-start | bytes 3096580
  60.3 30.8 %collective-permute-start.15 = (bf16[336,1536]{1,0:T(8,128)(2,1)S(1)}, bf16[336,1536]{1,0:T(8,128)(2,1)S(1)}, u32[]{:S(2)}, u32[]{:S(2)}) collective-permute-start(bf16[336,1536]{1,0:T(8,128)(2,1)S(1)} %broadcast_select_fusion.rest_8_.rest_11_), channel_id=1, source_target_pairs={{0,2},{1,3},{2,0},{3,1},{4,6},{5,7},{6,4},{7,5},{8,10},{9,11},{10,... | collective-permute-start | bytes 3096584 | tf_op jit(solution)/shard_map/ppermute | solution.py:34
  60.3 46.3 %collective-permute-start.12 = (bf16[336,1536]{1,0:T(8,128)(2,1)S(1)}, bf16[336,1536]{1,0:T(8,128)(2,1)S(1)}, u32[]{:S(2)}, u32[]{:S(2)}) collective-permute-start(bf16[336,1536]{1,0:T(8,128)(2,1)S(1)} %broadcast_select_fusion.rest_8_.rest_11_), channel_id=1, source_target_pairs={{0,4},{1,5},{2,6},{3,7},{4,0},{5,1},{6,2},{7,3},{8,12},{9,13},{10,... | collective-permute-start | bytes 3096584 | tf_op jit(solution)/shard_map/ppermute | solution.py:34
  62.1 49.7 %collective-permute-start.13 = (bf16[336,1536]{1,0:T(8,128)(2,1)S(1)}, bf16[336,1536]{1,0:T(8,128)(2,1)S(1)}, u32[]{:S(2)}, u32[]{:S(2)}) collective-permute-start(bf16[336,1536]{1,0:T(8,128)(2,1)S(1)} %collective-permute-done.6), channel_id=1, source_target_pairs={{8,0},{9,1},{10,2},{11,3},{12,4},{13,5},{14,6},{15,7},{16,24},{17,... | collective-permute-start | bytes 3096584 | tf_op jit(solution)/shard_map/ppermute | solution.py:34
  63.4 48.4 %collective-permute-start.14 = (bf16[336,1536]{1,0:T(8,128)(2,1)}, bf16[336,1536]{1,0:T(8,128)(2,1)S(1)}, u32[]{:S(2)}, u32[]{:S(2)}) collective-permute-start(bf16[336,1536]{1,0:T(8,128)(2,1)} %collective-permute-done.7.rest_5_.rest_8_), channel_id=1, source_target_pairs={{0,2},{1,3},{2,0},{3,1},{4,6},{5,7},{6,4},{7,5},{8,10},{9,11},{10,... | collective-permute-start | bytes 3096584 | tf_op jit(solution)/shard_map/ppermute | solution.py:34
  63.7 27.4 %collective-permute-start.11 = (bf16[320,1536]{1,0:T(8,128)(2,1)S(1)}, bf16[320,1536]{1,0:T(8,128)(2,1)S(1)}, u32[]{:S(2)}, u32[]{:S(2)}) collective-permute-start(bf16[320,1536]{1,0:T(8,128)(2,1)S(1)} %copy-done.12), channel_id=1, source_target_pairs={{0,31},{1,30},{2,29},{3,28},{4,27},{5,26},{6,25},{7,24},{8,23},{9,... | collective-permute-start | bytes 2949128 | tf_op jit(solution)/shard_map/ppermute | solution.py:34
  91.1 20.8 %copy-start.11 = (bf16[320,1536]{1,0:T(8,128)(2,1)}, bf16[320,1536]{1,0:T(8,128)(2,1)S(1)}, u32[]{:S(2)}) copy-start(bf16[320,1536]{1,0:T(8,128)(2,1)S(1)} %collective-permute-done.11.first) | copy-start | bytes 2949124
  91.1 34.2 %copy-start.7 = (bf16[336,1536]{1,0:T(8,128)(2,1)}, bf16[336,1536]{1,0:T(8,128)(2,1)S(1)}, u32[]{:S(2)}) copy-start(bf16[336,1536]{1,0:T(8,128)(2,1)S(1)} %collective-permute-done.15.rest_10_.rest_13_) | copy-start | bytes 3096580
  106.6 18.6 %copy-start.8 = (bf16[336,1536]{1,0:T(8,128)(2,1)}, bf16[336,1536]{1,0:T(8,128)(2,1)S(1)}, u32[]{:S(2)}) copy-start(bf16[336,1536]{1,0:T(8,128)(2,1)S(1)} %collective-permute-done.12.rest_9_.rest_12_) | copy-start | bytes 3096580
  111.8 13.4 %copy-start.9 = (bf16[336,1536]{1,0:T(8,128)(2,1)}, bf16[336,1536]{1,0:T(8,128)(2,1)S(1)}, u32[]{:S(2)}) copy-start(bf16[336,1536]{1,0:T(8,128)(2,1)S(1)} %collective-permute-done.14.rest_7_.rest_10_) | copy-start | bytes 3096580
  111.8 13.4 %collective-permute-start.20 = (bf16[336,1536]{1,0:T(8,128)(2,1)S(1)}, bf16[336,1536]{1,0:T(8,128)(2,1)S(1)}, u32[]{:S(2)}, u32[]{:S(2)}) collective-permute-start(bf16[336,1536]{1,0:T(8,128)(2,1)S(1)} %collective-permute-done.12.rest_9_.rest_12_), channel_id=1, source_target_pairs={{0,2},{1,3},{2,0},{3,1},{4,6},{5,7},{6,4},{7,5},{8,10},{9,11},{10,... | collective-permute-start | bytes 3096584 | tf_op jit(solution)/shard_map/ppermute | solution.py:34
  112.0 13.3 %copy-start.3 = (bf16[96,1536]{1,0:T(8,128)(2,1)}, bf16[96,1536]{1,0:T(8,128)(2,1)S(1)}, u32[]{:S(2)}) copy-start(bf16[96,1536]{1,0:T(8,128)(2,1)S(1)} %slice_select_fusion.1.rest_12_.rest_15_) | copy-start | bytes 884740
  112.0 11.8 %collective-permute-start.21 = (bf16[96,1536]{1,0:T(8,128)(2,1)S(1)}, bf16[96,1536]{1,0:T(8,128)(2,1)S(1)}, u32[]{:S(2)}, u32[]{:S(2)}) collective-permute-start(bf16[96,1536]{1,0:T(8,128)(2,1)S(1)} %slice_select_fusion.1.rest_12_.rest_15_), channel_id=1, source_target_pairs={{0,2},{1,3},{2,0},{3,1},{4,6},{5,7},{6,4},{7,5},{8,10},{9,11},{10,... | collective-permute-start | bytes 884744 | tf_op jit(solution)/shard_map/ppermute | solution.py:34
  112.5 9.0 %collective-permute-start.16 = (bf16[96,1536]{1,0:T(8,128)(2,1)S(1)}, bf16[96,1536]{1,0:T(8,128)(2,1)S(1)}, u32[]{:S(2)}, u32[]{:S(2)}) collective-permute-start(bf16[96,1536]{1,0:T(8,128)(2,1)S(1)} %slice_select_fusion.1.rest_12_.rest_15_), channel_id=1, source_target_pairs={{0,4},{1,5},{2,6},{3,7},{4,0},{5,1},{6,2},{7,3},{8,12},{9,13},{10,... | collective-permute-start | bytes 884744 | tf_op jit(solution)/shard_map/ppermute | solution.py:34
  114.3 32.3 %copy-start.2 = (bf16[240,1536]{1,0:T(8,128)(2,1)}, bf16[240,1536]{1,0:T(8,128)(2,1)S(1)}, u32[]{:S(2)}) copy-start(bf16[240,1536]{1,0:T(8,128)(2,1)S(1)} %slice_select_fusion.rest_19_) | copy-start | bytes 2211844
  121.5 3.0 %copy-start.18 = (bf16[96,1536]{1,0:T(8,128)(2,1)}, bf16[96,1536]{1,0:T(8,128)(2,1)S(1)}, u32[]{:S(2)}) copy-start(bf16[96,1536]{1,0:T(8,128)(2,1)S(1)} %collective-permute-done.16.rest_13_.rest_16_) | copy-start | bytes 884740
  121.5 3.0 %collective-permute-start.22 = (bf16[96,1536]{1,0:T(8,128)(2,1)S(1)}, bf16[96,1536]{1,0:T(8,128)(2,1)S(1)}, u32[]{:S(2)}, u32[]{:S(2)}) collective-permute-start(bf16[96,1536]{1,0:T(8,128)(2,1)S(1)} %collective-permute-done.16.rest_13_.rest_16_), channel_id=1, source_target_pairs={{0,2},{1,3},{2,0},{3,1},{4,6},{5,7},{6,4},{7,5},{8,10},{9,11},{10,... | collective-permute-start | bytes 884744 | tf_op jit(solution)/shard_map/ppermute | solution.py:34
  121.5 25.2 %collective-permute-start.19 = (bf16[240,1536]{1,0:T(8,128)(2,1)S(1)}, bf16[240,1536]{1,0:T(8,128)(2,1)S(1)}, u32[]{:S(2)}, u32[]{:S(2)}) collective-permute-start(bf16[240,1536]{1,0:T(8,128)(2,1)S(1)} %slice_select_fusion.rest_19_), channel_id=1, source_target_pairs={{0,2},{1,3},{2,0},{3,1},{4,6},{5,7},{6,4},{7,5},{8,10},{9,11},{10,... | collective-permute-start | bytes 2211848 | tf_op jit(solution)/shard_map/ppermute | solution.py:34
  122.0 31.0 %collective-permute-start.18 = (bf16[240,1536]{1,0:T(8,128)(2,1)S(1)}, bf16[240,1536]{1,0:T(8,128)(2,1)S(1)}, u32[]{:S(2)}, u32[]{:S(2)}) collective-permute-start(bf16[240,1536]{1,0:T(8,128)(2,1)S(1)} %slice_select_fusion.rest_19_), channel_id=1, source_target_pairs={{0,4},{1,5},{2,6},{3,7},{4,0},{5,1},{6,2},{7,3},{8,12},{9,13},{10,... | collective-permute-start | bytes 2211848 | tf_op jit(solution)/shard_map/ppermute | solution.py:34
  123.8 0.7 copy-start.17
  123.8 22.9 %collective-permute-start.17 = (bf16[192,1536]{1,0:T(8,128)(2,1)}, bf16[192,1536]{1,0:T(8,128)(2,1)S(1)}, u32[]{:S(2)}, u32[]{:S(2)}) collective-permute-start(bf16[192,1536]{1,0:T(8,128)(2,1)} %get-tuple-element.67), channel_id=1, source_target_pairs={{0,31},{1,30},{2,29},{3,28},{4,27},{5,26},{6,25},{7,24},{8,23},{9,... | collective-permute-start | bytes 1769480 | tf_op jit(solution)/shard_map/ppermute | solution.py:34
  124.5 0.7 copy-start.19
  125.3 1.0 copy-start.10
  146.7 8.6 %copy-start.16 = (bf16[192,1536]{1,0:T(8,128)(2,1)}, bf16[192,1536]{1,0:T(8,128)(2,1)S(1)}, u32[]{:S(2)}) copy-start(bf16[192,1536]{1,0:T(8,128)(2,1)S(1)} %collective-permute-done.17.rest_1_) | copy-start | bytes 1769476
  146.7 8.6 %copy-start.13 = (bf16[240,1536]{1,0:T(8,128)(2,1)}, bf16[240,1536]{1,0:T(8,128)(2,1)S(1)}, u32[]{:S(2)}) copy-start(bf16[240,1536]{1,0:T(8,128)(2,1)S(1)} %collective-permute-done.19.rest_21_) | copy-start | bytes 2211844
  153.1 2.2 %copy-start.14 = (bf16[240,1536]{1,0:T(8,128)(2,1)}, bf16[240,1536]{1,0:T(8,128)(2,1)S(1)}, u32[]{:S(2)}) copy-start(bf16[240,1536]{1,0:T(8,128)(2,1)S(1)} %collective-permute-done.18.rest_20_) | copy-start | bytes 2211844
  153.1 2.2 %collective-permute-start.23 = (bf16[240,1536]{1,0:T(8,128)(2,1)S(1)}, bf16[240,1536]{1,0:T(8,128)(2,1)S(1)}, u32[]{:S(2)}, u32[]{:S(2)}) collective-permute-start(bf16[240,1536]{1,0:T(8,128)(2,1)S(1)} %collective-permute-done.18.rest_20_), channel_id=1, source_target_pairs={{0,2},{1,3},{2,0},{3,1},{4,6},{5,7},{6,4},{7,5},{8,10},{9,11},{10,... | collective-permute-start | bytes 2211848 | tf_op jit(solution)/shard_map/ppermute | solution.py:34
  155.3 0.9 copy-start.15

commit v6 on v5

--- a/solution.py
+++ b/solution.py
@@ -220,14 +220,24 @@
             jnp.bfloat16
         )
 
-    step = 384
     for copy in near_copies:
         copy.wait()
 
-    @pl.loop(0, half_tracks // step)
-    def _(j):
-        columns = columns_of(j, step)
-        target = pl.ds(pl.multiple_of(near_start + j * step, 128), step)
+    def in_blocks(body):
+        step = 256
+        full = half_tracks // step
+
+        @pl.loop(0, full)
+        def _(j):
+            body(pl.multiple_of(j * step, step), step)
+
+        if half_tracks % step:
+            body(full * step, half_tracks % step)
+
+    @in_blocks
+    def _(start, size):
+        columns = pl.ds(start, size)
+        target = pl.ds(pl.multiple_of(near_start + start, 128), size)
         product = rows_by_rows(values[bins + part :, :], near[columns, :])
         other[part:, target] = softplus(product + head_bias[:, target]).astype(jnp.bfloat16)
 
@@ -235,10 +245,10 @@
     for copy in far_copies:
         copy.wait()
 
-    @pl.loop(0, half_tracks // step)
-    def _(j):
-        columns = columns_of(j, step)
-        target = pl.ds(pl.multiple_of(far_start + j * step, 128), step)
+    @in_blocks
+    def _(start, size):
+        columns = pl.ds(start, size)
+        target = pl.ds(pl.multiple_of(far_start + start, 128), size)
         product = rows_by_rows(values[...], far[columns, :])
         heads = softplus(product + head_bias[:, target]).astype(jnp.bfloat16)
         own[:, target] = heads[:bins]

time: 194 us -> 194 us (level)
  no operation moved by 1% of the time
where the time goes in v6:
time: 194 us; the launch traced here: 193 us
  waiting for transfers between devices  79.3 us (41%)
  Pallas kernels  64 us (33%)
  starting transfers between devices  41.2 us (21%)
  local copies, waits for them, and re-layouts  5.2 us (3%)
  other arithmetic  2.98 us (2%)
    ppermute x24, waiting for transfers between devices, send(): return lax.ppermute(array, BOTH, route(seq, batch, move))  79.3 us
    ppermute x24, starting transfers between devices, send(): return lax.ppermute(array, BOTH, route(seq, batch, move))  41.2 us
    pallas_call x1, Pallas kernels, finish(): pl.pallas_call(functools.partial(finish_kernel, sep_blocks, near_blocks,...  36.8 us
    pallas_call x1, Pallas kernels, early(): pl.pallas_call(functools.partial(early_kernel, sep_blocks, near_blocks),...  20.4 us
    pallas_call x1, Pallas kernels, conv(): pl.pallas_call(conv_kernel, grid=(width // step,), in_specs=[column(coars...  6.79 us
  transfers between devices with their start and end apart: 24, of which 10 were waited for; matrix products, arithmetic and copies ran while one was open for 2% of the time, Pallas kernels for 14%

profile of v6, /device:TPU:0, one launch (start us, length us, event | category | flops | bytes accessed | tf_op | source)
XLA Modules:
  0.0 193.0 jit_solution(13499915606266469783)
XLA Ops:
  0.0 1.3 pad_maximum_fusion.rest_0_.rest_3_
  1.3 0.5 collective-permute-start.3
  1.8 2.6 %collective-permute-start.2 = (bf16[336,1536]{1,0:T(8,128)(2,1)S(1)}, bf16[336,1536]{1,0:T(8,128)(2,1)}, u32[]{:S(2)}, u32[]{:S(2)}) collective-permute-start(bf16[336,1536]{1,0:T(8,128)(2,1)S(1)} %pad_maximum_fusion.rest_0_.rest_3_), channel_id=1, source_target_pairs={{0,4},{1,5},{2,6},{3,7},{4,0},{5,1},{6,2},{7,3},{8,12},{9,13},{10,... | collective-permute-start | bytes 3096584 | tf_op jit(solution)/shard_map/ppermute | solution.py:34
  4.4 0.7 collective-permute-start.1
  5.1 4.4 %collective-permute-start = (bf16[336,1536]{1,0:T(8,128)(2,1)S(1)}, bf16[336,1536]{1,0:T(8,128)(2,1)}, u32[]{:S(2)}, u32[]{:S(2)}) collective-permute-start(bf16[336,1536]{1,0:T(8,128)(2,1)S(1)} %pad_maximum_fusion.rest_0_.rest_3_), channel_id=1, source_target_pairs={{0,8},{1,9},{2,10},{3,11},{4,12},{5,13},{6,14},{7,15},{8,0},{9,1},... | collective-permute-start | bytes 3096584 | tf_op jit(solution)/shard_map/ppermute | solution.py:34
  9.5 0.8 fusion.1
  10.4 0.7 collective-permute-start.5
  11.0 17.1 %collective-permute-start.4 = (bf16[1,1536]{1,0:T(2,128)(2,1)S(1)}, bf16[1,1536]{1,0:T(2,128)(2,1)S(1)}, u32[]{:S(2)}, u32[]{:S(2)}) collective-permute-start(bf16[1,1536]{1,0:T(2,128)(2,1)S(1)} %get-tuple-element.86), channel_id=1, source_target_pairs={{0,2},{1,3},{2,0},{3,1},{4,6},{5,7},{6,4},{7,5},{8,10},{9,11},{10,... | collective-permute-start | bytes 9224 | tf_op jit(solution)/shard_map/ppermute | solution.py:34
  28.1 0.8 collective-permute-done.4
  28.9 0.0 collective-permute-done.2.rest_1_.rest_4_
  28.9 3.6 %collective-permute-done.rest_4_.rest_7_ = bf16[336,1536]{1,0:T(8,128)(2,1)} collective-permute-done((bf16[336,1536]{1,0:T(8,128)(2,1)S(1)}, bf16[336,1536]{1,0:T(8,128)(2,1)}, u32[]{:S(2)}, u32[]{:S(2)}) %collective-permute-start) | collective-permute-done | bytes 1032224 | tf_op jit(solution)/shard_map/ppermute | solution.py:34
  32.5 1.3 collective-permute-start.8
  33.8 0.1 collective-permute-start.9
  33.9 0.5 collective-permute-start.10
  34.4 2.1 %collective-permute-start.7 = (bf16[336,1536]{1,0:T(8,128)(2,1)}, bf16[336,1536]{1,0:T(8,128)(2,1)}, u32[]{:S(2)}, u32[]{:S(2)}) collective-permute-start(bf16[336,1536]{1,0:T(8,128)(2,1)} %collective-permute-done.rest_4_.rest_7_), channel_id=1, source_target_pairs={{0,4},{1,5},{2,6},{3,7},{4,0},{5,1},{6,2},{7,3},{8,12},{9,13},{10,... | collective-permute-start | bytes 3096584 | tf_op jit(solution)/shard_map/ppermute | solution.py:34
  36.5 0.7 collective-permute-start.6
  37.3 0.7 stack.135.place
  38.0 0.6 broadcast_in_dim.12.sep_bias
  38.6 0.6 broadcast_in_dim.13.head_bias
  39.3 0.6 broadcast_in_dim.14.pair
  39.9 0.6 broadcast_select_fusion.1
  40.5 6.8 %conv.1 = (bf16[512,1536]{1,0:T(8,128)(2,1)}, bf16[320,1536]{1,0:T(8,128)(2,1)}, bf16[192,1536]{1,0:T(8,128)(2,1)}) custom-call(bf16[256,1536]{1,0:T(8,128)(2,1)} %bitcast.42, bf16[512,1536]{1,0:T(8,128)(2,1)} %bitcast.43, bf16[1,1536]{1,0:T(2,128)(2,1)} %get-tuple-element.88.top, bf16[1,1536]{1,0:T(2,128)(2,1)} %get-tuple-element.87.bottom, f32[3,1536]{1,0:T(4,128)} %taps.1), custom_call_target="tpu_custom_call" | custom-call | flops 805306368 | bytes 4718592 | tf_op jit(solution)/shard_map/conv/pallas_call | solution.py:69
  47.3 11.4 %collective-permute-done.8 = bf16[336,1536]{1,0:T(8,128)(2,1)S(1)} collective-permute-done((bf16[336,1536]{1,0:T(8,128)(2,1)S(1)}, bf16[336,1536]{1,0:T(8,128)(2,1)S(1)}, u32[]{:S(2)}, u32[]{:S(2)}) %collective-permute-start.8) | collective-permute-done | bytes 1032224 | tf_op jit(solution)/shard_map/ppermute | solution.py:34
  58.7 1.4 collective-permute-done.7.rest_5_.rest_8_
  60.1 0.1 broadcast_select_fusion.rest_8_.rest_11_
  60.3 0.1 collective-permute-start.15
  60.3 1.8 collective-permute-start.12
  62.1 1.3 collective-permute-start.13
  63.4 0.2 collective-permute-start.14
  63.7 1.8 collective-permute-start.11
  65.5 25.6 %collective-permute-done.11.first = bf16[320,1536]{1,0:T(8,128)(2,1)S(1)} collective-permute-done((bf16[320,1536]{1,0:T(8,128)(2,1)S(1)}, bf16[320,1536]{1,0:T(8,128)(2,1)S(1)}, u32[]{:S(2)}, u32[]{:S(2)}) %collective-permute-start.11) | collective-permute-done | bytes 983072 | tf_op jit(solution)/shard_map/ppermute | solution.py:34
  91.1 15.6 %collective-permute-done.12.rest_9_.rest_12_ = bf16[336,1536]{1,0:T(8,128)(2,1)S(1)} collective-permute-done((bf16[336,1536]{1,0:T(8,128)(2,1)S(1)}, bf16[336,1536]{1,0:T(8,128)(2,1)S(1)}, u32[]{:S(2)}, u32[]{:S(2)}) %collective-permute-start.12) | collective-permute-done | bytes 1032224 | tf_op jit(solution)/shard_map/ppermute | solution.py:34
  106.6 5.2 %collective-permute-done.13 = bf16[336,1536]{1,0:T(8,128)(2,1)S(1)} collective-permute-done((bf16[336,1536]{1,0:T(8,128)(2,1)S(1)}, bf16[336,1536]{1,0:T(8,128)(2,1)S(1)}, u32[]{:S(2)}, u32[]{:S(2)}) %collective-permute-start.13) | collective-permute-done | bytes 1032224 | tf_op jit(solution)/shard_map/ppermute | solution.py:34
  111.8 0.1 collective-permute-start.20
  112.0 0.6 collective-permute-start.21
  112.5 1.7 collective-permute-start.16
  114.3 0.1 slice_select_fusion.rest_19_
  114.4 7.2 %collective-permute-done.16.rest_13_.rest_16_ = bf16[96,1536]{1,0:T(8,128)(2,1)S(1)} collective-permute-done((bf16[96,1536]{1,0:T(8,128)(2,1)S(1)}, bf16[96,1536]{1,0:T(8,128)(2,1)S(1)}, u32[]{:S(2)}, u32[]{:S(2)}) %collective-permute-start.16) | collective-permute-done | bytes 294944 | tf_op jit(solution)/shard_map/ppermute | solution.py:34
  121.5 0.5 collective-permute-start.19
  122.0 1.7 collective-permute-start.18
  123.8 0.7 collective-permute-start.17
  124.5 0.7 copy-done.19
  125.3 1.0 copy-done.10
  126.3 20.4 %early.1 = (bf16[832,1536]{1,0:T(8,128)(2,1)}, bf16[832,1920]{1,0:T(8,128)(2,1)}) custom-call(s32[33]{0:T(128)} %stack.135.place, f32[1,1536]{1,0:T(1,128)} %broadcast_in_dim.12.sep_bias, f32[1,3840]{1,0:T(1,128)} %broadcast_in_dim.13.head_bias, bf16[512,1536]{1,0:T(8,128)(2,1)} %get-tuple-element.69.own_values, bf16[320,1536]{1,0:T(8,128)(2,1)} %copy-done.11, ...), custom_call_target="tpu_custom_call" | custom-call | flops 8833204224 | bytes 9437184 | tf_op jit(solution)/shard_map/early/pallas_call | solution.py:157
  146.7 6.3 %collective-permute-done.18.rest_20_ = bf16[240,1536]{1,0:T(8,128)(2,1)S(1)} collective-permute-done((bf16[240,1536]{1,0:T(8,128)(2,1)S(1)}, bf16[240,1536]{1,0:T(8,128)(2,1)S(1)}, u32[]{:S(2)}, u32[]{:S(2)}) %collective-permute-start.18) | collective-permute-done | bytes 737312 | tf_op jit(solution)/shard_map/ppermute | solution.py:34
  153.1 2.2 %collective-permute-done.23.rest_22_ = bf16[240,1536]{1,0:T(8,128)(2,1)S(1)} collective-permute-done((bf16[240,1536]{1,0:T(8,128)(2,1)S(1)}, bf16[240,1536]{1,0:T(8,128)(2,1)S(1)}, u32[]{:S(2)}, u32[]{:S(2)}) %collective-permute-start.23) | collective-permute-done | bytes 737312 | tf_op jit(solution)/shard_map/ppermute | solution.py:34
  155.3 0.9 copy-done.15
  156.2 36.8 %finish.1 = bf16[512,3840]{1,0:T(8,128)(2,1)} custom-call(s32[33]{0:T(128)} %stack.135.place, f32[1,1536]{1,0:T(1,128)} %broadcast_in_dim.12.sep_bias, f32[1,3840]{1,0:T(1,128)} %broadcast_in_dim.13.head_bias, s32[1,3840]{1,0:T(1,128)} %broadcast_in_dim.14.pair, bf16[832,1536]{1,0:T(8,128)(2,1)} %get-tuple-element.80.rest_0_, bf16[192,1536]{1,0:T(8,128)(2,1)} %copy-done.16, ...), custom_call_target="tpu_custom_call" | custom-call | flops 60397977600 | bytes 31457280 | tf_op jit(solution)/shard_map/finish/pallas_call | solution.py:305
  (53 shorter events, 0.1 us)
Async XLA Ops:
  0.0 39.3 %copy-start.5 = (s32[3840]{0:T(1024)S(1)}, s32[3840]{0:T(1024)}, u32[]{:S(2)}) copy-start(s32[3840]{0:T(1024)} %param.15) | copy-start | bytes 46084
  0.0 38.6 %copy-start.4 = (f32[3840]{0:T(1024)S(1)}, f32[3840]{0:T(1024)}, u32[]{:S(2)}) copy-start(f32[3840]{0:T(1024)} %param.14) | copy-start | bytes 46084
  0.0 38.0 %copy-start.6 = (f32[1536]{0:T(1024)S(1)}, f32[1536]{0:T(1024)}, u32[]{:S(2)}) copy-start(f32[1536]{0:T(1024)} %param.12) | copy-start | bytes 18436
  1.3 33.1 %copy-start.1 = (bf16[336,1536]{1,0:T(8,128)(2,1)}, bf16[336,1536]{1,0:T(8,128)(2,1)S(1)}, u32[]{:S(2)}) copy-start(bf16[336,1536]{1,0:T(8,128)(2,1)S(1)} %pad_maximum_fusion.rest_0_.rest_3_) | copy-start | bytes 3096580
  1.3 27.6 %collective-permute-start.3 = (bf16[336,1536]{1,0:T(8,128)(2,1)S(1)}, bf16[336,1536]{1,0:T(8,128)(2,1)}, u32[]{:S(2)}, u32[]{:S(2)}) collective-permute-start(bf16[336,1536]{1,0:T(8,128)(2,1)S(1)} %pad_maximum_fusion.rest_0_.rest_3_), channel_id=1, source_target_pairs={{0,2},{1,3},{2,0},{3,1},{4,6},{5,7},{6,4},{7,5},{8,10},{9,11},{10,... | collective-permute-start | bytes 3096584 | tf_op jit(solution)/shard_map/ppermute | solution.py:34
  1.8 27.1 %collective-permute-start.2 = (bf16[336,1536]{1,0:T(8,128)(2,1)S(1)}, bf16[336,1536]{1,0:T(8,128)(2,1)}, u32[]{:S(2)}, u32[]{:S(2)}) collective-permute-start(bf16[336,1536]{1,0:T(8,128)(2,1)S(1)} %pad_maximum_fusion.rest_0_.rest_3_), channel_id=1, source_target_pairs={{0,4},{1,5},{2,6},{3,7},{4,0},{5,1},{6,2},{7,3},{8,12},{9,13},{10,... | collective-permute-start | bytes 3096584 | tf_op jit(solution)/shard_map/ppermute | solution.py:34
  4.4 24.5 %collective-permute-start.1 = (bf16[336,1536]{1,0:T(8,128)(2,1)S(1)}, bf16[336,1536]{1,0:T(8,128)(2,1)S(1)}, u32[]{:S(2)}, u32[]{:S(2)}) collective-permute-start(bf16[336,1536]{1,0:T(8,128)(2,1)S(1)} %pad_maximum_fusion.rest_0_.rest_3_), channel_id=1, source_target_pairs={{8,16},{9,17},{10,18},{11,19},{12,20},{13,21},{14,22},{15,23},{16,... | collective-permute-start | bytes 3096584 | tf_op jit(solution)/shard_map/ppermute | solution.py:34
  5.1 27.4 %collective-permute-start = (bf16[336,1536]{1,0:T(8,128)(2,1)S(1)}, bf16[336,1536]{1,0:T(8,128)(2,1)}, u32[]{:S(2)}, u32[]{:S(2)}) collective-permute-start(bf16[336,1536]{1,0:T(8,128)(2,1)S(1)} %pad_maximum_fusion.rest_0_.rest_3_), channel_id=1, source_target_pairs={{0,8},{1,9},{2,10},{3,11},{4,12},{5,13},{6,14},{7,15},{8,0},{9,1},... | collective-permute-start | bytes 3096584 | tf_op jit(solution)/shard_map/ppermute | solution.py:34
  10.4 0.7 collective-permute-start.5
  11.0 17.9 %collective-permute-start.4 = (bf16[1,1536]{1,0:T(2,128)(2,1)S(1)}, bf16[1,1536]{1,0:T(2,128)(2,1)S(1)}, u32[]{:S(2)}, u32[]{:S(2)}) collective-permute-start(bf16[1,1536]{1,0:T(2,128)(2,1)S(1)} %get-tuple-element.86), channel_id=1, source_target_pairs={{0,2},{1,3},{2,0},{3,1},{4,6},{5,7},{6,4},{7,5},{8,10},{9,11},{10,... | collective-permute-start | bytes 9224 | tf_op jit(solution)/shard_map/ppermute | solution.py:34
  32.5 26.2 %collective-permute-start.8 = (bf16[336,1536]{1,0:T(8,128)(2,1)S(1)}, bf16[336,1536]{1,0:T(8,128)(2,1)S(1)}, u32[]{:S(2)}, u32[]{:S(2)}) collective-permute-start(bf16[336,1536]{1,0:T(8,128)(2,1)S(1)} %collective-permute-done.1), channel_id=1, source_target_pairs={{8,0},{9,1},{10,2},{11,3},{12,4},{13,5},{14,6},{15,7},{16,24},{17,... | collective-permute-start | bytes 3096584 | tf_op jit(solution)/shard_map/ppermute | solution.py:34
  33.8 24.9 %collective-permute-start.9 = (bf16[336,1536]{1,0:T(8,128)(2,1)}, bf16[336,1536]{1,0:T(8,128)(2,1)}, u32[]{:S(2)}, u32[]{:S(2)}) collective-permute-start(bf16[336,1536]{1,0:T(8,128)(2,1)} %collective-permute-done.2.rest_1_.rest_4_), channel_id=1, source_target_pairs={{0,2},{1,3},{2,0},{3,1},{4,6},{5,7},{6,4},{7,5},{8,10},{9,11},{10,... | collective-permute-start | bytes 3096584 | tf_op jit(solution)/shard_map/ppermute | solution.py:34
  33.9 24.9 %collective-permute-start.10 = (bf16[336,1536]{1,0:T(8,128)(2,1)}, bf16[336,1536]{1,0:T(8,128)(2,1)}, u32[]{:S(2)}, u32[]{:S(2)}) collective-permute-start(bf16[336,1536]{1,0:T(8,128)(2,1)} %collective-permute-done.rest_4_.rest_7_), channel_id=1, source_target_pairs={{0,2},{1,3},{2,0},{3,1},{4,6},{5,7},{6,4},{7,5},{8,10},{9,11},{10,... | collective-permute-start | bytes 3096584 | tf_op jit(solution)/shard_map/ppermute | solution.py:34
  34.4 25.7 %collective-permute-start.7 = (bf16[336,1536]{1,0:T(8,128)(2,1)}, bf16[336,1536]{1,0:T(8,128)(2,1)}, u32[]{:S(2)}, u32[]{:S(2)}) collective-permute-start(bf16[336,1536]{1,0:T(8,128)(2,1)} %collective-permute-done.rest_4_.rest_7_), channel_id=1, source_target_pairs={{0,4},{1,5},{2,6},{3,7},{4,0},{5,1},{6,2},{7,3},{8,12},{9,13},{10,... | collective-permute-start | bytes 3096584 | tf_op jit(solution)/shard_map/ppermute | solution.py:34
  36.5 23.6 %collective-permute-start.6 = (bf16[336,1536]{1,0:T(8,128)(2,1)}, bf16[336,1536]{1,0:T(8,128)(2,1)S(1)}, u32[]{:S(2)}, u32[]{:S(2)}) collective-permute-start(bf16[336,1536]{1,0:T(8,128)(2,1)} %collective-permute-done.rest_4_.rest_7_), channel_id=1, source_target_pairs={{8,16},{9,17},{10,18},{11,19},{12,20},{13,21},{14,22},{15,23},{16,... | collective-permute-start | bytes 3096584 | tf_op jit(solution)/shard_map/ppermute | solution.py:34
  47.3 16.4 %copy-start.12 = (bf16[320,1536]{1,0:T(8,128)(2,1)S(1)}, bf16[320,1536]{1,0:T(8,128)(2,1)}, u32[]{:S(2)}) copy-start(bf16[320,1536]{1,0:T(8,128)(2,1)} %get-tuple-element.61) | copy-start | bytes 2949124
  60.2 65.0 %copy-start = (bf16[336,1536]{1,0:T(8,128)(2,1)}, bf16[336,1536]{1,0:T(8,128)(2,1)S(1)}, u32[]{:S(2)}) copy-start(bf16[336,1536]{1,0:T(8,128)(2,1)S(1)} %broadcast_select_fusion.rest_8_.rest_11_) | copy-start | bytes 3096580
  60.3 30.8 %collective-permute-start.15 = (bf16[336,1536]{1,0:T(8,128)(2,1)S(1)}, bf16[336,1536]{1,0:T(8,128)(2,1)S(1)}, u32[]{:S(2)}, u32[]{:S(2)}) collective-permute-start(bf16[336,1536]{1,0:T(8,128)(2,1)S(1)} %broadcast_select_fusion.rest_8_.rest_11_), channel_id=1, source_target_pairs={{0,2},{1,3},{2,0},{3,1},{4,6},{5,7},{6,4},{7,5},{8,10},{9,11},{10,... | collective-permute-start | bytes 3096584 | tf_op jit(solution)/shard_map/ppermute | solution.py:34
  60.3 46.3 %collective-permute-start.12 = (bf16[336,1536]{1,0:T(8,128)(2,1)S(1)}, bf16[336,1536]{1,0:T(8,128)(2,1)S(1)}, u32[]{:S(2)}, u32[]{:S(2)}) collective-permute-start(bf16[336,1536]{1,0:T(8,128)(2,1)S(1)} %broadcast_select_fusion.rest_8_.rest_11_), channel_id=1, source_target_pairs={{0,4},{1,5},{2,6},{3,7},{4,0},{5,1},{6,2},{7,3},{8,12},{9,13},{10,... | collective-permute-start | bytes 3096584 | tf_op jit(solution)/shard_map/ppermute | solution.py:34
  62.1 49.7 %collective-permute-start.13 = (bf16[336,1536]{1,0:T(8,128)(2,1)S(1)}, bf16[336,1536]{1,0:T(8,128)(2,1)S(1)}, u32[]{:S(2)}, u32[]{:S(2)}) collective-permute-start(bf16[336,1536]{1,0:T(8,128)(2,1)S(1)} %collective-permute-done.6), channel_id=1, source_target_pairs={{8,0},{9,1},{10,2},{11,3},{12,4},{13,5},{14,6},{15,7},{16,24},{17,... | collective-permute-start | bytes 3096584 | tf_op jit(solution)/shard_map/ppermute | solution.py:34
  63.4 48.4 %collective-permute-start.14 = (bf16[336,1536]{1,0:T(8,128)(2,1)}, bf16[336,1536]{1,0:T(8,128)(2,1)S(1)}, u32[]{:S(2)}, u32[]{:S(2)}) collective-permute-start(bf16[336,1536]{1,0:T(8,128)(2,1)} %collective-permute-done.7.rest_5_.rest_8_), channel_id=1, source_target_pairs={{0,2},{1,3},{2,0},{3,1},{4,6},{5,7},{6,4},{7,5},{8,10},{9,11},{10,... | collective-permute-start | bytes 3096584 | tf_op jit(solution)/shard_map/ppermute | solution.py:34
  63.7 27.4 %collective-permute-start.11 = (bf16[320,1536]{1,0:T(8,128)(2,1)S(1)}, bf16[320,1536]{1,0:T(8,128)(2,1)S(1)}, u32[]{:S(2)}, u32[]{:S(2)}) collective-permute-start(bf16[320,1536]{1,0:T(8,128)(2,1)S(1)} %copy-done.12), channel_id=1, source_target_pairs={{0,31},{1,30},{2,29},{3,28},{4,27},{5,26},{6,25},{7,24},{8,23},{9,... | collective-permute-start | bytes 2949128 | tf_op jit(solution)/shard_map/ppermute | solution.py:34
  91.1 20.8 %copy-start.11 = (bf16[320,1536]{1,0:T(8,128)(2,1)}, bf16[320,1536]{1,0:T(8,128)(2,1)S(1)}, u32[]{:S(2)}) copy-start(bf16[320,1536]{1,0:T(8,128)(2,1)S(1)} %collective-permute-done.11.first) | copy-start | bytes 2949124
  91.1 34.2 %copy-start.7 = (bf16[336,1536]{1,0:T(8,128)(2,1)}, bf16[336,1536]{1,0:T(8,128)(2,1)S(1)}, u32[]{:S(2)}) copy-start(bf16[336,1536]{1,0:T(8,128)(2,1)S(1)} %collective-permute-done.15.rest_10_.rest_13_) | copy-start | bytes 3096580
  106.6 18.6 %copy-start.8 = (bf16[336,1536]{1,0:T(8,128)(2,1)}, bf16[336,1536]{1,0:T(8,128)(2,1)S(1)}, u32[]{:S(2)}) copy-start(bf16[336,1536]{1,0:T(8,128)(2,1)S(1)} %collective-permute-done.12.rest_9_.rest_12_) | copy-start | bytes 3096580
  111.8 13.4 %copy-start.9 = (bf16[336,1536]{1,0:T(8,128)(2,1)}, bf16[336,1536]{1,0:T(8,128)(2,1)S(1)}, u32[]{:S(2)}) copy-start(bf16[336,1536]{1,0:T(8,128)(2,1)S(1)} %collective-permute-done.14.rest_7_.rest_10_) | copy-start | bytes 3096580
  111.8 13.4 %collective-permute-start.20 = (bf16[336,1536]{1,0:T(8,128)(2,1)S(1)}, bf16[336,1536]{1,0:T(8,128)(2,1)S(1)}, u32[]{:S(2)}, u32[]{:S(2)}) collective-permute-start(bf16[336,1536]{1,0:T(8,128)(2,1)S(1)} %collective-permute-done.12.rest_9_.rest_12_), channel_id=1, source_target_pairs={{0,2},{1,3},{2,0},{3,1},{4,6},{5,7},{6,4},{7,5},{8,10},{9,11},{10,... | collective-permute-start | bytes 3096584 | tf_op jit(solution)/shard_map/ppermute | solution.py:34
  112.0 13.3 %copy-start.3 = (bf16[96,1536]{1,0:T(8,128)(2,1)}, bf16[96,1536]{1,0:T(8,128)(2,1)S(1)}, u32[]{:S(2)}) copy-start(bf16[96,1536]{1,0:T(8,128)(2,1)S(1)} %slice_select_fusion.1.rest_12_.rest_15_) | copy-start | bytes 884740
  112.0 11.8 %collective-permute-start.21 = (bf16[96,1536]{1,0:T(8,128)(2,1)S(1)}, bf16[96,1536]{1,0:T(8,128)(2,1)S(1)}, u32[]{:S(2)}, u32[]{:S(2)}) collective-permute-start(bf16[96,1536]{1,0:T(8,128)(2,1)S(1)} %slice_select_fusion.1.rest_12_.rest_15_), channel_id=1, source_target_pairs={{0,2},{1,3},{2,0},{3,1},{4,6},{5,7},{6,4},{7,5},{8,10},{9,11},{10,... | collective-permute-start | bytes 884744 | tf_op jit(solution)/shard_map/ppermute | solution.py:34
  112.5 9.0 %collective-permute-start.16 = (bf16[96,1536]{1,0:T(8,128)(2,1)S(1)}, bf16[96,1536]{1,0:T(8,128)(2,1)S(1)}, u32[]{:S(2)}, u32[]{:S(2)}) collective-permute-start(bf16[96,1536]{1,0:T(8,128)(2,1)S(1)} %slice_select_fusion.1.rest_12_.rest_15_), channel_id=1, source_target_pairs={{0,4},{1,5},{2,6},{3,7},{4,0},{5,1},{6,2},{7,3},{8,12},{9,13},{10,... | collective-permute-start | bytes 884744 | tf_op jit(solution)/shard_map/ppermute | solution.py:34
  114.3 32.3 %copy-start.2 = (bf16[240,1536]{1,0:T(8,128)(2,1)}, bf16[240,1536]{1,0:T(8,128)(2,1)S(1)}, u32[]{:S(2)}) copy-start(bf16[240,1536]{1,0:T(8,128)(2,1)S(1)} %slice_select_fusion.rest_19_) | copy-start | bytes 2211844
  121.5 3.0 %copy-start.18 = (bf16[96,1536]{1,0:T(8,128)(2,1)}, bf16[96,1536]{1,0:T(8,128)(2,1)S(1)}, u32[]{:S(2)}) copy-start(bf16[96,1536]{1,0:T(8,128)(2,1)S(1)} %collective-permute-done.16.rest_13_.rest_16_) | copy-start | bytes 884740
  121.5 3.0 %collective-permute-start.22 = (bf16[96,1536]{1,0:T(8,128)(2,1)S(1)}, bf16[96,1536]{1,0:T(8,128)(2,1)S(1)}, u32[]{:S(2)}, u32[]{:S(2)}) collective-permute-start(bf16[96,1536]{1,0:T(8,128)(2,1)S(1)} %collective-permute-done.16.rest_13_.rest_16_), channel_id=1, source_target_pairs={{0,2},{1,3},{2,0},{3,1},{4,6},{5,7},{6,4},{7,5},{8,10},{9,11},{10,... | collective-permute-start | bytes 884744 | tf_op jit(solution)/shard_map/ppermute | solution.py:34
  121.5 25.2 %collective-permute-start.19 = (bf16[240,1536]{1,0:T(8,128)(2,1)S(1)}, bf16[240,1536]{1,0:T(8,128)(2,1)S(1)}, u32[]{:S(2)}, u32[]{:S(2)}) collective-permute-start(bf16[240,1536]{1,0:T(8,128)(2,1)S(1)} %slice_select_fusion.rest_19_), channel_id=1, source_target_pairs={{0,2},{1,3},{2,0},{3,1},{4,6},{5,7},{6,4},{7,5},{8,10},{9,11},{10,... | collective-permute-start | bytes 2211848 | tf_op jit(solution)/shard_map/ppermute | solution.py:34
  122.0 31.0 %collective-permute-start.18 = (bf16[240,1536]{1,0:T(8,128)(2,1)S(1)}, bf16[240,1536]{1,0:T(8,128)(2,1)S(1)}, u32[]{:S(2)}, u32[]{:S(2)}) collective-permute-start(bf16[240,1536]{1,0:T(8,128)(2,1)S(1)} %slice_select_fusion.rest_19_), channel_id=1, source_target_pairs={{0,4},{1,5},{2,6},{3,7},{4,0},{5,1},{6,2},{7,3},{8,12},{9,13},{10,... | collective-permute-start | bytes 2211848 | tf_op jit(solution)/shard_map/ppermute | solution.py:34
  123.8 0.7 copy-start.17
  123.8 22.9 %collective-permute-start.17 = (bf16[192,1536]{1,0:T(8,128)(2,1)}, bf16[192,1536]{1,0:T(8,128)(2,1)S(1)}, u32[]{:S(2)}, u32[]{:S(2)}) collective-permute-start(bf16[192,1536]{1,0:T(8,128)(2,1)} %get-tuple-element.67), channel_id=1, source_target_pairs={{0,31},{1,30},{2,29},{3,28},{4,27},{5,26},{6,25},{7,24},{8,23},{9,... | collective-permute-start | bytes 1769480 | tf_op jit(solution)/shard_map/ppermute | solution.py:34
  124.5 0.7 copy-start.19
  125.3 1.0 copy-start.10
  146.7 8.6 %copy-start.16 = (bf16[192,1536]{1,0:T(8,128)(2,1)}, bf16[192,1536]{1,0:T(8,128)(2,1)S(1)}, u32[]{:S(2)}) copy-start(bf16[192,1536]{1,0:T(8,128)(2,1)S(1)} %collective-permute-done.17.rest_1_) | copy-start | bytes 1769476
  146.7 8.6 %copy-start.13 = (bf16[240,1536]{1,0:T(8,128)(2,1)}, bf16[240,1536]{1,0:T(8,128)(2,1)S(1)}, u32[]{:S(2)}) copy-start(bf16[240,1536]{1,0:T(8,128)(2,1)S(1)} %collective-permute-done.19.rest_21_) | copy-start | bytes 2211844
  153.1 2.2 %copy-start.14 = (bf16[240,1536]{1,0:T(8,128)(2,1)}, bf16[240,1536]{1,0:T(8,128)(2,1)S(1)}, u32[]{:S(2)}) copy-start(bf16[240,1536]{1,0:T(8,128)(2,1)S(1)} %collective-permute-done.18.rest_20_) | copy-start | bytes 2211844
  153.1 2.2 %collective-permute-start.23 = (bf16[240,1536]{1,0:T(8,128)(2,1)S(1)}, bf16[240,1536]{1,0:T(8,128)(2,1)S(1)}, u32[]{:S(2)}, u32[]{:S(2)}) collective-permute-start(bf16[240,1536]{1,0:T(8,128)(2,1)S(1)} %collective-permute-done.18.rest_20_), channel_id=1, source_target_pairs={{0,2},{1,3},{2,0},{3,1},{4,6},{5,7},{6,4},{7,5},{8,10},{9,11},{10,... | collective-permute-start | bytes 2211848 | tf_op jit(solution)/shard_map/ppermute | solution.py:34
  155.3 0.9 copy-start.15
